TPU v7x, 512 devices: a whole 4x4x16 slice. The times are simulated.
512 devices in a mesh: tile: 64 (over z_hi, x, y), mem: 8 (over z_lo, core).
Axes of the slice: x: 4, y: 4, z: 16 (z_hi: 4, z_lo: 4; z = z_hi * 4 + z_lo), core: 2. Of those that a mesh axis runs over, the one named last changes fastest.
Arguments:
- control: float32 [64, 32, 16384], P('mem', None, 'tile'), may hold values from -13.5 to 13.5
- perts: bfloat16 [64, 32, 16384], P('mem', None, 'tile'), may hold values from -6 to 6
- diffusivity: float32 [32], replicated, may hold values from 0.08 to 0.245
- vertical: float32 [32, 32], replicated, may hold values from -1 to 1
- gain: float32 [32, 16384], P(None, 'tile'), may hold values from 0.25 to 1.75
- edge_flip: int32 [64, 4], P('tile'), may hold values from 0 to 1, as said below
Outputs:
- increment: float32 [32, 16384], P('mem', 'tile')
- member_cost: float32 [64], P('mem')
Inputs may be any that keep to these rules, and one draw needn't show every extreme that they name: edge_flip[t, e] is 1 where the ghost strip beyond edge e of tile t runs in reverse order; both edges of a glued pair carry the same flag.
All inputs are finite; a program needn't handle non-finite values.
Results may differ from a plain program's by a relative error of at most 0.0004.
Values sent between devices are 32-bit elements; how exact they have to be, the bound alone decides.
No kernel may reach another device: no remote copies, remote signals or barrier semaphores. Data moves between devices by JAX's collectives and lax.ppermute only.
A program may use at most 64 MiB of HBM per device.

v0:
```python
import math

import jax
import jax.numpy as jnp
from jax import lax
from jax.sharding import PartitionSpec as P

PASSES = 3


def extended_2(shard, sides, width):
    for axis, dim in sides:
        devices, length = (lax.axis_size(axis), shard.shape[dim])
        up = [(i, (i + 1) % devices) for i in range(devices)]
        down = [(j, i) for i, j in up]
        last = lax.slice_in_dim(shard, length - width, length, axis=dim)
        leading = lax.slice_in_dim(shard, 0, width, axis=dim)
        before = lax.ppermute(last, axis, up)
        after = lax.ppermute(leading, axis, down)
        shard = jnp.concatenate([before, shard, after], axis=dim)
    return shard


def swapped(value, axis, stride):
    mask = 2**stride
    pairs = [(source, source ^ mask) for source in range(lax.axis_size(axis))]
    return lax.ppermute(value, axis, pairs)


def orient(edge_strip, edge_flag):
    return jnp.where(edge_flag == 1, edge_strip[..., ::-1], edge_strip)


def control_norms(control, tile_count):
    level_count = control.shape[1]
    cell_count = control.shape[2]
    partial_value = (
        0.5 * jnp.sum(control * control, axis=(1, 2)) / (level_count * cell_count * tile_count)
    )
    return lax.psum(partial_value, "tile")


def local(control, perts, diffusivity, vertical, gain, edge_flip):
    member_count, level_count, cell_count = control.shape
    edge_len = math.isqrt(cell_count)
    tile_count = lax.axis_size("tile")
    top_bit = tile_count.bit_length() - 2
    flip_row = edge_flip[0]
    rates = diffusivity[:, None, None]
    field = control
    for repeat in range(PASSES):
        grid = field.reshape(member_count, level_count, edge_len, edge_len)
        col_pair = jnp.stack([grid[..., 0], grid[..., edge_len - 1]])
        col_pair = col_pair.reshape(2, member_count, level_count * edge_len)
        extended = extended_2(col_pair, (("tile", 0),), 1)
        h_west = orient(extended[0].reshape(member_count, level_count, edge_len), flip_row[3])
        h_east = orient(extended[3].reshape(member_count, level_count, edge_len), flip_row[1])
        rim_pair = jnp.stack([field[..., :edge_len], field[..., cell_count - edge_len :]])
        rim_pair = rim_pair.reshape(2, member_count, level_count * edge_len)
        partner_rims = swapped(rim_pair, "tile", top_bit)
        h_north = orient(partner_rims[0].reshape(member_count, level_count, edge_len), flip_row[2])
        h_south = orient(partner_rims[1].reshape(member_count, level_count, edge_len), flip_row[0])
        neighbours = jnp.concatenate([grid[:, :, 1:, :], h_north[:, :, None, :]], axis=2)
        neighbours = neighbours + jnp.concatenate(
            [h_south[:, :, None, :], grid[:, :, :-1, :]], axis=2
        )
        neighbours = neighbours + jnp.concatenate([grid[..., 1:], h_east[..., None]], axis=3)
        neighbours = neighbours + jnp.concatenate([h_west[..., None], grid[..., :-1]], axis=3)
        updated = grid + rates * (neighbours - 4.0 * grid)
        field = updated.reshape(member_count, level_count, cell_count)
    vertical_mix = jnp.einsum("lm,kmc->klc", vertical, field, precision=lax.Precision.HIGHEST)
    member_term = jnp.sum(perts.astype(jnp.float32) * (gain[None] * vertical_mix), axis=0)
    members_all = member_count * lax.axis_size("mem")
    summed = lax.psum(member_term, "mem")
    level_rows = level_count // lax.axis_size("mem")
    level_share = lax.dynamic_slice_in_dim(
        summed, lax.axis_index("mem") * level_rows, level_rows, 0
    )
    increment = level_share / jnp.sqrt(jnp.float32(members_all - 1))
    member_cost = control_norms(control, tile_count)
    return (increment, member_cost)


def solution(mesh):
    placed = (
        P("mem", None, "tile"),
        P("mem", None, "tile"),
        P(),
        P(),
        P(None, "tile"),
        P("tile", None),
    )
    return jax.shard_map(
        local, mesh=mesh, in_specs=placed, out_specs=(P("mem", "tile"), P("mem")), check_vma=False
    )
```

profile of v0, /device:TPU:1, one launch (start us, length us, event | category | flops | bytes accessed | tf_op | source)
XLA Modules:
  0.0 354.0 jit_solution(442704307470117087)
XLA Ops:
  0.6 1.1 fusion.30
  1.7 0.1 stack.30
  1.8 0.1 stack.31
  2.0 16.3 %collective-permute-start = (f32[2,8,512]{2,1,0:T(8,128)S(1)}, f32[2,8,512]{2,1,0:T(8,128)S(1)}, u32[]{:S(2)}, u32[]{:S(2)}) collective-permute-start(f32[2,8,512]{2,1,0:T(8,128)S(1)} %pad_maximum_fusion), channel_id=1, source_target_pairs={{0,256},{8,264},{16,272},{24,280},{32,288},{40,296},{48,304},{56,3... | collective-permute-start | bytes 98312 | tf_op jit(solution)/shard_map/ppermute | solution.py:27
  18.3 0.3 copy.62
  18.6 0.1 fusion.27
  18.8 0.1 slice.152
  18.9 3.2 collective-permute-start.2
  22.2 0.1 slice.149
  22.3 10.2 %collective-permute-start.1 = (f32[1,8,512]{2,1,0:T(8,128)S(1)}, f32[1,8,512]{2,1,0:T(8,128)S(1)}, u32[]{:S(2)}, u32[]{:S(2)}) collective-permute-start(f32[1,8,512]{2,1,0:T(8,128)S(1)} %slice.149), channel_id=1, source_target_pairs={{8,0},{16,8},{24,16},{32,24},{40,32},{48,40},{56,48},{64,56},{72,6... | collective-permute-start | bytes 49160 | tf_op jit(solution)/shard_map/ppermute | solution.py:19
  32.5 1.5 fusion.26
  34.1 1.4 fusion.25
  35.5 0.7 fusion.34
  38.8 0.1 reshape_squeeze.39
  39.0 0.1 reshape_squeeze.38
  39.3 0.1 reshape_squeeze.36
  39.5 0.1 reshape_squeeze.37
  39.7 0.6 copy-done.8
  40.4 2.8 multiply_add_fusion.1
  43.1 0.1 fusion.24
  43.2 1.2 fusion.23
  44.4 1.4 fusion.22
  45.9 1.0 copy.75
  46.9 1.1 multiply_reduce_fusion
  48.0 0.1 fusion.29
  48.1 0.6 copy-done.2
  48.7 0.1 stack.33
  48.8 0.1 stack.34
  48.9 4.2 %collective-permute-start.3 = (f32[2,8,512]{2,1,0:T(8,128)S(1)}, f32[2,8,512]{2,1,0:T(8,128)S(1)}, u32[]{:S(2)}, u32[]{:S(2)}) collective-permute-start(f32[2,8,512]{2,1,0:T(8,128)S(1)} %pad_maximum_fusion.1), channel_id=1, source_target_pairs={{0,256},{8,264},{16,272},{24,280},{32,288},{40,296},{48,304},{56,3... | collective-permute-start | bytes 98312 | tf_op jit(solution)/shard_map/ppermute | solution.py:27
  53.2 0.1 slice.162
  53.3 6.1 %collective-permute-start.4 = (f32[1,8,512]{2,1,0:T(8,128)S(1)}, f32[1,8,512]{2,1,0:T(8,128)S(1)}, u32[]{:S(2)}, u32[]{:S(2)}) collective-permute-start(f32[1,8,512]{2,1,0:T(8,128)S(1)} %slice.162), channel_id=1, source_target_pairs={{8,0},{16,8},{24,16},{32,24},{40,32},{48,40},{56,48},{64,56},{72,6... | collective-permute-start | bytes 49160 | tf_op jit(solution)/shard_map/ppermute | solution.py:19
  59.6 0.1 slice.164
  59.7 1.9 collective-permute-start.5
  61.6 197.2 %psum.15 = f32[8]{0:T(128)} all-reduce(f32[8]{0:T(128)S(1)} %broadcast_multiply_fusion), channel_id=1, replica_groups=mesh['tile'=64,'mem'=8] {'tile'}, use_global_device_ids=true, to_apply=%region_3.4 | all-reduce | flops 8 | bytes 64 | tf_op jit(solution)/shard_map/psum | solution.py:40
  258.8 0.1 reshape_squeeze.42
  259.0 0.1 reshape_squeeze.43
  259.3 0.1 reshape_squeeze.40
  259.5 0.1 reshape_squeeze.41
  259.8 0.6 copy-done.9
  260.4 2.4 multiply_add_fusion
  262.9 0.1 fusion.19
  263.0 0.2 fusion.20
  263.2 1.5 fusion.21
  264.7 0.1 slice.176
  264.8 1.9 collective-permute-start.8
  266.9 0.1 slice.174
  267.0 11.5 %collective-permute-start.7 = (f32[1,8,512]{2,1,0:T(8,128)S(1)}, f32[1,8,512]{2,1,0:T(8,128)S(1)}, u32[]{:S(2)}, u32[]{:S(2)}) collective-permute-start(f32[1,8,512]{2,1,0:T(8,128)S(1)} %slice.174), channel_id=1, source_target_pairs={{8,0},{16,8},{24,16},{32,24},{40,32},{48,40},{56,48},{64,56},{72,6... | collective-permute-start | bytes 49160 | tf_op jit(solution)/shard_map/ppermute | solution.py:19
  278.5 1.0 copy.90
  279.5 1.0 multiply_add_fusion.2
  280.5 0.1 fusion.28
  280.6 0.6 copy-done.4
  281.2 0.1 stack.36
  281.3 0.1 stack.37
  281.5 10.0 %collective-permute-start.6 = (f32[2,8,512]{2,1,0:T(8,128)S(1)}, f32[2,8,512]{2,1,0:T(8,128)S(1)}, u32[]{:S(2)}, u32[]{:S(2)}) collective-permute-start(f32[2,8,512]{2,1,0:T(8,128)S(1)} %pad_maximum_fusion.2), channel_id=1, source_target_pairs={{0,256},{8,264},{16,272},{24,280},{32,288},{40,296},{48,304},{56,3... | collective-permute-start | bytes 98312 | tf_op jit(solution)/shard_map/ppermute | solution.py:27
  291.5 0.1 reshape_squeeze.47
  291.8 0.1 reshape_squeeze.46
  292.0 2.8 collective-permute-done.6
  294.8 0.1 reshape_squeeze.45
  295.3 2.0 fusion.8
  297.3 0.3 copy.103
  297.6 0.6 copy-done.5
  298.3 0.4 fusion.2
  298.7 54.7 %psum.14 = f32[32,256]{1,0:T(8,128)S(1)} all-reduce(f32[32,256]{1,0:T(8,128)S(1)} %fusion.2), channel_id=1, replica_groups=mesh['tile'=64,'mem'=8] {'mem'}, use_global_device_ids=true, to_apply=%region_1.2 | all-reduce | flops 8192 | bytes 65536 | tf_op jit(solution)/shard_map/psum | solution.py:74
  353.4 0.6 dynamic-slice_multiply_fusion
  (74 shorter events, 2.1 us)
Async XLA Ops:
  0.6 297.0 %copy-start = (f32[32,32]{1,0:T(8,128)S(1)}, f32[32,32]{1,0:T(8,128)}, u32[]{:S(2)}) copy-start(f32[32,32]{1,0:T(8,128)} %param.9) | copy-start | bytes 12292
  1.7 16.5 %copy-start.1 = (f32[8,32,256]{2,1,0:T(8,128)S(1)}, f32[8,32,256]{2,1,0:T(8,128)}, u32[]{:S(2)}) copy-start(f32[8,32,256]{2,1,0:T(8,128)} %param.6) | copy-start | bytes 786436
  2.0 37.3 %collective-permute-start = (f32[2,8,512]{2,1,0:T(8,128)S(1)}, f32[2,8,512]{2,1,0:T(8,128)S(1)}, u32[]{:S(2)}, u32[]{:S(2)}) collective-permute-start(f32[2,8,512]{2,1,0:T(8,128)S(1)} %pad_maximum_fusion), channel_id=1, source_target_pairs={{0,256},{8,264},{16,272},{24,280},{32,288},{40,296},{48,304},{56,3... | collective-permute-start | bytes 98312 | tf_op jit(solution)/shard_map/ppermute | solution.py:27
  18.9 19.9 %collective-permute-start.2 = (f32[1,8,512]{2,1,0:T(8,128)S(1)}, f32[1,8,512]{2,1,0:T(8,128)S(1)}, u32[]{:S(2)}, u32[]{:S(2)}) collective-permute-start(f32[1,8,512]{2,1,0:T(8,128)S(1)} %slice.152), channel_id=1, source_target_pairs={{0,8},{8,16},{16,24},{24,32},{32,40},{40,48},{48,56},{56,64},{64,7... | collective-permute-start | bytes 49160 | tf_op jit(solution)/shard_map/ppermute | solution.py:18
  22.3 16.7 %collective-permute-start.1 = (f32[1,8,512]{2,1,0:T(8,128)S(1)}, f32[1,8,512]{2,1,0:T(8,128)S(1)}, u32[]{:S(2)}, u32[]{:S(2)}) collective-permute-start(f32[1,8,512]{2,1,0:T(8,128)S(1)} %slice.149), channel_id=1, source_target_pairs={{8,0},{16,8},{24,16},{32,24},{40,32},{48,40},{56,48},{64,56},{72,6... | collective-permute-start | bytes 49160 | tf_op jit(solution)/shard_map/ppermute | solution.py:19
  34.1 1.5 copy-start.10
  39.7 0.7 copy-start.8
  48.0 0.7 copy-start.2
  48.9 210.4 %collective-permute-start.3 = (f32[2,8,512]{2,1,0:T(8,128)S(1)}, f32[2,8,512]{2,1,0:T(8,128)S(1)}, u32[]{:S(2)}, u32[]{:S(2)}) collective-permute-start(f32[2,8,512]{2,1,0:T(8,128)S(1)} %pad_maximum_fusion.1), channel_id=1, source_target_pairs={{0,256},{8,264},{16,272},{24,280},{32,288},{40,296},{48,304},{56,3... | collective-permute-start | bytes 98312 | tf_op jit(solution)/shard_map/ppermute | solution.py:27
  53.3 205.5 %collective-permute-start.4 = (f32[1,8,512]{2,1,0:T(8,128)S(1)}, f32[1,8,512]{2,1,0:T(8,128)S(1)}, u32[]{:S(2)}, u32[]{:S(2)}) collective-permute-start(f32[1,8,512]{2,1,0:T(8,128)S(1)} %slice.162), channel_id=1, source_target_pairs={{8,0},{16,8},{24,16},{32,24},{40,32},{48,40},{56,48},{64,56},{72,6... | collective-permute-start | bytes 49160 | tf_op jit(solution)/shard_map/ppermute | solution.py:19
  59.7 199.4 %collective-permute-start.5 = (f32[1,8,512]{2,1,0:T(8,128)S(1)}, f32[1,8,512]{2,1,0:T(8,128)S(1)}, u32[]{:S(2)}, u32[]{:S(2)}) collective-permute-start(f32[1,8,512]{2,1,0:T(8,128)S(1)} %slice.164), channel_id=1, source_target_pairs={{0,8},{8,16},{16,24},{24,32},{32,40},{40,48},{48,56},{56,64},{64,7... | collective-permute-start | bytes 49160 | tf_op jit(solution)/shard_map/ppermute | solution.py:18
  259.8 0.7 copy-start.9
  264.8 26.7 %collective-permute-start.8 = (f32[1,8,512]{2,1,0:T(8,128)S(1)}, f32[1,8,512]{2,1,0:T(8,128)S(1)}, u32[]{:S(2)}, u32[]{:S(2)}) collective-permute-start(f32[1,8,512]{2,1,0:T(8,128)S(1)} %slice.176), channel_id=1, source_target_pairs={{0,8},{8,16},{16,24},{24,32},{32,40},{40,48},{48,56},{56,64},{64,7... | collective-permute-start | bytes 49160 | tf_op jit(solution)/shard_map/ppermute | solution.py:18
  267.0 24.8 %collective-permute-start.7 = (f32[1,8,512]{2,1,0:T(8,128)S(1)}, f32[1,8,512]{2,1,0:T(8,128)S(1)}, u32[]{:S(2)}, u32[]{:S(2)}) collective-permute-start(f32[1,8,512]{2,1,0:T(8,128)S(1)} %slice.174), channel_id=1, source_target_pairs={{8,0},{16,8},{24,16},{32,24},{40,32},{48,40},{56,48},{64,56},{72,6... | collective-permute-start | bytes 49160 | tf_op jit(solution)/shard_map/ppermute | solution.py:19
  278.5 1.0 copy-start.3
  280.5 0.7 copy-start.4
  281.5 13.4 %collective-permute-start.6 = (f32[2,8,512]{2,1,0:T(8,128)S(1)}, f32[2,8,512]{2,1,0:T(8,128)S(1)}, u32[]{:S(2)}, u32[]{:S(2)}) collective-permute-start(f32[2,8,512]{2,1,0:T(8,128)S(1)} %pad_maximum_fusion.2), channel_id=1, source_target_pairs={{0,256},{8,264},{16,272},{24,280},{32,288},{40,296},{48,304},{56,3... | collective-permute-start | bytes 98312 | tf_op jit(solution)/shard_map/ppermute | solution.py:27
  297.3 1.0 copy-start.5
  297.3 1.0 copy-start.6
  297.3 1.0 copy-start.7
where the time goes:
time: 355 us; the launch traced here: 354 us
  blocking collectives  252 us (71%)
  starting transfers between devices  65.4 us (18%)
  local copies, waits for them, and re-layouts  19.5 us (5%)
  other arithmetic  10.1 us (3%)
  between operations  3.89 us (1%)
    psum x1, blocking collectives, control_norms(): return lax.psum(partial_value, 'tile')  197 us
    psum x1, blocking collectives, local(): summed = lax.psum(member_term, 'mem')  54.7 us
    ppermute x3, starting transfers between devices, swapped(): return lax.ppermute(value, axis, pairs)  30.5 us
    ppermute x3, starting transfers between devices, extended_2(): after = lax.ppermute(leading, axis, down)  27.8 us
  transfers between devices with their start and end apart: 9, of which 1 were waited for; matrix products, arithmetic and copies ran while one was open for 2% of the time, Pallas kernels for 0%

commit v1 on v0

v1 whole, which is shorter than its diff:
```python
import math

import jax
import jax.numpy as jnp
import numpy as np
from jax import lax
from jax.sharding import PartitionSpec as P

PASSES = 3
SIDE = 16
CELLS = SIDE * SIDE
CORNER = ((0, 0), (0, 1), (1, 0))
LAST = SIDE - 1

EW_ROWS = 64
NS_ROWS = 128
S_, E_, N_, W_ = range(4)


def cell(row, col):
    return row * SIDE + col


def walk_operators():
    names = [("own", i, j) for i in range(SIDE) for j in range(SIDE)]
    for side in "EWNS":
        names += [(side, a, i) for a in range(PASSES) for i in range(SIDE)]
    ends = ("EN", "ES", "WN", "WS", "NE", "NW", "SE", "SW")
    for end in ends:
        names += [(end, a, b) for a, b in CORNER]
    names += [("q", end) for end in ends]
    place = {name: k for k, name in enumerate(names)}
    size = len(names)
    lap = np.zeros((size, size), np.int64)

    def link(name, others):
        row = place[name]
        lap[row, row] -= 4
        for other in others:
            lap[row, place[other]] += 1

    def inside(i, j):
        if i < 0:
            return ("S", -1 - i, j)
        if i > LAST:
            return ("N", i - SIDE, j)
        if j < 0:
            return ("W", -1 - j, i)
        if j > LAST:
            return ("E", j - SIDE, i)
        return ("own", i, j)

    for i in range(SIDE):
        for j in range(SIDE):
            link(("own", i, j), [inside(i + 1, j), inside(i - 1, j), inside(i, j + 1), inside(i, j - 1)])
    border = {
        "E": lambda i: ("own", i, LAST),
        "W": lambda i: ("own", i, 0),
        "N": lambda j: ("own", LAST, j),
        "S": lambda j: ("own", 0, j),
    }
    beyond = {"E": ("EN", "ES"), "W": ("WN", "WS"), "N": ("NE", "NW"), "S": ("SE", "SW")}
    for side in "EWNS":
        high, low = beyond[side]
        for a in range(PASSES - 1):
            for i in range(SIDE):
                link(
                    (side, a, i),
                    [
                        border[side](i) if a == 0 else (side, a - 1, i),
                        (side, a + 1, i),
                        (side, a, i + 1) if i < LAST else (high, a, 0),
                        (side, a, i - 1) if i > 0 else (low, a, 0),
                    ],
                )
        for end, last in ((high, LAST), (low, 0)):
            link((end, 0, 0), [(side, 0, last), (end, 1, 0), (end, 0, 1), ("q", end)])
    powers = [lap[:CELLS]]
    for _ in range(PASSES - 1):
        powers.append(powers[-1] @ lap)
    return place, np.concatenate([p.T for p in powers], axis=1).astype(np.float32)


PLACE, WALKS = walk_operators()
WALKS_OWN = WALKS[:CELLS]


def pack_cells():
    west, east, far = [], [], []
    for a in range(PASSES):
        for i in range(SIDE):
            west.append((cell(i, a), cell(LAST - i, a), W_))
            east.append((cell(i, LAST - a), cell(LAST - i, LAST - a), E_))
    for a, b in CORNER:
        west.append((cell(b, a), cell(b, LAST - a), S_))
        east.append((cell(b, LAST - a), cell(b, a), S_))
    for a, b in CORNER:
        west.append((cell(LAST - b, a), cell(LAST - b, LAST - a), N_))
        east.append((cell(LAST - b, LAST - a), cell(LAST - b, a), N_))
    west += [(cell(LAST, 0), cell(LAST, LAST), N_), (cell(0, 0), cell(0, LAST), S_)]
    east += [(cell(LAST, LAST), cell(LAST, 0), N_), (cell(0, LAST), cell(0, 0), S_)]
    north_south = []
    for a in range(PASSES):
        for j in range(SIDE):
            north_south.append((cell(a, j), cell(a, LAST - j), S_))
    for a in range(PASSES):
        for j in range(SIDE):
            north_south.append((cell(LAST - a, j), cell(LAST - a, LAST - j), N_))
    own_q = [
        (cell(0, LAST), cell(LAST, LAST), E_),
        (cell(LAST, LAST), cell(0, LAST), E_),
        (cell(0, 0), cell(LAST, 0), W_),
        (cell(LAST, 0), cell(0, 0), W_),
    ]
    return west, east, north_south, own_q


def split(value):
    high = lax.reduce_precision(value, 8, 7)
    return high.astype(jnp.bfloat16), (value - high).astype(jnp.bfloat16)


def dot(left, right, dims):
    return lax.dot_general(left, right, (dims, ((), ())), preferred_element_type=jnp.float32)


def picked(table, flags, field):
    zero, one, edge = (np.array(column, np.int32)[:, None] for column in zip(*table))
    flag = jnp.zeros(zero.shape, jnp.int32)
    for k in range(4):
        flag = jnp.where(jnp.asarray(edge == k), flags[k], flag)
    index = jnp.where(flag == 1, jnp.asarray(one), jnp.asarray(zero))
    chosen = (lax.broadcasted_iota(jnp.int32, (len(table), CELLS), 1) == index).astype(jnp.bfloat16)
    high, low = split(field)
    return dot(chosen, high, ((1,), (1,))) + dot(chosen, low, ((1,), (1,)))


def halo_operator(flags, far_flags):
    by_flag = [np.zeros((NS_ROWS + 2 * EW_ROWS, PASSES * CELLS), np.float32) for _ in range(2)]
    edge = np.full((NS_ROWS + 2 * EW_ROWS, 1), -1, np.int32)

    def put(row, zero, one=None, which=-1):
        by_flag[0][row] = WALKS[PLACE[zero]]
        by_flag[1][row] = WALKS[PLACE[one or zero]]
        edge[row] = which

    for a in range(PASSES):
        for i in range(SIDE):
            k = a * SIDE + i
            put(k, ("N", a, i))
            put(48 + k, ("S", a, i))
            put(NS_ROWS + k, ("E", a, i))
            put(NS_ROWS + EW_ROWS + k, ("W", a, i))
    for k, (a, b) in enumerate(CORNER):
        put(96 + k, ("NE", a, b), ("NW", a, b), N_)
        put(99 + k, ("SE", a, b), ("SW", a, b), S_)
        put(102 + k, ("NW", a, b), ("NE", a, b), N_)
        put(105 + k, ("SW", a, b), ("SE", a, b), S_)
        put(108 + k, ("EN", a, b), ("ES", a, b), E_)
        put(111 + k, ("ES", a, b), ("EN", a, b), E_)
        put(114 + k, ("WN", a, b), ("WS", a, b), W_)
        put(117 + k, ("WS", a, b), ("WN", a, b), W_)
    put(120, ("q", "EN"), ("q", "ES"), E_)
    put(121, ("q", "ES"), ("q", "EN"), E_)
    put(122, ("q", "WN"), ("q", "WS"), W_)
    put(123, ("q", "WS"), ("q", "WN"), W_)
    flag = jnp.zeros(edge.shape, jnp.int32)
    for k in range(4):
        flag = jnp.where(jnp.asarray(edge == k), flags[k], flag)
    operator = jnp.where(
        flag == 1, jnp.asarray(by_flag[1], jnp.bfloat16), jnp.asarray(by_flag[0], jnp.bfloat16)
    )
    third = 2 * CELLS
    far_e, far_w = far_flags
    north_e = jnp.where(flags[N_] == 1, third + cell(LAST, 0), third + cell(LAST, LAST))
    north_w = jnp.where(flags[N_] == 1, third + cell(LAST, LAST), third + cell(LAST, 0))
    south_e = jnp.where(flags[S_] == 1, third + cell(0, 0), third + cell(0, LAST))
    south_w = jnp.where(flags[S_] == 1, third + cell(0, LAST), third + cell(0, 0))
    rows = lax.broadcasted_iota(jnp.int32, operator.shape, 0)
    columns = lax.broadcasted_iota(jnp.int32, operator.shape, 1)
    for row, column in (
        (NS_ROWS + 54, jnp.where(far_e == 1, south_e, north_e)),
        (NS_ROWS + 55, jnp.where(far_e == 1, north_e, south_e)),
        (NS_ROWS + EW_ROWS + 54, jnp.where(far_w == 1, south_w, north_w)),
        (NS_ROWS + EW_ROWS + 55, jnp.where(far_w == 1, north_w, south_w)),
    ):
        operator = jnp.where((rows == row) & (columns == column), jnp.bfloat16(1), operator)
    return operator


def local(control, perts, diffusivity, vertical, gain, edge_flip):
    member_count, level_count, cell_count = control.shape
    tile_count = lax.axis_size("tile")
    mem_count = lax.axis_size("mem")
    lanes = member_count * level_count
    flags = edge_flip[0]
    field = control.reshape(lanes, cell_count)
    west_table, east_table, ns_table, q_table = pack_cells()

    def shifted(value, by):
        return lax.ppermute(value, "tile", [(i, (i + by) % tile_count) for i in range(tile_count)])

    def swapped(value, mask):
        return lax.ppermute(value, "tile", [(i, i ^ mask) for i in range(tile_count)])

    squares = field * field
    high, low = split(squares)
    ones = jnp.ones((1, cell_count), jnp.bfloat16)
    norms = dot(ones, high, ((1,), (1,))) + dot(ones, low, ((1,), (1,)))
    flag_row = [jnp.broadcast_to(flags[k].astype(jnp.float32), (1, lanes)) for k in range(4)]
    tail = jnp.concatenate([flag_row[S_], flag_row[N_], norms, jnp.zeros((5, lanes), jnp.float32)])
    west_pack = jnp.concatenate([picked(west_table, flags, field), tail])
    east_pack = jnp.concatenate([picked(east_table, flags, field), tail])
    ends = jnp.array([0, LAST])
    pad = jnp.zeros((5, lanes), jnp.float32)
    west_far = jnp.concatenate([west_pack[0:1], west_pack[15:16], norms, pad])
    east_far = jnp.concatenate([east_pack[0:1], east_pack[15:16], norms, pad])
    from_east = shifted(west_pack, -1)
    from_west = shifted(east_pack, 1)
    from_east2 = shifted(west_far, -2)
    from_west2 = shifted(east_far, 2)

    own_q = picked(q_table, flags, field)
    strips = picked(ns_table, flags, field)
    window = from_west[58:59] + norms + from_east[58:59] + from_east2[2:3]
    by_row = [b * SIDE + a for a, b in CORNER]
    by_row += [b * SIDE + LAST - a for a, b in CORNER]
    corners_e = jnp.concatenate([from_east[k : k + 1] for k in by_row])
    corners_w = jnp.concatenate([from_west[k : k + 1] for k in by_row])
    q_rows = jnp.concatenate(
        [
            jnp.where(from_east[56:57] == 1, from_east2[0:1], own_q[0:1]),
            jnp.where(from_east[57:58] == 1, from_east2[1:2], own_q[1:2]),
            jnp.where(from_west[56:57] == 1, from_west2[0:1], own_q[2:3]),
            jnp.where(from_west[57:58] == 1, from_west2[1:2], own_q[3:4]),
        ]
    )
    ns_pack = jnp.concatenate(
        [strips, corners_e, corners_w, from_east[48:54], from_west[48:54], q_rows]
        + [flag_row[E_], flag_row[W_], window, jnp.zeros((1, lanes), jnp.float32)]
    )
    arrived = swapped(ns_pack, tile_count // 2)

    total = window + arrived[126:127]
    mask = 4
    while mask < tile_count // 2:
        total = total + swapped(total, mask)
        mask *= 2

    high, low = split(field)
    own = jnp.asarray(WALKS_OWN, jnp.bfloat16)
    walks = dot(high, own, ((1,), (0,))) + dot(low, own, ((1,), (0,)))
    halo = jnp.concatenate([arrived, from_east, from_west])
    far_flags = (arrived[124, 0].astype(jnp.int32), arrived[125, 0].astype(jnp.int32))
    operator = halo_operator(flags, far_flags)
    high, low = split(halo)
    walks = walks + dot(high, operator, ((0,), (0,))) + dot(low, operator, ((0,), (0,)))
    rates = jnp.tile(diffusivity, member_count)[:, None]
    diffused = field + rates * (
        3.0 * walks[:, :cell_count]
        + rates * (3.0 * walks[:, cell_count : 2 * cell_count] + rates * walks[:, 2 * cell_count :])
    )
    diffused = diffused.reshape(member_count, level_count, cell_count)
    mix = jnp.einsum("lm,kmc->klc", vertical, diffused, precision=lax.Precision.HIGHEST)
    term = jnp.sum(perts.astype(jnp.float32) * (gain[None] * mix), axis=0)
    pieces = term.reshape(mem_count, level_count // mem_count, cell_count)
    pieces = lax.all_to_all(pieces, "mem", 0, 0, tiled=True)
    members_all = member_count * mem_count
    increment = jnp.sum(pieces, axis=0) / jnp.sqrt(jnp.float32(members_all - 1))
    norm_count = level_count * cell_count * tile_count
    member_cost = 0.5 * jnp.sum(total.reshape(member_count, level_count), axis=1) / norm_count
    return (increment, member_cost)


def solution(mesh):
    placed = (
        P("mem", None, "tile"),
        P("mem", None, "tile"),
        P(),
        P(),
        P(None, "tile"),
        P("tile", None),
    )
    return jax.shard_map(
        local, mesh=mesh, in_specs=placed, out_specs=(P("mem", "tile"), P("mem")), check_vma=False
    )
```

time: 355 us -> 104 us (0.29)
  blocking collectives: 252 us -> 0 us
  local copies, waits for them, and re-layouts: 19.5 us -> 5.21 us
  waiting for transfers between devices: 2.86 us -> 9.68 us
  matrix products: 0.45 us -> 4.17 us
    psum x2 -> x0, blocking collectives: 252 us -> none  [the longest x1 197 us: control_norms(): return lax.psum(partial_value, 'tile')]
    all_to_all x0 -> x1, starting transfers between devices: none -> 16.7 us  [local(): pieces = lax.all_to_all(pieces, 'mem', 0, 0, tiled=True)]
    ppermute x9 -> x8, starting transfers between devices: 65.4 us -> 50.8 us  [the longest x4 33.4 us: shifted(): lax.ppermute(value, 'tile', [(i, (i + by) % tile_count) for i in range(ti...]
    slice x28 -> x7, local copies, waits for them, and re-layouts: 10.7 us -> 1.13 us  [the longest x1 0.59 us: picked(): flag = jnp.where(jnp.asarray(edge == k), flags[k], flag)]
    add x4 -> x6, other arithmetic: 8.23 us -> 0.17 us  [the longest x1 0.13 us: local(): field + rates * (3.0 * walks[:, :cell_count] + rates * (3.0 * walks[:, ce...]
    eq x0 -> x10, other arithmetic: none -> 7.65 us  [the longest x3 5.06 us: picked(): lax.broadcasted_iota(jnp.int32, (len(table), CELLS), 1) == index]
    all_to_all x0 -> x1, waiting for transfers between devices: none -> 4.23 us  [local(): pieces = lax.all_to_all(pieces, 'mem', 0, 0, tiled=True)]
    dot_general x1 -> x15, matrix products: 0.45 us -> 4.17 us  [the longest x14 3.8 us: dot(): lax.dot_general(left, right, (dims, ((), ())), preferred_element_type=jnp...]
  transfers between devices with their start and end apart: 9 -> 9, of which waited for: 1 -> 4; matrix products, arithmetic and copies ran while one was open for 2% -> 10% of each run, Pallas kernels for 0% -> 0%
where the time goes in v1:
time: 104 us; the launch traced here: 103 us
  starting transfers between devices  67.5 us (65%)
  other arithmetic  10.2 us (10%)
  waiting for transfers between devices  9.68 us (9%)
  between operations  6.43 us (6%)
  local copies, waits for them, and re-layouts  5.21 us (5%)
  matrix products  4.17 us (4%)
    ppermute x4, starting transfers between devices, shifted(): lax.ppermute(value, 'tile', [(i, (i + by) % tile_count) for i in range(ti...  33.4 us
    ppermute x4, starting transfers between devices, swapped(): lax.ppermute(value, 'tile', [(i, i ^ mask) for i in range(tile_count)])  17.4 us
    all_to_all x1, starting transfers between devices, local(): pieces = lax.all_to_all(pieces, 'mem', 0, 0, tiled=True)  16.7 us
    ppermute x4, waiting for transfers between devices, swapped(): lax.ppermute(value, 'tile', [(i, i ^ mask) for i in range(tile_count)])  5.44 us
    eq x3, other arithmetic, picked(): lax.broadcasted_iota(jnp.int32, (len(table), CELLS), 1) == index  5.06 us
    all_to_all x1, waiting for transfers between devices, local(): pieces = lax.all_to_all(pieces, 'mem', 0, 0, tiled=True)  4.23 us
    dot_general x14, matrix products, dot(): lax.dot_general(left, right, (dims, ((), ())), preferred_element_type=jnp...  3.8 us
    unnamed x58, local copies, waits for them, and re-layouts  3.04 us
  transfers between devices with their start and end apart: 9, of which 4 were waited for; matrix products, arithmetic and copies ran while one was open for 10% of the time, Pallas kernels for 0%

profile of v1, /device:TPU:1, one launch (start us, length us, event | category | flops | bytes accessed | tf_op | source)
XLA Modules:
  0.0 103.2 jit_solution(9489652737770592704)
XLA Ops:
  0.6 0.0 copy-start
  0.7 1.1 %fusion.6 = (bf16[8,32,256]{2,1,0:T(8,128)(2,1)S(1)}, bf16[8,32,256]{2,1,0:T(8,128)(2,1)S(1)}) fusion(f32[8,32,256]{2,1,0:T(8,128)} %param.37), kind=kLoop, calls=%fused_computation.23 | loop fusion | flops 327680 | bytes 524288 | tf_op jit(solution)/shard_map/convert_element_type | solution.py:120
  1.8 0.6 copy-done.5
  2.4 0.6 fusion.45
  3.0 0.1 fusion.34
  3.1 0.0 copy-start.25
  3.2 0.1 fusion.36
  3.3 0.5 copy-done.22
  3.8 0.0 copy-done.23
  3.8 0.0 copy-done.24
  3.8 0.0 copy-done.25
  3.9 0.1 copy-done.19
  4.0 0.0 copy-done.20
  4.0 0.0 copy-done.21
  4.0 2.5 %fusion.31 = (s32[56]{0:T(128)S(1)}, s32[56]{0:T(128)S(1)}) fusion(s32[56,1]{0,1:T(1,128)S(1)} %copy-done.20, s32[56,1]{0,1:T(1,128)S(1)} %copy-done.19, pred[56,1]{0,1:T(4,128)(4,1)S(1)} %copy-done.24, pred[56,1]{0,1:T(4,128)(4,1)S(1)} %copy-done.23, pred[56,1]{0,1:T(4,128)(4,1)S(1)} %copy-done.25, s32[]{:T(128)} %bitcast.3, s32[]{:T(128)} %bitcast.12, ...), kind=kLoop, calls=%fused_computation.86 | loop fusion | flops 504 | bytes 1528 | tf_op jit(solution)/shard_map/eq | solution.py:133
  6.6 0.2 fusion.16
  6.8 0.2 fusion.17
  7.0 0.2 convolution_add_fusion.2
  7.2 0.2 convolution_add_fusion.3
  7.4 5.7 %collective-permute-start.3 = (f32[8,256]{1,0:T(8,128)S(1)}, f32[8,256]{1,0:T(8,128)S(1)}, u32[]{:S(2)}, u32[]{:S(2)}) collective-permute-start(f32[8,256]{1,0:T(8,128)S(1)} %get-tuple-element.31), channel_id=1, source_target_pairs={{0,16},{8,24},{16,32},{24,40},{32,48},{40,56},{48,64},{56,72},{64,... | collective-permute-start | bytes 24584 | tf_op jit(solution)/shard_map/ppermute | solution.py:201
  13.1 14.4 %collective-permute-start.2 = (f32[8,256]{1,0:T(8,128)S(1)}, f32[8,256]{1,0:T(8,128)S(1)}, u32[]{:S(2)}, u32[]{:S(2)}) collective-permute-start(f32[8,256]{1,0:T(8,128)S(1)} %get-tuple-element.32), channel_id=1, source_target_pairs={{0,496},{8,504},{16,0},{24,8},{32,16},{40,24},{48,32},{56,40},{64,... | collective-permute-start | bytes 24584 | tf_op jit(solution)/shard_map/ppermute | solution.py:201
  28.8 2.3 %collective-permute-start.1 = (f32[64,256]{1,0:T(8,128)S(1)}, f32[64,256]{1,0:T(8,128)S(1)}, u32[]{:S(2)}, u32[]{:S(2)}) collective-permute-start(f32[64,256]{1,0:T(8,128)S(1)} %concatenate.22), channel_id=1, source_target_pairs={{0,8},{8,16},{16,24},{24,32},{32,40},{40,48},{48,56},{56,64},{64,7... | collective-permute-start | bytes 196616 | tf_op jit(solution)/shard_map/ppermute | solution.py:201
  31.2 11.1 %collective-permute-start = (f32[64,256]{1,0:T(8,128)S(1)}, f32[64,256]{1,0:T(8,128)S(1)}, u32[]{:S(2)}, u32[]{:S(2)}) collective-permute-start(f32[64,256]{1,0:T(8,128)S(1)} %concatenate.21), channel_id=1, source_target_pairs={{0,504},{8,0},{16,8},{24,16},{32,24},{40,32},{48,40},{56,48},{64,5... | collective-permute-start | bytes 196616 | tf_op jit(solution)/shard_map/ppermute | solution.py:201
  42.8 0.0 copy-start.15
  42.9 0.0 copy-start.16
  43.6 1.2 %fusion.33 = s32[4]{0:T(128)S(1)} fusion(s32[4,1]{0,1:T(1,128)S(1)} %copy-done.16, s32[4,1]{0,1:T(1,128)S(1)} %copy-done.15, pred[4,1]{0,1:T(4,128)(4,1)S(1)} %copy-done.17, pred[4,1]{0,1:T(4,128)(4,1)S(1)} %copy-done.18, s32[]{:T(128)} %bitcast.12, s32[]{:T(128)} %bitcast.5), kind=kLoop, calls=%fused_computation.88 | loop fusion | flops 16 | bytes 64 | tf_op jit(solution)/shard_map/eq | solution.py:133
  44.8 0.2 fusion.25
  45.0 0.2 convolution_add_fusion.4
  45.2 0.3 copy-done.11
  45.5 0.0 copy-done.12
  45.5 0.0 copy-done.13
  45.5 0.0 copy-done.14
  45.5 1.3 %fusion.32 = s32[96]{0:T(128)S(1)} fusion(s32[96,1]{0,1:T(1,128)S(1)} %copy-done.12, s32[96,1]{0,1:T(1,128)S(1)} %copy-done.11, pred[96,1]{0,1:T(4,128)(4,1)S(1)} %copy-done.13, pred[96,1]{0,1:T(4,128)(4,1)S(1)} %copy-done.14, s32[]{:T(128)} %bitcast.3, s32[]{:T(128)} %bitcast.2), kind=kLoop, calls=%fused_computation.87 | loop fusion | flops 384 | bytes 1352 | tf_op jit(solution)/shard_map/eq | solution.py:133
  46.8 0.2 fusion.15
  47.0 0.2 convolution_add_fusion.1
  47.3 0.3 fusion.46
  47.5 0.3 fusion
  48.0 0.2 concatenate.25
  48.2 9.9 %collective-permute-start.4 = (f32[128,256]{1,0:T(8,128)S(1)}, f32[128,256]{1,0:T(8,128)S(1)}, u32[]{:S(2)}, u32[]{:S(2)}) collective-permute-start(f32[128,256]{1,0:T(8,128)S(1)} %concatenate.25), channel_id=1, source_target_pairs={{0,256},{8,264},{16,272},{24,280},{32,288},{40,296},{48,304},{56,3... | collective-permute-start | bytes 393224 | tf_op jit(solution)/shard_map/ppermute | solution.py:204
  59.5 0.6 copy-done.10
  60.1 0.1 mul.46
  60.2 0.6 copy-done.6
  60.8 0.0 copy-done.7
  60.8 0.0 copy-done.8
  60.8 0.0 copy-done.9
  60.8 2.5 %compare_reduce_fusion = pred[256]{0:T(512)(128)(4,1)S(1)} fusion(pred[256,1]{0,1:T(4,128)(4,1)S(1)} %copy-done.6, pred[256,1]{0,1:T(4,128)(4,1)S(1)} %copy-done.7, pred[256,1]{0,1:T(4,128)(4,1)S(1)} %copy-done.8, pred[256,1]{0,1:T(4,128)(4,1)S(1)} %copy-done.9, s32[]{:T(128)} %bitcast.3, s32[]{:T(128)} %bitcast.12, s32[]{:T(128)} %bitcast.2, s32[]{:T(128)} %bitcast.5), kind=kLoop, calls=%fused_computation.60 | loop fusion | flops 1280 | bytes 1296 | tf_op jit(solution)/shard_map/eq | solution.py:171
  63.4 0.8 collective-permute-done.4
  64.2 0.5 fusion.40
  66.1 1.9 %collective-permute-start.5 = (f32[1,256]{1,0:T(1,128)S(1)}, f32[1,256]{1,0:T(1,128)S(1)}, u32[]{:S(2)}, u32[]{:S(2)}) collective-permute-start(f32[1,256]{1,0:T(1,128)S(1)} %slice_add_fusion), channel_id=1, source_target_pairs={{0,32},{8,40},{16,48},{24,56},{32,0},{40,8},{48,16},{56,24},{64,96... | collective-permute-start | bytes 3080 | tf_op jit(solution)/shard_map/ppermute | solution.py:204
  68.1 0.7 fusion.13
  68.9 0.7 fusion.1
  69.6 0.8 collective-permute-done.5
  70.5 2.0 %collective-permute-start.6 = (f32[1,256]{1,0:T(1,128)S(1)}, f32[1,256]{1,0:T(1,128)S(1)}, u32[]{:S(2)}, u32[]{:S(2)}) collective-permute-start(f32[1,256]{1,0:T(1,128)S(1)} %add.73), channel_id=1, source_target_pairs={{0,64},{8,72},{16,80},{24,88},{32,96},{40,104},{48,112},{56,120},{... | collective-permute-start | bytes 3080 | tf_op jit(solution)/shard_map/ppermute | solution.py:204
  72.5 0.1 fusion.12
  72.7 3.8 %collective-permute-done.6 = f32[1,256]{1,0:T(1,128)S(1)} collective-permute-done((f32[1,256]{1,0:T(1,128)S(1)}, f32[1,256]{1,0:T(1,128)S(1)}, u32[]{:S(2)}, u32[]{:S(2)}) %collective-permute-start.6) | collective-permute-done | bytes 1056 | tf_op jit(solution)/shard_map/ppermute | solution.py:204
  76.4 3.5 %collective-permute-start.7 = (f32[1,256]{1,0:T(1,128)S(1)}, f32[1,256]{1,0:T(1,128)S(1)}, u32[]{:S(2)}, u32[]{:S(2)}) collective-permute-start(f32[1,256]{1,0:T(1,128)S(1)} %add.74), channel_id=1, source_target_pairs={{0,128},{8,136},{16,144},{24,152},{32,160},{40,168},{48,176},{56,1... | collective-permute-start | bytes 3080 | tf_op jit(solution)/shard_map/ppermute | solution.py:204
  79.9 0.4 fusion.4
  80.3 0.6 reshape.42
  80.9 16.7 %all-to-all-start = ((f32[8,4,256]{2,1,0:T(4,128)}), f32[8,4,256]{2,1,0:T(4,128)S(1)}, u32[]{:S(2)}, u32[]{:S(2)}) async-start(f32[8,4,256]{2,1,0:T(4,128)} %reshape.42), calls=%async_computation | async-start | bytes 65536 | tf_op jit(solution)/shard_map/all_to_all | solution.py:267
  97.6 0.1 reshape.43
  97.7 0.1 reduce_sum.29
  97.8 0.5 broadcast_multiply_fusion.1
  98.3 4.2 %all-to-all-done = f32[8,4,256]{2,1,0:T(4,128)S(1)} async-done(((f32[8,4,256]{2,1,0:T(4,128)}), f32[8,4,256]{2,1,0:T(4,128)S(1)}, u32[]{:S(2)}, u32[]{:S(2)}) %all-to-all-start) | async-done | bytes 32800 | tf_op jit(solution)/shard_map/all_to_all | solution.py:267
  102.6 0.6 broadcast_multiply_fusion
  (72 shorter events, 0.4 us)
Async XLA Ops:
  0.6 79.3 %copy-start = (f32[32,32]{1,0:T(8,128)S(1)}, f32[32,32]{1,0:T(8,128)}, u32[]{:S(2)}) copy-start(f32[32,32]{1,0:T(8,128)} %param.40) | copy-start | bytes 12292
  0.6 1.1 %copy-start.1 = (f32[8,32,256]{2,1,0:T(8,128)S(1)}, f32[8,32,256]{2,1,0:T(8,128)}, u32[]{:S(2)}) copy-start(f32[8,32,256]{2,1,0:T(8,128)} %param.37) | copy-start | bytes 786436
  1.7 0.7 copy-start.5
  3.1 0.7 copy-start.22
  3.1 0.7 copy-start.23
  3.1 0.7 copy-start.24
  3.1 0.7 copy-start.25
  3.3 0.7 copy-start.19
  3.3 0.7 copy-start.20
  3.3 0.7 copy-start.21
  7.4 40.5 %collective-permute-start.3 = (f32[8,256]{1,0:T(8,128)S(1)}, f32[8,256]{1,0:T(8,128)S(1)}, u32[]{:S(2)}, u32[]{:S(2)}) collective-permute-start(f32[8,256]{1,0:T(8,128)S(1)} %get-tuple-element.31), channel_id=1, source_target_pairs={{0,16},{8,24},{16,32},{24,40},{32,48},{40,56},{48,64},{56,72},{64,... | collective-permute-start | bytes 24584 | tf_op jit(solution)/shard_map/ppermute | solution.py:201
  13.1 34.8 %collective-permute-start.2 = (f32[8,256]{1,0:T(8,128)S(1)}, f32[8,256]{1,0:T(8,128)S(1)}, u32[]{:S(2)}, u32[]{:S(2)}) collective-permute-start(f32[8,256]{1,0:T(8,128)S(1)} %get-tuple-element.32), channel_id=1, source_target_pairs={{0,496},{8,504},{16,0},{24,8},{32,16},{40,24},{48,32},{56,40},{64,... | collective-permute-start | bytes 24584 | tf_op jit(solution)/shard_map/ppermute | solution.py:201
  28.8 19.0 %collective-permute-start.1 = (f32[64,256]{1,0:T(8,128)S(1)}, f32[64,256]{1,0:T(8,128)S(1)}, u32[]{:S(2)}, u32[]{:S(2)}) collective-permute-start(f32[64,256]{1,0:T(8,128)S(1)} %concatenate.22), channel_id=1, source_target_pairs={{0,8},{8,16},{16,24},{24,32},{32,40},{40,48},{48,56},{56,64},{64,7... | collective-permute-start | bytes 196616 | tf_op jit(solution)/shard_map/ppermute | solution.py:201
  31.1 12.4 %copy-start.18 = (pred[4,1]{0,1:T(4,128)(4,1)S(1)}, pred[4,1]{0,1:T(4,128)(4,1)}, u32[]{:S(2)}) copy-start(pred[4,1]{0,1:T(4,128)(4,1)} %constant.107.clone) | copy-start | bytes 16
  31.2 16.6 %collective-permute-start = (f32[64,256]{1,0:T(8,128)S(1)}, f32[64,256]{1,0:T(8,128)S(1)}, u32[]{:S(2)}, u32[]{:S(2)}) collective-permute-start(f32[64,256]{1,0:T(8,128)S(1)} %concatenate.21), channel_id=1, source_target_pairs={{0,504},{8,0},{16,8},{24,16},{32,24},{40,32},{48,40},{56,48},{64,5... | collective-permute-start | bytes 196616 | tf_op jit(solution)/shard_map/ppermute | solution.py:201
  42.8 0.7 copy-start.15
  42.9 0.7 copy-start.16
  42.9 0.7 copy-start.17
  44.8 0.7 copy-start.11
  44.8 0.7 copy-start.12
  44.8 0.7 copy-start.13
  44.8 0.7 copy-start.14
  45.0 2.2 %copy-start.2 = (bf16[256,768]{1,0:T(8,128)(2,1)S(1)}, bf16[256,768]{1,0:T(8,128)(2,1)}, u32[]{:S(2)}) copy-start(bf16[256,768]{1,0:T(8,128)(2,1)} %constant.115.clone) | copy-start | bytes 1179652
  47.8 20.3 %copy-start.27 = (bf16[256,768]{1,0:T(8,128)(2,1)S(1)}, bf16[256,768]{1,0:T(8,128)(2,1)}, u32[]{:S(2)}) copy-start(bf16[256,768]{1,0:T(8,128)(2,1)} %constant.120.clone) | copy-start | bytes 1179652
  48.2 16.1 %collective-permute-start.4 = (f32[128,256]{1,0:T(8,128)S(1)}, f32[128,256]{1,0:T(8,128)S(1)}, u32[]{:S(2)}, u32[]{:S(2)}) collective-permute-start(f32[128,256]{1,0:T(8,128)S(1)} %concatenate.25), channel_id=1, source_target_pairs={{0,256},{8,264},{16,272},{24,280},{32,288},{40,296},{48,304},{56,3... | collective-permute-start | bytes 393224 | tf_op jit(solution)/shard_map/ppermute | solution.py:204
  59.5 0.7 copy-start.10
  60.1 0.7 copy-start.6
  60.1 0.7 copy-start.7
  60.1 0.7 copy-start.8
  60.1 0.7 copy-start.9
  60.1 8.0 %copy-start.26 = (bf16[256,768]{1,0:T(8,128)(2,1)S(1)}, bf16[256,768]{1,0:T(8,128)(2,1)}, u32[]{:S(2)}) copy-start(bf16[256,768]{1,0:T(8,128)(2,1)} %constant.121.clone) | copy-start | bytes 1179652
  66.1 4.3 %collective-permute-start.5 = (f32[1,256]{1,0:T(1,128)S(1)}, f32[1,256]{1,0:T(1,128)S(1)}, u32[]{:S(2)}, u32[]{:S(2)}) collective-permute-start(f32[1,256]{1,0:T(1,128)S(1)} %slice_add_fusion), channel_id=1, source_target_pairs={{0,32},{8,40},{16,48},{24,56},{32,0},{40,8},{48,16},{56,24},{64,96... | collective-permute-start | bytes 3080 | tf_op jit(solution)/shard_map/ppermute | solution.py:204
  70.5 9.4 %copy-start.3 = (bf16[8,32,256]{2,1,0:T(8,128)(2,1)S(1)}, bf16[8,32,256]{2,1,0:T(8,128)(2,1)}, u32[]{:S(2)}) copy-start(bf16[8,32,256]{2,1,0:T(8,128)(2,1)} %param.38) | copy-start | bytes 393220
  70.5 9.4 %copy-start.4 = (f32[32,256]{1,0:T(8,128)S(1)}, f32[32,256]{1,0:T(8,128)}, u32[]{:S(2)}) copy-start(f32[32,256]{1,0:T(8,128)} %param.41) | copy-start | bytes 98308
  70.5 5.9 %collective-permute-start.6 = (f32[1,256]{1,0:T(1,128)S(1)}, f32[1,256]{1,0:T(1,128)S(1)}, u32[]{:S(2)}, u32[]{:S(2)}) collective-permute-start(f32[1,256]{1,0:T(1,128)S(1)} %add.73), channel_id=1, source_target_pairs={{0,64},{8,72},{16,80},{24,88},{32,96},{40,104},{48,112},{56,120},{... | collective-permute-start | bytes 3080 | tf_op jit(solution)/shard_map/ppermute | solution.py:204
  76.4 21.2 %collective-permute-start.7 = (f32[1,256]{1,0:T(1,128)S(1)}, f32[1,256]{1,0:T(1,128)S(1)}, u32[]{:S(2)}, u32[]{:S(2)}) collective-permute-start(f32[1,256]{1,0:T(1,128)S(1)} %add.74), channel_id=1, source_target_pairs={{0,128},{8,136},{16,144},{24,152},{32,160},{40,168},{48,176},{56,1... | collective-permute-start | bytes 3080 | tf_op jit(solution)/shard_map/ppermute | solution.py:204
  80.9 21.7 %all-to-all-start = ((f32[8,4,256]{2,1,0:T(4,128)}), f32[8,4,256]{2,1,0:T(4,128)S(1)}, u32[]{:S(2)}, u32[]{:S(2)}) async-start(f32[8,4,256]{2,1,0:T(4,128)} %reshape.42), calls=%async_computation | async-start | bytes 65536 | tf_op jit(solution)/shard_map/all_to_all | solution.py:267

commit v2 on v1

v2 whole, which is shorter than its diff:
```python
import jax
import jax.numpy as jnp
import numpy as np
from jax import lax
from jax.experimental import pallas as pl
from jax.experimental.pallas import tpu as pltpu
from jax.sharding import PartitionSpec as P

PASSES = 3
SIDE = 16
CELLS = SIDE * SIDE
CORNER = ((0, 0), (0, 1), (1, 0))
LAST = SIDE - 1

EW_ROWS = 64
NS_ROWS = 128
S_, E_, N_, W_ = range(4)


def cell(row, col):
    return row * SIDE + col


def walk_operators():
    names = [("own", i, j) for i in range(SIDE) for j in range(SIDE)]
    for side in "EWNS":
        names += [(side, a, i) for a in range(PASSES) for i in range(SIDE)]
    ends = ("EN", "ES", "WN", "WS", "NE", "NW", "SE", "SW")
    for end in ends:
        names += [(end, a, b) for a, b in CORNER]
    names += [("q", end) for end in ends]
    place = {name: k for k, name in enumerate(names)}
    size = len(names)
    lap = np.zeros((size, size), np.int64)

    def link(name, others):
        row = place[name]
        lap[row, row] -= 4
        for other in others:
            lap[row, place[other]] += 1

    def inside(i, j):
        if i < 0:
            return ("S", -1 - i, j)
        if i > LAST:
            return ("N", i - SIDE, j)
        if j < 0:
            return ("W", -1 - j, i)
        if j > LAST:
            return ("E", j - SIDE, i)
        return ("own", i, j)

    for i in range(SIDE):
        for j in range(SIDE):
            link(("own", i, j), [inside(i + 1, j), inside(i - 1, j), inside(i, j + 1), inside(i, j - 1)])
    border = {
        "E": lambda i: ("own", i, LAST),
        "W": lambda i: ("own", i, 0),
        "N": lambda j: ("own", LAST, j),
        "S": lambda j: ("own", 0, j),
    }
    beyond = {"E": ("EN", "ES"), "W": ("WN", "WS"), "N": ("NE", "NW"), "S": ("SE", "SW")}
    for side in "EWNS":
        high, low = beyond[side]
        for a in range(PASSES - 1):
            for i in range(SIDE):
                link(
                    (side, a, i),
                    [
                        border[side](i) if a == 0 else (side, a - 1, i),
                        (side, a + 1, i),
                        (side, a, i + 1) if i < LAST else (high, a, 0),
                        (side, a, i - 1) if i > 0 else (low, a, 0),
                    ],
                )
        for end, last in ((high, LAST), (low, 0)):
            link((end, 0, 0), [(side, 0, last), (end, 1, 0), (end, 0, 1), ("q", end)])
    powers = [lap[:CELLS]]
    for _ in range(PASSES - 1):
        powers.append(powers[-1] @ lap)
    return place, np.concatenate([p.T for p in powers], axis=1).astype(np.float32)


PLACE, WALKS = walk_operators()
WALKS_OWN = WALKS[:CELLS]


def pack_cells():
    west, east, far = [], [], []
    for a in range(PASSES):
        for i in range(SIDE):
            west.append((cell(i, a), cell(LAST - i, a), W_))
            east.append((cell(i, LAST - a), cell(LAST - i, LAST - a), E_))
    for a, b in CORNER:
        west.append((cell(b, a), cell(b, LAST - a), S_))
        east.append((cell(b, LAST - a), cell(b, a), S_))
    for a, b in CORNER:
        west.append((cell(LAST - b, a), cell(LAST - b, LAST - a), N_))
        east.append((cell(LAST - b, LAST - a), cell(LAST - b, a), N_))
    west += [(cell(LAST, 0), cell(LAST, LAST), N_), (cell(0, 0), cell(0, LAST), S_)]
    east += [(cell(LAST, LAST), cell(LAST, 0), N_), (cell(0, LAST), cell(0, 0), S_)]
    north_south = []
    for a in range(PASSES):
        for j in range(SIDE):
            north_south.append((cell(a, j), cell(a, LAST - j), S_))
    for a in range(PASSES):
        for j in range(SIDE):
            north_south.append((cell(LAST - a, j), cell(LAST - a, LAST - j), N_))
    own_q = [
        (cell(0, LAST), cell(LAST, LAST), E_),
        (cell(LAST, LAST), cell(0, LAST), E_),
        (cell(0, 0), cell(LAST, 0), W_),
        (cell(LAST, 0), cell(0, 0), W_),
    ]
    return west, east, north_south, own_q


def split(value):
    high = value.astype(jnp.bfloat16)
    return high, (value - high.astype(jnp.float32)).astype(jnp.bfloat16)


def dot(left, right, dims=((1,), (0,))):
    return lax.dot_general(left, right, (dims, ((), ())), preferred_element_type=jnp.float32)


def table_columns(table):
    rows = np.zeros((len(table), 8), np.int32)
    rows[:, :3] = np.array(table, np.int32)
    return rows


def per_row(edge, flags, shape):
    flag = jnp.zeros(shape, jnp.int32)
    for k in range(4):
        flag = jnp.where(edge == k, flags[k], flag)
    return flag


def pack_kernel(field_ref, flip_ref, table_ref, west_ref, east_ref, far_w_ref, far_e_ref, strips_ref):
    field = field_ref[...].reshape(-1, CELLS)
    lanes = field.shape[0]
    flags = [flip_ref[0, k] for k in range(4)]
    edge = table_ref[:, 2:3]
    flag = per_row(edge, flags, edge.shape)
    index = jnp.where(flag == 1, table_ref[:, 1:2], table_ref[:, 0:1])
    lane = lax.broadcasted_iota(jnp.int32, (edge.shape[0], CELLS), 1)
    chosen = jnp.where(lane == index, 1.0, 0.0).astype(jnp.bfloat16)
    high, low = split(field)
    nt = ((1,), (1,))
    rows = dot(chosen, high, nt) + dot(chosen, low, nt)
    high, low = split(field * field)
    ones = jnp.ones((8, CELLS), jnp.bfloat16)
    norms = (dot(ones, high, nt) + dot(ones, low, nt))[0:1]
    level = [jnp.full((1, lanes), flags[k].astype(jnp.float32)) for k in range(4)]
    for ref, far_ref, start in ((west_ref, far_w_ref, 0), (east_ref, far_e_ref, 56)):
        ref[0:56] = rows[start : start + 56]
        ref[56:57] = level[S_]
        ref[57:58] = level[N_]
        ref[58:59] = norms
        ref[59:64] = jnp.zeros((5, lanes), jnp.float32)
        far_ref[0:1] = rows[start : start + 1]
        far_ref[1:2] = rows[start + 15 : start + 16]
        far_ref[2:3] = norms
        far_ref[3:8] = jnp.zeros((5, lanes), jnp.float32)
    strips_ref[0:100] = rows[112:212]
    strips_ref[100:101] = level[E_]
    strips_ref[101:102] = level[W_]
    strips_ref[102:103] = norms
    strips_ref[103:104] = jnp.zeros((1, lanes), jnp.float32)


def relay_kernel(strips_ref, east_ref, west_ref, east2_ref, west2_ref, out_ref):
    out_ref[0:96] = strips_ref[0:96]
    row = 96
    for ref in (east_ref, west_ref):
        for a, b in CORNER:
            out_ref[row : row + 1] = ref[b * SIDE + a : b * SIDE + a + 1]
            row += 1
        for a, b in CORNER:
            out_ref[row : row + 1] = ref[b * SIDE + LAST - a : b * SIDE + SIDE - a]
            row += 1
    out_ref[108:114] = east_ref[48:54]
    out_ref[114:120] = west_ref[48:54]
    out_ref[120:122] = jnp.where(east_ref[56:58] == 1, east2_ref[0:2], strips_ref[96:98])
    out_ref[122:124] = jnp.where(west_ref[56:58] == 1, west2_ref[0:2], strips_ref[98:100])
    out_ref[124:126] = strips_ref[100:102]
    window = west_ref[58:59] + strips_ref[102:103] + east_ref[58:59] + east2_ref[2:3]
    out_ref[126:127] = window
    out_ref[127:128] = jnp.zeros_like(window)


def rate_column(diffusivity_ref, member_count):
    levels = diffusivity_ref.shape[1]
    here = lax.broadcasted_iota(jnp.int32, (levels, levels), 0)
    there = lax.broadcasted_iota(jnp.int32, (levels, levels), 1)
    column = jnp.sum(jnp.where(here == there, diffusivity_ref[...], 0.0), axis=1, keepdims=True)
    return jnp.concatenate([column] * member_count, axis=0)


def weighted(walks, rates):
    one, two, three = (walks[:, k * CELLS : (k + 1) * CELLS] for k in range(PASSES))
    return rates * (3.0 * one + rates * (3.0 * two + rates * three))


def own_kernel(
    field_ref, diffusivity_ref, vertical_ref, flip_ref, walks_ref, zero_ref, one_ref, edge_ref,
    base_ref, operator_ref, high_ref, low_ref,
):
    member_count, level_count, _ = field_ref.shape
    field = field_ref[...].reshape(-1, CELLS)
    rates = rate_column(diffusivity_ref, member_count)
    high, low = split(field)
    walks = dot(high, walks_ref[...]) + dot(low, walks_ref[...])
    base_ref[...] = field + weighted(walks, rates)
    flags = [flip_ref[0, k] for k in range(4)]
    flag = per_row(edge_ref[:, 0:1], flags, (edge_ref.shape[0], 1))
    flag = jnp.broadcast_to(flag, zero_ref.shape) == 1
    operator_ref[...] = jnp.where(
        flag, one_ref[...].astype(jnp.float32), zero_ref[...].astype(jnp.float32)
    ).astype(jnp.bfloat16)
    lanes = member_count * level_count
    across = jnp.concatenate([vertical_ref[...]] * member_count, axis=1)
    whole = jnp.concatenate([across] * member_count, axis=0)
    here = lax.broadcasted_iota(jnp.int32, (lanes, lanes), 0) // level_count
    there = lax.broadcasted_iota(jnp.int32, (lanes, lanes), 1) // level_count
    high, low = split(jnp.where(here == there, whole, 0.0))
    high_ref[...] = high
    low_ref[...] = low


def final_kernel(
    base_ref, operator_ref, high_ref, low_ref, arrived_ref, east_ref, west_ref, diffusivity_ref, flip_ref,
    perts_ref, gain_ref, term_ref,
):
    member_count, level_count, _ = perts_ref.shape
    rates = rate_column(diffusivity_ref, member_count)
    halo = jnp.concatenate([arrived_ref[...], east_ref[...], west_ref[...]], axis=0)
    flags = [flip_ref[0, k] for k in range(4)]
    north_e = jnp.where(flags[N_] == 1, cell(LAST, 0), cell(LAST, LAST))
    north_w = jnp.where(flags[N_] == 1, cell(LAST, LAST), cell(LAST, 0))
    south_e = jnp.where(flags[S_] == 1, cell(0, 0), cell(0, LAST))
    south_w = jnp.where(flags[S_] == 1, cell(0, LAST), cell(0, 0))
    far_e = arrived_ref[124:125, 0:1] == 1
    far_w = arrived_ref[125:126, 0:1] == 1
    rows = lax.broadcasted_iota(jnp.int32, (halo.shape[0], 1), 0)
    target = jnp.full(rows.shape, -1, jnp.int32)
    for row, yes, no, far in (
        (NS_ROWS + 54, south_e, north_e, far_e),
        (NS_ROWS + 55, north_e, south_e, far_e),
        (NS_ROWS + EW_ROWS + 54, south_w, north_w, far_w),
        (NS_ROWS + EW_ROWS + 55, north_w, south_w, far_w),
    ):
        target = jnp.where(rows == row, jnp.where(far, yes, no), target)
    lane = lax.broadcasted_iota(jnp.int32, (halo.shape[0], CELLS), 1)
    corner = jnp.where(lane == target, 1.0, 0.0).astype(jnp.bfloat16)
    high, low = split(halo.T)
    operator = operator_ref[...]
    walks = dot(high, operator) + dot(low, operator)
    extra = dot(high, corner) + dot(low, corner)
    diffused = base_ref[...] + weighted(walks, rates) + rates * rates * rates * extra
    high, low = split(diffused)
    mix = dot(high_ref[...], high) + dot(high_ref[...], low) + dot(low_ref[...], high)
    total = jnp.zeros((level_count, CELLS), jnp.float32)
    for k in range(member_count):
        rows = slice(k * level_count, (k + 1) * level_count)
        total = total + perts_ref[k].astype(jnp.float32) * mix[rows]
    term_ref[...] = (gain_ref[...] * total).reshape(term_ref.shape)


def halo_rows():
    by_flag = [np.zeros((NS_ROWS + 2 * EW_ROWS, PASSES * CELLS), np.float32) for _ in range(2)]
    edge = np.full((NS_ROWS + 2 * EW_ROWS, 8), -1, np.int32)

    def put(row, zero, one=None, which=-1):
        by_flag[0][row] = WALKS[PLACE[zero]]
        by_flag[1][row] = WALKS[PLACE[one or zero]]
        edge[row] = which

    for a in range(PASSES):
        for i in range(SIDE):
            k = a * SIDE + i
            put(k, ("N", a, i))
            put(48 + k, ("S", a, i))
            put(NS_ROWS + k, ("E", a, i))
            put(NS_ROWS + EW_ROWS + k, ("W", a, i))
    for k, (a, b) in enumerate(CORNER):
        put(96 + k, ("NE", a, b), ("NW", a, b), N_)
        put(99 + k, ("SE", a, b), ("SW", a, b), S_)
        put(102 + k, ("NW", a, b), ("NE", a, b), N_)
        put(105 + k, ("SW", a, b), ("SE", a, b), S_)
        put(108 + k, ("EN", a, b), ("ES", a, b), E_)
        put(111 + k, ("ES", a, b), ("EN", a, b), E_)
        put(114 + k, ("WN", a, b), ("WS", a, b), W_)
        put(117 + k, ("WS", a, b), ("WN", a, b), W_)
    put(120, ("q", "EN"), ("q", "ES"), E_)
    put(121, ("q", "ES"), ("q", "EN"), E_)
    put(122, ("q", "WN"), ("q", "WS"), W_)
    put(123, ("q", "WS"), ("q", "WN"), W_)
    return by_flag[0], by_flag[1], edge


def vmem(count):
    return [pl.BlockSpec(memory_space=pltpu.VMEM)] * count


SMEM = pl.BlockSpec(memory_space=pltpu.SMEM)


def local(control, perts, diffusivity, vertical, gain, edge_flip):
    member_count, level_count, cell_count = control.shape
    tile_count = lax.axis_size("tile")
    mem_count = lax.axis_size("mem")
    lanes = member_count * level_count
    west_table, east_table, ns_table, q_table = pack_cells()

    def shifted(value, by):
        return lax.ppermute(value, "tile", [(i, (i + by) % tile_count) for i in range(tile_count)])

    def swapped(value, mask):
        return lax.ppermute(value, "tile", [(i, i ^ mask) for i in range(tile_count)])

    def rows_of(count):
        return jax.ShapeDtypeStruct((count, lanes), jnp.float32)

    table = table_columns(west_table + east_table + ns_table + q_table + [(0, 0, -1)] * 4)
    west_pack, east_pack, west_far, east_far, strips = pl.pallas_call(
        pack_kernel,
        out_shape=[rows_of(EW_ROWS), rows_of(EW_ROWS), rows_of(8), rows_of(8), rows_of(104)],
        in_specs=vmem(1) + [SMEM] + vmem(1),
        out_specs=vmem(5),
        name="packs",
    )(control, edge_flip, jnp.asarray(table))
    from_east2 = shifted(west_far, -2)
    from_west2 = shifted(east_far, 2)
    from_east = shifted(west_pack, -1)
    from_west = shifted(east_pack, 1)

    ns_pack = pl.pallas_call(
        relay_kernel,
        out_shape=rows_of(NS_ROWS),
        in_specs=vmem(5),
        out_specs=vmem(1)[0],
        name="relay",
    )(strips, from_east, from_west, from_east2, from_west2)
    arrived = swapped(ns_pack, tile_count // 2)

    zero, one, edge = halo_rows()
    spread = diffusivity.reshape(1, level_count)
    wide = PASSES * cell_count
    base, operator, high, low = pl.pallas_call(
        own_kernel,
        out_shape=[
            jax.ShapeDtypeStruct((lanes, cell_count), jnp.float32),
            jax.ShapeDtypeStruct((NS_ROWS + 2 * EW_ROWS, wide), jnp.bfloat16),
            jax.ShapeDtypeStruct((lanes, lanes), jnp.bfloat16),
            jax.ShapeDtypeStruct((lanes, lanes), jnp.bfloat16),
        ],
        in_specs=vmem(3) + [SMEM] + vmem(4),
        out_specs=vmem(4),
        name="own_cells",
    )(
        control,
        spread,
        vertical,
        edge_flip,
        jnp.asarray(WALKS_OWN, jnp.bfloat16),
        jnp.asarray(zero, jnp.bfloat16),
        jnp.asarray(one, jnp.bfloat16),
        jnp.asarray(edge),
    )

    sums = jnp.broadcast_to(ns_pack[126:127] + arrived[126:127], (8, lanes))
    groups = [
        [low_bits + 32 * half + 4 * k for k in range(8)] for half in range(2) for low_bits in range(4)
    ]
    sums = lax.all_to_all(sums, "tile", 0, 0, tiled=True, axis_index_groups=groups)

    pieces = pl.pallas_call(
        final_kernel,
        out_shape=jax.ShapeDtypeStruct((mem_count, level_count // mem_count, cell_count), jnp.float32),
        in_specs=vmem(8) + [SMEM] + vmem(2),
        out_specs=vmem(1)[0],
        name="localized",
    )(base, operator, high, low, arrived, from_east, from_west, spread, edge_flip, perts, gain)
    pieces = lax.all_to_all(pieces, "mem", 0, 0, tiled=True)
    members_all = member_count * mem_count
    increment = jnp.sum(pieces, axis=0) / jnp.sqrt(jnp.float32(members_all - 1))
    norm_count = level_count * cell_count * tile_count
    member_cost = 0.5 * jnp.sum(sums.reshape(8, member_count, level_count), axis=(0, 2)) / norm_count
    return (increment, member_cost)


def solution(mesh):
    placed = (
        P("mem", None, "tile"),
        P("mem", None, "tile"),
        P(),
        P(),
        P(None, "tile"),
        P("tile", None),
    )
    return jax.shard_map(
        local, mesh=mesh, in_specs=placed, out_specs=(P("mem", "tile"), P("mem")), check_vma=False
    )
```

time: 104 us -> 96.5 us (0.928)
  the two profiles are of different devices: /device:TPU:1 before, /device:TPU:8 now
where the time goes in v2:
time: 96.5 us; the launch traced here: 96 us
  starting transfers between devices  44.4 us (46%)
  waiting for transfers between devices  38.3 us (40%)
  Pallas kernels  9.18 us (10%)
  other arithmetic  1.98 us (2%)
  local copies, waits for them, and re-layouts  1.31 us (1%)
    ppermute x4, starting transfers between devices, shifted(): lax.ppermute(value, 'tile', [(i, (i + by) % tile_count) for i in range(ti...  32.5 us
    ppermute x1, waiting for transfers between devices, swapped(): lax.ppermute(value, 'tile', [(i, i ^ mask) for i in range(tile_count)])  16.6 us
    ppermute x4, waiting for transfers between devices, shifted(): lax.ppermute(value, 'tile', [(i, (i + by) % tile_count) for i in range(ti...  12.2 us
    all_to_all x1, waiting for transfers between devices, local(): pieces = lax.all_to_all(pieces, 'mem', 0, 0, tiled=True)  5 us
    all_to_all x1, starting transfers between devices, local(): pieces = lax.all_to_all(pieces, 'mem', 0, 0, tiled=True)  4.94 us
    all_to_all x1, waiting for transfers between devices, local(): lax.all_to_all(sums, 'tile', 0, 0, tiled=True, axis_index_groups=groups)  4.52 us
    ppermute x1, starting transfers between devices, swapped(): lax.ppermute(value, 'tile', [(i, i ^ mask) for i in range(tile_count)])  3.63 us
    all_to_all x1, starting transfers between devices, local(): lax.all_to_all(sums, 'tile', 0, 0, tiled=True, axis_index_groups=groups)  3.32 us
  transfers between devices with their start and end apart: 7, of which 4 were waited for; matrix products, arithmetic and copies ran while one was open for 1% of the time, Pallas kernels for 6%

profile of v2, /device:TPU:8, one launch (start us, length us, event | category | flops | bytes accessed | tf_op | source)
XLA Modules:
  0.0 96.0 jit_solution(1668526807945493085)
XLA Ops:
  0.6 2.0 %packs.1 = (f32[64,256]{1,0:T(8,128)}, f32[64,256]{1,0:T(8,128)}, f32[8,256]{1,0:T(8,128)}, f32[8,256]{1,0:T(8,128)}, f32[104,256]{1,0:T(8,128)}) custom-call(f32[8,32,256]{2,1,0:T(8,128)} %field_ref.3, s32[1,4]{1,0:T(1,128)} %flip_ref.5, s32[216,8]{1,0:T(8,128)} %constant.20.clone.table_ref), custom_call_target="tpu_custom_call" | custom-call | tf_op jit(solution)/shard_map/packs/pallas_call | solution.py:327
  2.7 7.7 %collective-permute-start = (f32[64,256]{1,0:T(8,128)}, f32[64,256]{1,0:T(8,128)S(1)}, u32[]{:S(2)}, u32[]{:S(2)}) collective-permute-start(f32[64,256]{1,0:T(8,128)} %get-tuple-element.16), channel_id=1, source_target_pairs={{0,504},{8,0},{16,8},{24,16},{32,24},{40,32},{48,40},{56,48},{64,5... | collective-permute-start | bytes 196616 | tf_op jit(solution)/shard_map/ppermute | solution.py:318
  10.4 1.9 %collective-permute-start.1 = (f32[64,256]{1,0:T(8,128)}, f32[64,256]{1,0:T(8,128)S(1)}, u32[]{:S(2)}, u32[]{:S(2)}) collective-permute-start(f32[64,256]{1,0:T(8,128)} %get-tuple-element.17), channel_id=1, source_target_pairs={{0,8},{8,16},{16,24},{24,32},{32,40},{40,48},{48,56},{56,64},{64,7... | collective-permute-start | bytes 196616 | tf_op jit(solution)/shard_map/ppermute | solution.py:318
  12.3 21.0 %collective-permute-start.2 = (f32[8,256]{1,0:T(8,128)}, f32[8,256]{1,0:T(8,128)S(1)}, u32[]{:S(2)}, u32[]{:S(2)}) collective-permute-start(f32[8,256]{1,0:T(8,128)} %get-tuple-element.18), channel_id=1, source_target_pairs={{0,496},{8,504},{16,0},{24,8},{32,16},{40,24},{48,32},{56,40},{64,... | collective-permute-start | bytes 24584 | tf_op jit(solution)/shard_map/ppermute | solution.py:318
  33.3 1.9 %collective-permute-start.3 = (f32[8,256]{1,0:T(8,128)}, f32[8,256]{1,0:T(8,128)S(1)}, u32[]{:S(2)}, u32[]{:S(2)}) collective-permute-start(f32[8,256]{1,0:T(8,128)} %get-tuple-element.19), channel_id=1, source_target_pairs={{0,16},{8,24},{16,32},{24,40},{32,48},{40,56},{48,64},{56,72},{64,... | collective-permute-start | bytes 24584 | tf_op jit(solution)/shard_map/ppermute | solution.py:318
  35.2 0.0 collective-permute-done.2.east2_ref
  35.3 0.0 copy-start.3
  35.3 12.2 %collective-permute-done.3.west2_ref = f32[8,256]{1,0:T(8,128)S(1)} collective-permute-done((f32[8,256]{1,0:T(8,128)}, f32[8,256]{1,0:T(8,128)S(1)}, u32[]{:S(2)}, u32[]{:S(2)}) %collective-permute-start.3) | collective-permute-done | bytes 8224 | tf_op jit(solution)/shard_map/ppermute | solution.py:318
  47.5 0.0 copy-start.4
  47.5 0.0 collective-permute-done.east_ref
  47.5 0.0 copy-start
  47.5 0.0 collective-permute-done.1.west_ref
  47.5 0.0 copy-start.1
  47.5 0.0 copy-done.3
  47.5 0.6 copy-done.4
  48.1 0.0 copy-done
  48.1 0.0 copy-done.1
  48.2 1.6 %relay.1 = f32[128,256]{1,0:T(8,128)} custom-call(f32[104,256]{1,0:T(8,128)} %get-tuple-element.15.strips_ref, f32[64,256]{1,0:T(8,128)} %copy-done, f32[64,256]{1,0:T(8,128)} %copy-done.1, f32[8,256]{1,0:T(8,128)} %copy-done.3, f32[8,256]{1,0:T(8,128)} %copy-done.4), custom_call_target="tpu_custom_call" | custom-call | tf_op jit(solution)/shard_map/relay/pallas_call | solution.py:339
  49.8 3.6 %collective-permute-start.4 = (f32[128,256]{1,0:T(8,128)}, f32[128,256]{1,0:T(8,128)S(1)}, u32[]{:S(2)}, u32[]{:S(2)}) collective-permute-start(f32[128,256]{1,0:T(8,128)} %relay.1), channel_id=1, source_target_pairs={{0,256},{8,264},{16,272},{24,280},{32,288},{40,296},{48,304},{56,3... | collective-permute-start | bytes 393224 | tf_op jit(solution)/shard_map/ppermute | solution.py:321
  53.4 16.6 %collective-permute-done.4.arrived_ref = f32[128,256]{1,0:T(8,128)S(1)} collective-permute-done((f32[128,256]{1,0:T(8,128)}, f32[128,256]{1,0:T(8,128)S(1)}, u32[]{:S(2)}, u32[]{:S(2)}) %collective-permute-start.4) | collective-permute-done | bytes 131104 | tf_op jit(solution)/shard_map/ppermute | solution.py:321
  70.0 0.0 copy-start.2
  70.0 0.7 slice_add_fusion
  70.7 0.6 broadcast_in_dim.2
  71.3 3.3 %all-to-all-start.1 = ((f32[8,1,256]{2,1,0:T(1,128)}), f32[8,1,256]{2,1,0:T(1,128)S(1)}, u32[]{:S(2)}, u32[]{:S(2)}) async-start(f32[8,1,256]{2,1,0:T(1,128)} %broadcast_in_dim.2), calls=%async_computation.1 | async-start | bytes 16384 | tf_op jit(solution)/shard_map/all_to_all | solution.py:377
  74.7 2.7 %own_cells.1 = (f32[256,256]{1,0:T(8,128)}, bf16[256,768]{1,0:T(8,128)(2,1)}, bf16[256,256]{1,0:T(8,128)(2,1)}, bf16[256,256]{1,0:T(8,128)(2,1)}) custom-call(f32[8,32,256]{2,1,0:T(8,128)} %field_ref.3, f32[1,32]{1,0:T(1,128)} %bitcast.3, f32[32,32]{1,0:T(8,128)} %vertical_ref.1, s32[1,4]{1,0:T(1,128)} %flip_ref.5, ...), custom_call_target="tpu_custom_call" | custom-call | tf_op jit(solution)/shard_map/own_cells/pallas_call | solution.py:351
  77.3 0.0 copy-done.2
  77.3 2.8 %localized.1 = f32[8,4,256]{2,1,0:T(4,128)} custom-call(f32[256,256]{1,0:T(8,128)} %get-tuple-element.11.base_ref, bf16[256,768]{1,0:T(8,128)(2,1)} %get-tuple-element.12.operator_ref, bf16[256,256]{1,0:T(8,128)(2,1)} %get-tuple-element.13.high_ref, bf16[256,256]{1,0:T(8,128)(2,1)} %get-tuple-element.14.low_ref, f32[128,256]{1,0:T(8,128)} %copy-done.2, ...), custom_call_target="tpu_custom_call" | custom-call | tf_op jit(solution)/shard_map/localized/pallas_call | solution.py:379
  80.2 4.5 %all-to-all-done.1 = f32[8,1,256]{2,1,0:T(1,128)S(1)} async-done(((f32[8,1,256]{2,1,0:T(1,128)}), f32[8,1,256]{2,1,0:T(1,128)S(1)}, u32[]{:S(2)}, u32[]{:S(2)}) %all-to-all-start.1) | async-done | bytes 8224 | tf_op jit(solution)/shard_map/all_to_all | solution.py:377
  84.7 4.9 %all-to-all-start = ((f32[8,4,256]{2,1,0:T(4,128)}), f32[8,4,256]{2,1,0:T(4,128)S(1)}, u32[]{:S(2)}, u32[]{:S(2)}) async-start(f32[8,4,256]{2,1,0:T(4,128)} %localized.1), calls=%async_computation | async-start | bytes 65536 | tf_op jit(solution)/shard_map/all_to_all | solution.py:386
  89.6 0.1 reduce_sum.27
  89.7 0.1 reduce_sum.28
  89.8 0.5 broadcast_multiply_fusion.1
  90.4 5.0 %all-to-all-done = f32[8,4,256]{2,1,0:T(4,128)S(1)} async-done(((f32[8,4,256]{2,1,0:T(4,128)}), f32[8,4,256]{2,1,0:T(4,128)S(1)}, u32[]{:S(2)}, u32[]{:S(2)}) %all-to-all-start) | async-done | bytes 32800 | tf_op jit(solution)/shard_map/all_to_all | solution.py:386
  95.4 0.6 broadcast_multiply_fusion
  (2 shorter events, 0.0 us)
Async XLA Ops:
  2.7 44.8 %collective-permute-start = (f32[64,256]{1,0:T(8,128)}, f32[64,256]{1,0:T(8,128)S(1)}, u32[]{:S(2)}, u32[]{:S(2)}) collective-permute-start(f32[64,256]{1,0:T(8,128)} %get-tuple-element.16), channel_id=1, source_target_pairs={{0,504},{8,0},{16,8},{24,16},{32,24},{40,32},{48,40},{56,48},{64,5... | collective-permute-start | bytes 196616 | tf_op jit(solution)/shard_map/ppermute | solution.py:318
  10.4 37.1 %collective-permute-start.1 = (f32[64,256]{1,0:T(8,128)}, f32[64,256]{1,0:T(8,128)S(1)}, u32[]{:S(2)}, u32[]{:S(2)}) collective-permute-start(f32[64,256]{1,0:T(8,128)} %get-tuple-element.17), channel_id=1, source_target_pairs={{0,8},{8,16},{16,24},{24,32},{32,40},{40,48},{48,56},{56,64},{64,7... | collective-permute-start | bytes 196616 | tf_op jit(solution)/shard_map/ppermute | solution.py:318
  12.3 22.9 %collective-permute-start.2 = (f32[8,256]{1,0:T(8,128)}, f32[8,256]{1,0:T(8,128)S(1)}, u32[]{:S(2)}, u32[]{:S(2)}) collective-permute-start(f32[8,256]{1,0:T(8,128)} %get-tuple-element.18), channel_id=1, source_target_pairs={{0,496},{8,504},{16,0},{24,8},{32,16},{40,24},{48,32},{56,40},{64,... | collective-permute-start | bytes 24584 | tf_op jit(solution)/shard_map/ppermute | solution.py:318
  33.3 14.2 %collective-permute-start.3 = (f32[8,256]{1,0:T(8,128)}, f32[8,256]{1,0:T(8,128)S(1)}, u32[]{:S(2)}, u32[]{:S(2)}) collective-permute-start(f32[8,256]{1,0:T(8,128)} %get-tuple-element.19), channel_id=1, source_target_pairs={{0,16},{8,24},{16,32},{24,40},{32,48},{40,56},{48,64},{56,72},{64,... | collective-permute-start | bytes 24584 | tf_op jit(solution)/shard_map/ppermute | solution.py:318
  35.3 12.3 %copy-start.3 = (f32[8,256]{1,0:T(8,128)}, f32[8,256]{1,0:T(8,128)S(1)}, u32[]{:S(2)}) copy-start(f32[8,256]{1,0:T(8,128)S(1)} %collective-permute-done.2.east2_ref) | copy-start | bytes 24580
  47.5 0.6 copy-start.4
  47.5 0.6 copy-start
  47.5 0.6 copy-start.1
  49.8 20.2 %collective-permute-start.4 = (f32[128,256]{1,0:T(8,128)}, f32[128,256]{1,0:T(8,128)S(1)}, u32[]{:S(2)}, u32[]{:S(2)}) collective-permute-start(f32[128,256]{1,0:T(8,128)} %relay.1), channel_id=1, source_target_pairs={{0,256},{8,264},{16,272},{24,280},{32,288},{40,296},{48,304},{56,3... | collective-permute-start | bytes 393224 | tf_op jit(solution)/shard_map/ppermute | solution.py:321
  70.0 7.3 %copy-start.2 = (f32[128,256]{1,0:T(8,128)}, f32[128,256]{1,0:T(8,128)S(1)}, u32[]{:S(2)}) copy-start(f32[128,256]{1,0:T(8,128)S(1)} %collective-permute-done.4.arrived_ref) | copy-start | bytes 393220
  71.3 13.4 %all-to-all-start.1 = ((f32[8,1,256]{2,1,0:T(1,128)}), f32[8,1,256]{2,1,0:T(1,128)S(1)}, u32[]{:S(2)}, u32[]{:S(2)}) async-start(f32[8,1,256]{2,1,0:T(1,128)} %broadcast_in_dim.2), calls=%async_computation.1 | async-start | bytes 16384 | tf_op jit(solution)/shard_map/all_to_all | solution.py:377
  84.7 10.7 %all-to-all-start = ((f32[8,4,256]{2,1,0:T(4,128)}), f32[8,4,256]{2,1,0:T(4,128)S(1)}, u32[]{:S(2)}, u32[]{:S(2)}) async-start(f32[8,4,256]{2,1,0:T(4,128)} %localized.1), calls=%async_computation | async-start | bytes 65536 | tf_op jit(solution)/shard_map/all_to_all | solution.py:386

commit v3 on v2

--- a/solution.py
+++ b/solution.py
@@ -14,6 +14,7 @@
 
 EW_ROWS = 64
 NS_ROWS = 128
+GROUP = 16
 S_, E_, N_, W_ = range(4)
 
 
@@ -137,7 +138,7 @@
     return flag
 
 
-def pack_kernel(field_ref, flip_ref, table_ref, west_ref, east_ref, far_w_ref, far_e_ref, strips_ref):
+def pack_kernel(field_ref, flip_ref, place_ref, table_ref, first_ref, second_ref, far_ref, strips_ref):
     field = field_ref[...].reshape(-1, CELLS)
     lanes = field.shape[0]
     flags = [flip_ref[0, k] for k in range(4)]
@@ -153,16 +154,18 @@
     ones = jnp.ones((8, CELLS), jnp.bfloat16)
     norms = (dot(ones, high, nt) + dot(ones, low, nt))[0:1]
     level = [jnp.full((1, lanes), flags[k].astype(jnp.float32)) for k in range(4)]
-    for ref, far_ref, start in ((west_ref, far_w_ref, 0), (east_ref, far_e_ref, 56)):
-        ref[0:56] = rows[start : start + 56]
+    west, east = rows[0:56], rows[56:112]
+    even = place_ref[0, 0] % 2 == 0
+    first_ref[0:56] = jnp.where(even, east, west)
+    second_ref[0:56] = jnp.where(even, west, east)
+    for ref in (first_ref, second_ref):
         ref[56:57] = level[S_]
         ref[57:58] = level[N_]
         ref[58:59] = norms
         ref[59:64] = jnp.zeros((5, lanes), jnp.float32)
-        far_ref[0:1] = rows[start : start + 1]
-        far_ref[1:2] = rows[start + 15 : start + 16]
-        far_ref[2:3] = norms
-        far_ref[3:8] = jnp.zeros((5, lanes), jnp.float32)
+    far_ref[0:1] = first_ref[0:1]
+    far_ref[1:2] = first_ref[LAST : LAST + 1]
+    far_ref[2:8] = jnp.zeros((6, lanes), jnp.float32)
     strips_ref[0:100] = rows[112:212]
     strips_ref[100:101] = level[E_]
     strips_ref[101:102] = level[W_]
@@ -170,24 +173,45 @@
     strips_ref[103:104] = jnp.zeros((1, lanes), jnp.float32)
 
 
-def relay_kernel(strips_ref, east_ref, west_ref, east2_ref, west2_ref, out_ref):
+def second_kernel(second_ref, near_ref, out_ref):
+    out_ref[0:59] = second_ref[0:59]
+    out_ref[59:60] = near_ref[0:1]
+    out_ref[60:61] = near_ref[LAST : LAST + 1]
+    out_ref[61:62] = second_ref[58:59] + near_ref[58:59]
+    out_ref[62:64] = jnp.zeros((2, out_ref.shape[1]), jnp.float32)
+
+
+def third_kernel(second_ref, other_ref, wrap_ref, out_ref):
+    out_ref[0:1] = other_ref[0:1] + wrap_ref[0:1]
+    out_ref[1:2] = other_ref[LAST : LAST + 1] + wrap_ref[LAST : LAST + 1]
+    out_ref[2:3] = second_ref[61:62] + other_ref[61:62]
+    out_ref[3:8] = jnp.zeros((5, out_ref.shape[1]), jnp.float32)
+
+
+def relay_kernel(strips_ref, second_ref, near_ref, other_ref, wrap_ref, back_ref, place_ref, out_ref):
+    place = place_ref[0, 0]
+    even = place % 2 == 0
+    near = near_ref[...]
+    other = other_ref[...] + wrap_ref[...]
     out_ref[0:96] = strips_ref[0:96]
     row = 96
-    for ref in (east_ref, west_ref):
+    for pack, far in (
+        (jnp.where(even, near, other), jnp.where(even, back_ref[0:2], other[59:61])),
+        (jnp.where(even, other, near), jnp.where(even, other[59:61], back_ref[0:2])),
+    ):
+        side = (row - 96) // 6
         for a, b in CORNER:
-            out_ref[row : row + 1] = ref[b * SIDE + a : b * SIDE + a + 1]
+            out_ref[row : row + 1] = pack[b * SIDE + a : b * SIDE + a + 1]
+            out_ref[row + 3 : row + 4] = pack[b * SIDE + LAST - a : b * SIDE + SIDE - a]
             row += 1
-        for a, b in CORNER:
-            out_ref[row : row + 1] = ref[b * SIDE + LAST - a : b * SIDE + SIDE - a]
-            row += 1
-    out_ref[108:114] = east_ref[48:54]
-    out_ref[114:120] = west_ref[48:54]
-    out_ref[120:122] = jnp.where(east_ref[56:58] == 1, east2_ref[0:2], strips_ref[96:98])
-    out_ref[122:124] = jnp.where(west_ref[56:58] == 1, west2_ref[0:2], strips_ref[98:100])
+        row += 3
+        out_ref[108 + 6 * side : 114 + 6 * side] = pack[48:54]
+        own = strips_ref[96 + 2 * side : 98 + 2 * side]
+        out_ref[120 + 2 * side : 122 + 2 * side] = jnp.where(pack[56:58] == 1, far, own)
     out_ref[124:126] = strips_ref[100:102]
-    window = west_ref[58:59] + strips_ref[102:103] + east_ref[58:59] + east2_ref[2:3]
-    out_ref[126:127] = window
-    out_ref[127:128] = jnp.zeros_like(window)
+    y = place % 4
+    out_ref[126:127] = jnp.where((y == 1) | (y == 2), second_ref[61:62] + other[61:62], back_ref[2:3])
+    out_ref[127:128] = jnp.zeros((1, out_ref.shape[1]), jnp.float32)
 
 
 def rate_column(diffusivity_ref, member_count):
@@ -228,14 +252,31 @@
     high_ref[...] = high
     low_ref[...] = low
 
+def sums_kernel(sent_ref, arrived_ref, out_ref):
+    out_ref[...] = jnp.broadcast_to(sent_ref[126:127] + arrived_ref[126:127], out_ref.shape)
+
 
 def final_kernel(
-    base_ref, operator_ref, high_ref, low_ref, arrived_ref, east_ref, west_ref, diffusivity_ref, flip_ref,
-    perts_ref, gain_ref, term_ref,
+    base_ref, operator_ref, high_ref, low_ref, arrived_ref, near_ref, other_ref, wrap_ref, far_ref, far2_ref,
+    diffusivity_ref, flip_ref, place_ref, perts_ref, gain_ref, term_ref,
+    halo_ref,
 ):
     member_count, level_count, _ = perts_ref.shape
     rates = rate_column(diffusivity_ref, member_count)
-    halo = jnp.concatenate([arrived_ref[...], east_ref[...], west_ref[...]], axis=0)
+    place = place_ref[0, 0]
+    even = place % 2 == 0
+    near = near_ref[...]
+    other = other_ref[...] + wrap_ref[...]
+    halo_ref[0:NS_ROWS] = arrived_ref[...]
+    halo_ref[NS_ROWS : NS_ROWS + EW_ROWS] = jnp.where(even, near, other)
+    halo_ref[NS_ROWS + EW_ROWS :] = jnp.where(even, other, near)
+    for here, start, row in ((GROUP - 1, NS_ROWS, 120), (0, NS_ROWS + EW_ROWS, 122)):
+        for k, flag in ((0, 57), (1, 56)):
+            flagged = (halo_ref[start + flag : start + flag + 1] == 1) & (place == here)
+            old = halo_ref[row + k : row + k + 1]
+            straight = far_ref[k : k + 1] + far2_ref[k : k + 1]
+            halo_ref[row + k : row + k + 1] = jnp.where(flagged, straight, old)
+    halo = halo_ref[...]
     flags = [flip_ref[0, k] for k in range(4)]
     north_e = jnp.where(flags[N_] == 1, cell(LAST, 0), cell(LAST, LAST))
     north_w = jnp.where(flags[N_] == 1, cell(LAST, LAST), cell(LAST, 0))
@@ -307,6 +348,10 @@
 SMEM = pl.BlockSpec(memory_space=pltpu.SMEM)
 
 
+def room(mebibytes):
+    return pltpu.CompilerParams(vmem_limit_bytes=mebibytes * 2**20)
+
+
 def local(control, perts, diffusivity, vertical, gain, edge_flip):
     member_count, level_count, cell_count = control.shape
     tile_count = lax.axis_size("tile")
@@ -314,37 +359,37 @@
     lanes = member_count * level_count
     west_table, east_table, ns_table, q_table = pack_cells()
 
-    def shifted(value, by):
-        return lax.ppermute(value, "tile", [(i, (i + by) % tile_count) for i in range(tile_count)])
+    place = (lax.axis_index("tile") % GROUP).astype(jnp.int32).reshape(1, 1)
+
+    def exchanged(value, pairs):
+        both = [(i % tile_count, j % tile_count) for i, j in pairs]
+        return lax.ppermute(value, "tile", both + [(j, i) for i, j in both])
 
     def swapped(value, mask):
         return lax.ppermute(value, "tile", [(i, i ^ mask) for i in range(tile_count)])
 
+    half = tile_count // 2
+    edges = range(GROUP, tile_count + 1, GROUP)
+    pairs = [(i, i + 1) for i in range(0, tile_count, 2)]
+    between = [(i, i + 1) for i in range(1, tile_count, 2) if (i + 1) % GROUP]
+
     def rows_of(count):
         return jax.ShapeDtypeStruct((count, lanes), jnp.float32)
 
     table = table_columns(west_table + east_table + ns_table + q_table + [(0, 0, -1)] * 4)
-    west_pack, east_pack, west_far, east_far, strips = pl.pallas_call(
+    first, second, far, strips = pl.pallas_call(
         pack_kernel,
-        out_shape=[rows_of(EW_ROWS), rows_of(EW_ROWS), rows_of(8), rows_of(8), rows_of(104)],
-        in_specs=vmem(1) + [SMEM] + vmem(1),
-        out_specs=vmem(5),
+        out_shape=[rows_of(count) for count in (EW_ROWS, EW_ROWS, 8, 104)],
+        in_specs=vmem(1) + [SMEM, SMEM] + vmem(1),
+        out_specs=vmem(4),
         name="packs",
-    )(control, edge_flip, jnp.asarray(table))
-    from_east2 = shifted(west_far, -2)
-    from_west2 = shifted(east_far, 2)
-    from_east = shifted(west_pack, -1)
-    from_west = shifted(east_pack, 1)
-
-    ns_pack = pl.pallas_call(
-        relay_kernel,
-        out_shape=rows_of(NS_ROWS),
-        in_specs=vmem(5),
-        out_specs=vmem(1)[0],
-        name="relay",
-    )(strips, from_east, from_west, from_east2, from_west2)
-    arrived = swapped(ns_pack, tile_count // 2)
-
+    )(control, edge_flip, place, jnp.asarray(table))
+    direct = [((k + half + 1) % tile_count, k - 1) for k in edges]
+    direct += [((k + half - 2) % tile_count, k % tile_count) for k in edges]
+    wrap = exchanged(second, [(k - 1, k) for k in edges])
+    far1 = lax.ppermute(far, "tile", [pair for pair in direct if pair[1] < half])
+    near = exchanged(first, pairs)
+    control_there, first = lax.optimization_barrier((control, first))
     zero, one, edge = halo_rows()
     spread = diffusivity.reshape(1, level_count)
     wide = PASSES * cell_count
@@ -360,7 +405,7 @@
         out_specs=vmem(4),
         name="own_cells",
     )(
-        control,
+        control_there,
         spread,
         vertical,
         edge_flip,
@@ -369,25 +414,58 @@
         jnp.asarray(one, jnp.bfloat16),
         jnp.asarray(edge),
     )
-
-    sums = jnp.broadcast_to(ns_pack[126:127] + arrived[126:127], (8, lanes))
+    near, base = lax.optimization_barrier((near, base))
+    second = pl.pallas_call(
+        second_kernel, out_shape=rows_of(EW_ROWS), in_specs=vmem(2), out_specs=vmem(1)[0], name="second", compiler_params=room(4)
+    )(second, near)
+    other = exchanged(second, between)
+    back = pl.pallas_call(
+        third_kernel, out_shape=rows_of(8), in_specs=vmem(3), out_specs=vmem(1)[0], name="third", compiler_params=room(4)
+    )(second, other, wrap)
+    back = exchanged(back, pairs)
+    ns_pack = pl.pallas_call(
+        relay_kernel,
+        out_shape=rows_of(NS_ROWS),
+        in_specs=vmem(6) + [SMEM],
+        out_specs=vmem(1)[0],
+        name="relay", compiler_params=room(4),
+    )(strips, second, near, other, wrap, back, place)
+    arrived = exchanged(ns_pack, [(i, i + half) for i in range(half)])
+    far, ns_pack, far1 = lax.optimization_barrier((far, ns_pack, far1))
+    far2 = lax.ppermute(far, "tile", [pair for pair in direct if pair[1] >= half])
+
+    arrived, far2 = lax.optimization_barrier((arrived, far2))
+    sums = pl.pallas_call(
+        sums_kernel,
+        out_shape=rows_of(64),
+        in_specs=vmem(2),
+        out_specs=vmem(1)[0],
+        name="sums",
+        compiler_params=room(4),
+    )(ns_pack, arrived)
     groups = [
-        [low_bits + 32 * half + 4 * k for k in range(8)] for half in range(2) for low_bits in range(4)
+        [low_bits + half * k + 4 * i for i in range(8)] for k in range(2) for low_bits in range(4)
     ]
     sums = lax.all_to_all(sums, "tile", 0, 0, tiled=True, axis_index_groups=groups)
-
     pieces = pl.pallas_call(
         final_kernel,
         out_shape=jax.ShapeDtypeStruct((mem_count, level_count // mem_count, cell_count), jnp.float32),
-        in_specs=vmem(8) + [SMEM] + vmem(2),
+        in_specs=vmem(11) + [SMEM, SMEM] + vmem(2),
         out_specs=vmem(1)[0],
+        scratch_shapes=[pltpu.VMEM((NS_ROWS + 2 * EW_ROWS, lanes), jnp.float32)],
         name="localized",
-    )(base, operator, high, low, arrived, from_east, from_west, spread, edge_flip, perts, gain)
+        compiler_params=room(16),
+    )(
+        base, operator, high, low, arrived, near, other, wrap, far1, far2,
+        spread, edge_flip, place, perts, gain,
+    )
+    pieces, sums = lax.optimization_barrier((pieces, sums))
     pieces = lax.all_to_all(pieces, "mem", 0, 0, tiled=True)
     members_all = member_count * mem_count
     increment = jnp.sum(pieces, axis=0) / jnp.sqrt(jnp.float32(members_all - 1))
     norm_count = level_count * cell_count * tile_count
-    member_cost = 0.5 * jnp.sum(sums.reshape(8, member_count, level_count), axis=(0, 2)) / norm_count
+    sums = jnp.sum(sums.reshape(64, member_count, level_count), axis=(0, 2)) / 8.0
+    member_cost = 0.5 * sums / norm_count
     return (increment, member_cost)
 
 

time: 96.5 us -> 87 us (0.902)
  the two profiles are of different devices: /device:TPU:8 before, /device:TPU:1 now
where the time goes in v3:
time: 87 us; the launch traced here: 86.6 us
  starting transfers between devices  50.5 us (58%)
  waiting for transfers between devices  25.7 us (30%)
  Pallas kernels  7.53 us (9%)
  other arithmetic  1.28 us (1%)
  between operations  0.89 us (1%)
    ppermute x5, starting transfers between devices, exchanged(): return lax.ppermute(value, 'tile', both + [(j, i) for i, j in both])  36.4 us
    ppermute x1, waiting for transfers between devices, local(): lax.ppermute(far, 'tile', [pair for pair in direct if pair[1] < half])  12.3 us
    all_to_all x1, starting transfers between devices, local(): pieces = lax.all_to_all(pieces, 'mem', 0, 0, tiled=True)  8.63 us
    all_to_all x1, waiting for transfers between devices, local(): lax.all_to_all(sums, 'tile', 0, 0, tiled=True, axis_index_groups=groups)  6.61 us
    all_to_all x1, waiting for transfers between devices, local(): pieces = lax.all_to_all(pieces, 'mem', 0, 0, tiled=True)  4.26 us
    all_to_all x1, starting transfers between devices, local(): lax.all_to_all(sums, 'tile', 0, 0, tiled=True, axis_index_groups=groups)  3.48 us
    pallas_call x1, Pallas kernels, local(): pl.pallas_call(own_kernel, out_shape=[jax.ShapeDtypeStruct((lanes, cell_c...  2.71 us
    ppermute x5, waiting for transfers between devices, exchanged(): return lax.ppermute(value, 'tile', both + [(j, i) for i, j in both])  2.48 us
  transfers between devices with their start and end apart: 9, of which 4 were waited for; matrix products, arithmetic and copies ran while one was open for 1% of the time, Pallas kernels for 6%

profile of v3, /device:TPU:1, one launch (start us, length us, event | category | flops | bytes accessed | tf_op | source)
XLA Modules:
  0.0 86.6 jit_solution(9115020657961655306)
XLA Ops:
  0.6 2.1 %packs.1 = (f32[64,256]{1,0:T(8,128)}, f32[64,256]{1,0:T(8,128)}, f32[8,256]{1,0:T(8,128)}, f32[104,256]{1,0:T(8,128)}) custom-call(f32[8,32,256]{2,1,0:T(8,128)} %field_ref.2, s32[1,4]{1,0:T(1,128)} %flip_ref.5, s32[1,1]{1,0:T(1,128)} %bitcast.place_ref, s32[216,8]{1,0:T(8,128)} %constant.42.clone.table_ref), custom_call_target="tpu_custom_call" | custom-call | tf_op jit(solution)/shard_map/packs/pallas_call | solution.py:380
  2.7 4.0 %collective-permute-start = (f32[64,256]{1,0:T(8,128)}, f32[64,256]{1,0:T(8,128)S(1)}, u32[]{:S(2)}, u32[]{:S(2)}) collective-permute-start(f32[64,256]{1,0:T(8,128)} %get-tuple-element.20), channel_id=1, source_target_pairs={{0,8},{16,24},{32,40},{48,56},{64,72},{80,88},{96,104},{112,120},{... | collective-permute-start | bytes 196616 | tf_op jit(solution)/shard_map/ppermute | solution.py:366
  6.7 16.3 %collective-permute-start.2 = (f32[64,256]{1,0:T(8,128)}, f32[64,256]{1,0:T(8,128)S(1)}, u32[]{:S(2)}, u32[]{:S(2)}) collective-permute-start(f32[64,256]{1,0:T(8,128)} %get-tuple-element.28.second_ref), channel_id=1, source_target_pairs={{120,128},{248,256},{376,384},{504,0},{128,120},{256,248},{384,376... | collective-permute-start | bytes 196616 | tf_op jit(solution)/shard_map/ppermute | solution.py:366
  23.0 0.0 copy-start.6
  23.0 2.7 %own_cells.1 = (f32[256,256]{1,0:T(8,128)}, bf16[256,768]{1,0:T(8,128)(2,1)}, bf16[256,256]{1,0:T(8,128)(2,1)}, bf16[256,256]{1,0:T(8,128)(2,1)}) custom-call(f32[8,32,256]{2,1,0:T(8,128)} %field_ref.2, f32[1,32]{1,0:T(1,128)} %bitcast.4, f32[32,32]{1,0:T(8,128)} %vertical_ref.1, s32[1,4]{1,0:T(1,128)} %flip_ref.5, ...), custom_call_target="tpu_custom_call" | custom-call | tf_op jit(solution)/shard_map/own_cells/pallas_call | solution.py:396
  25.7 0.0 collective-permute-done.near_ref
  25.7 0.0 copy-done.6
  25.8 0.0 copy-start.7
  25.8 0.0 copy-start.5
  25.8 0.8 collective-permute-start.1
  26.6 0.0 collective-permute-done.2.wrap_ref
  26.6 0.0 collective-permute-done.1.other_ref
  26.6 0.0 copy-start.10
  26.6 0.0 copy-start.4
  26.7 2.1 %collective-permute-start.3 = (f32[8,256]{1,0:T(8,128)S(1)}, f32[8,256]{1,0:T(8,128)S(1)}, u32[]{:S(2)}, u32[]{:S(2)}) collective-permute-start(f32[8,256]{1,0:T(8,128)S(1)} %third.1), channel_id=1, source_target_pairs={{0,8},{16,24},{32,40},{48,56},{64,72},{80,88},{96,104},{112,120},{... | collective-permute-start | bytes 24584 | tf_op jit(solution)/shard_map/ppermute | solution.py:366
  28.7 2.5 %collective-permute-done.3.back_ref = f32[8,256]{1,0:T(8,128)S(1)} collective-permute-done((f32[8,256]{1,0:T(8,128)S(1)}, f32[8,256]{1,0:T(8,128)S(1)}, u32[]{:S(2)}, u32[]{:S(2)}) %collective-permute-start.3) | collective-permute-done | bytes 8224 | tf_op jit(solution)/shard_map/ppermute | solution.py:366
  31.2 0.0 copy-done.5
  31.2 0.0 copy-start
  31.2 0.0 copy-start.3
  31.2 0.0 copy-start.1
  31.2 13.3 %collective-permute-start.4 = (f32[128,256]{1,0:T(8,128)S(1)}, f32[128,256]{1,0:T(8,128)S(1)}, u32[]{:S(2)}, u32[]{:S(2)}) collective-permute-start(f32[128,256]{1,0:T(8,128)S(1)} %relay.1.sent_ref), channel_id=1, source_target_pairs={{0,256},{8,264},{16,272},{24,280},{32,288},{40,296},{48,304},{56,3... | collective-permute-start | bytes 393224 | tf_op jit(solution)/shard_map/ppermute | solution.py:366
  44.5 0.0 copy-done.10
  44.5 1.3 %collective-permute-start.5 = (f32[8,256]{1,0:T(8,128)S(1)}, f32[8,256]{1,0:T(8,128)S(1)}, u32[]{:S(2)}, u32[]{:S(2)}) collective-permute-start(f32[8,256]{1,0:T(8,128)S(1)} %copy-done.10), channel_id=1, source_target_pairs={{392,120},{8,248},{368,128},{240,0},{393,121},{9,249},{369,129},{2... | collective-permute-start | bytes 24584 | tf_op jit(solution)/shard_map/ppermute | solution.py:390
  45.8 12.3 %collective-permute-done.5.far_ref = f32[8,256]{1,0:T(8,128)S(1)} collective-permute-done((f32[8,256]{1,0:T(8,128)S(1)}, f32[8,256]{1,0:T(8,128)S(1)}, u32[]{:S(2)}, u32[]{:S(2)}) %collective-permute-start.5) | collective-permute-done | bytes 8224 | tf_op jit(solution)/shard_map/ppermute | solution.py:390
  58.2 0.7 collective-permute-start.6
  58.8 0.0 collective-permute-done.6.far2_ref
  58.8 0.0 collective-permute-done.4.arrived_ref
  58.8 0.6 sums.1
  59.5 0.0 copy-start.2
  59.5 3.5 %all-to-all-start = ((f32[8,8,256]{2,1,0:T(8,128)}), f32[8,8,256]{2,1,0:T(8,128)S(1)}, u32[]{:S(2)}, u32[]{:S(2)}) async-start(f32[8,8,256]{2,1,0:T(8,128)} %bitcast.2), calls=%async_computation | async-start | bytes 131072 | tf_op jit(solution)/shard_map/all_to_all | solution.py:449
  63.0 0.0 copy-start.8
  63.0 0.0 copy-start.9
  63.0 0.0 copy-done.7
  63.0 0.0 copy-done.4
  63.0 0.0 copy-done
  63.0 0.0 copy-done.3
  63.0 0.0 copy-done.1
  63.0 0.0 copy-done.2
  63.0 0.6 copy-done.8
  63.6 0.0 copy-done.9
  63.6 2.1 %localized.1 = f32[8,4,256]{2,1,0:T(4,128)} custom-call(f32[256,256]{1,0:T(8,128)S(1)} %copy-done.1, bf16[256,768]{1,0:T(8,128)(2,1)S(1)} %copy-done, bf16[256,256]{1,0:T(8,128)(2,1)S(1)} %copy-done.3, bf16[256,256]{1,0:T(8,128)(2,1)S(1)} %copy-done.4, f32[128,256]{1,0:T(8,128)S(1)} %collective-permute-done.4.arrived_ref, ...), custom_call_target="tpu_custom_call" | custom-call | tf_op jit(solution)/shard_map/localized/pallas_call | solution.py:450
  65.7 6.6 %all-to-all-done = f32[8,8,256]{2,1,0:T(8,128)S(1)} async-done(((f32[8,8,256]{2,1,0:T(8,128)}), f32[8,8,256]{2,1,0:T(8,128)S(1)}, u32[]{:S(2)}, u32[]{:S(2)}) %all-to-all-start) | async-done | bytes 65568 | tf_op jit(solution)/shard_map/all_to_all | solution.py:449
  72.3 8.6 %all-to-all-start.1 = ((f32[8,4,256]{2,1,0:T(4,128)}), f32[8,4,256]{2,1,0:T(4,128)S(1)}, u32[]{:S(2)}, u32[]{:S(2)}) async-start(f32[8,4,256]{2,1,0:T(4,128)} %localized.1), calls=%async_computation.1 | async-start | bytes 65536 | tf_op jit(solution)/shard_map/all_to_all | solution.py:463
  81.0 0.1 reduce_sum.27
  81.1 0.1 reduce_sum.28
  81.2 0.5 broadcast_multiply_fusion.1
  81.7 4.3 %all-to-all-done.1 = f32[8,4,256]{2,1,0:T(4,128)S(1)} async-done(((f32[8,4,256]{2,1,0:T(4,128)}), f32[8,4,256]{2,1,0:T(4,128)S(1)}, u32[]{:S(2)}, u32[]{:S(2)}) %all-to-all-start.1) | async-done | bytes 32800 | tf_op jit(solution)/shard_map/all_to_all | solution.py:463
  86.0 0.6 broadcast_multiply_fusion
  (5 shorter events, 0.1 us)
Async XLA Ops:
  2.7 23.0 %collective-permute-start = (f32[64,256]{1,0:T(8,128)}, f32[64,256]{1,0:T(8,128)S(1)}, u32[]{:S(2)}, u32[]{:S(2)}) collective-permute-start(f32[64,256]{1,0:T(8,128)} %get-tuple-element.20), channel_id=1, source_target_pairs={{0,8},{16,24},{32,40},{48,56},{64,72},{80,88},{96,104},{112,120},{... | collective-permute-start | bytes 196616 | tf_op jit(solution)/shard_map/ppermute | solution.py:366
  6.7 19.9 %collective-permute-start.2 = (f32[64,256]{1,0:T(8,128)}, f32[64,256]{1,0:T(8,128)S(1)}, u32[]{:S(2)}, u32[]{:S(2)}) collective-permute-start(f32[64,256]{1,0:T(8,128)} %get-tuple-element.28.second_ref), channel_id=1, source_target_pairs={{120,128},{248,256},{376,384},{504,0},{128,120},{256,248},{384,376... | collective-permute-start | bytes 196616 | tf_op jit(solution)/shard_map/ppermute | solution.py:366
  23.0 2.7 %copy-start.6 = (f32[64,256]{1,0:T(8,128)S(1)}, f32[64,256]{1,0:T(8,128)}, u32[]{:S(2)}) copy-start(f32[64,256]{1,0:T(8,128)} %get-tuple-element.28.second_ref) | copy-start | bytes 196612
  25.8 37.2 %copy-start.7 = (f32[32,256]{1,0:T(8,128)S(1)}, f32[32,256]{1,0:T(8,128)}, u32[]{:S(2)}) copy-start(f32[32,256]{1,0:T(8,128)} %gain_ref.1) | copy-start | bytes 98308
  25.8 5.4 %copy-start.5 = (f32[104,256]{1,0:T(8,128)S(1)}, f32[104,256]{1,0:T(8,128)}, u32[]{:S(2)}) copy-start(f32[104,256]{1,0:T(8,128)} %get-tuple-element.27.strips_ref) | copy-start | bytes 319492
  25.8 0.8 collective-permute-start.1
  26.6 17.9 %copy-start.10 = (f32[8,256]{1,0:T(8,128)S(1)}, f32[8,256]{1,0:T(8,128)}, u32[]{:S(2)}) copy-start(f32[8,256]{1,0:T(8,128)} %get-tuple-element.31) | copy-start | bytes 24580
  26.6 36.4 %copy-start.4 = (bf16[256,256]{1,0:T(8,128)(2,1)S(1)}, bf16[256,256]{1,0:T(8,128)(2,1)}, u32[]{:S(2)}) copy-start(bf16[256,256]{1,0:T(8,128)(2,1)} %get-tuple-element.26.low_ref) | copy-start | bytes 393220
  26.7 4.5 %collective-permute-start.3 = (f32[8,256]{1,0:T(8,128)S(1)}, f32[8,256]{1,0:T(8,128)S(1)}, u32[]{:S(2)}, u32[]{:S(2)}) collective-permute-start(f32[8,256]{1,0:T(8,128)S(1)} %third.1), channel_id=1, source_target_pairs={{0,8},{16,24},{32,40},{48,56},{64,72},{80,88},{96,104},{112,120},{... | collective-permute-start | bytes 24584 | tf_op jit(solution)/shard_map/ppermute | solution.py:366
  31.2 31.8 %copy-start = (bf16[256,768]{1,0:T(8,128)(2,1)S(1)}, bf16[256,768]{1,0:T(8,128)(2,1)}, u32[]{:S(2)}) copy-start(bf16[256,768]{1,0:T(8,128)(2,1)} %get-tuple-element.24.operator_ref) | copy-start | bytes 1179652
  31.2 31.8 %copy-start.3 = (bf16[256,256]{1,0:T(8,128)(2,1)S(1)}, bf16[256,256]{1,0:T(8,128)(2,1)}, u32[]{:S(2)}) copy-start(bf16[256,256]{1,0:T(8,128)(2,1)} %get-tuple-element.25.high_ref) | copy-start | bytes 393220
  31.2 31.8 %copy-start.1 = (f32[256,256]{1,0:T(8,128)S(1)}, f32[256,256]{1,0:T(8,128)}, u32[]{:S(2)}) copy-start(f32[256,256]{1,0:T(8,128)} %get-tuple-element.23.base_ref) | copy-start | bytes 786436
  31.2 27.6 %collective-permute-start.4 = (f32[128,256]{1,0:T(8,128)S(1)}, f32[128,256]{1,0:T(8,128)S(1)}, u32[]{:S(2)}, u32[]{:S(2)}) collective-permute-start(f32[128,256]{1,0:T(8,128)S(1)} %relay.1.sent_ref), channel_id=1, source_target_pairs={{0,256},{8,264},{16,272},{24,280},{32,288},{40,296},{48,304},{56,3... | collective-permute-start | bytes 393224 | tf_op jit(solution)/shard_map/ppermute | solution.py:366
  44.5 13.6 %collective-permute-start.5 = (f32[8,256]{1,0:T(8,128)S(1)}, f32[8,256]{1,0:T(8,128)S(1)}, u32[]{:S(2)}, u32[]{:S(2)}) collective-permute-start(f32[8,256]{1,0:T(8,128)S(1)} %copy-done.10), channel_id=1, source_target_pairs={{392,120},{8,248},{368,128},{240,0},{393,121},{9,249},{369,129},{2... | collective-permute-start | bytes 24584 | tf_op jit(solution)/shard_map/ppermute | solution.py:390
  58.2 0.7 collective-permute-start.6
  59.5 3.6 %copy-start.2 = (bf16[8,32,256]{2,1,0:T(8,128)(2,1)S(1)}, bf16[8,32,256]{2,1,0:T(8,128)(2,1)}, u32[]{:S(2)}) copy-start(bf16[8,32,256]{2,1,0:T(8,128)(2,1)} %perts_ref.1) | copy-start | bytes 393220
  59.5 12.9 %all-to-all-start = ((f32[8,8,256]{2,1,0:T(8,128)}), f32[8,8,256]{2,1,0:T(8,128)S(1)}, u32[]{:S(2)}, u32[]{:S(2)}) async-start(f32[8,8,256]{2,1,0:T(8,128)} %bitcast.2), calls=%async_computation | async-start | bytes 131072 | tf_op jit(solution)/shard_map/all_to_all | solution.py:449
  63.0 0.7 copy-start.8
  63.0 0.7 copy-start.9
  72.3 13.6 %all-to-all-start.1 = ((f32[8,4,256]{2,1,0:T(4,128)}), f32[8,4,256]{2,1,0:T(4,128)S(1)}, u32[]{:S(2)}, u32[]{:S(2)}) async-start(f32[8,4,256]{2,1,0:T(4,128)} %localized.1), calls=%async_computation.1 | async-start | bytes 65536 | tf_op jit(solution)/shard_map/all_to_all | solution.py:463

commit v4 on v3

--- a/solution.py
+++ b/solution.py
@@ -138,7 +138,7 @@
     return flag
 
 
-def pack_kernel(field_ref, flip_ref, place_ref, table_ref, first_ref, second_ref, far_ref, strips_ref):
+def pack_kernel(field_ref, flip_ref, place_ref, table_ref, first_ref, second_ref, wrap_ref, strips_ref):
     field = field_ref[...].reshape(-1, CELLS)
     lanes = field.shape[0]
     flags = [flip_ref[0, k] for k in range(4)]
@@ -163,9 +163,8 @@
         ref[57:58] = level[N_]
         ref[58:59] = norms
         ref[59:64] = jnp.zeros((5, lanes), jnp.float32)
-    far_ref[0:1] = first_ref[0:1]
-    far_ref[1:2] = first_ref[LAST : LAST + 1]
-    far_ref[2:8] = jnp.zeros((6, lanes), jnp.float32)
+    at_end = (place_ref[0, 0] == 0) | (place_ref[0, 0] == GROUP - 1)
+    wrap_ref[...] = jnp.where(at_end, second_ref[...], first_ref[...])
     strips_ref[0:100] = rows[112:212]
     strips_ref[100:101] = level[E_]
     strips_ref[101:102] = level[W_]
@@ -181,18 +180,25 @@
     out_ref[62:64] = jnp.zeros((2, out_ref.shape[1]), jnp.float32)
 
 
-def third_kernel(second_ref, other_ref, wrap_ref, out_ref):
-    out_ref[0:1] = other_ref[0:1] + wrap_ref[0:1]
-    out_ref[1:2] = other_ref[LAST : LAST + 1] + wrap_ref[LAST : LAST + 1]
+def across(place, other, wrap):
+    return jnp.where((place == 0) | (place == GROUP - 1), wrap, other)
+
+
+def third_kernel(second_ref, other_ref, wrap_ref, place_ref, out_ref):
+    place = place_ref[0, 0]
+    out_ref[0:1] = across(place, other_ref[0:1], wrap_ref[0:1])
+    out_ref[1:2] = across(place, other_ref[LAST : LAST + 1], wrap_ref[LAST : LAST + 1])
     out_ref[2:3] = second_ref[61:62] + other_ref[61:62]
-    out_ref[3:8] = jnp.zeros((5, out_ref.shape[1]), jnp.float32)
-
-
-def relay_kernel(strips_ref, second_ref, near_ref, other_ref, wrap_ref, back_ref, place_ref, out_ref):
+    out_ref[3:4] = wrap_ref[0:1]
+    out_ref[4:5] = wrap_ref[LAST : LAST + 1]
+    out_ref[5:8] = jnp.zeros((3, out_ref.shape[1]), jnp.float32)
+
+
+def relay_kernel(strips_ref, second_ref, near_ref, other_ref, wrap_ref, back_ref, place_ref, out_ref, sums_ref):
     place = place_ref[0, 0]
     even = place % 2 == 0
     near = near_ref[...]
-    other = other_ref[...] + wrap_ref[...]
+    other = across(place, other_ref[...], wrap_ref[...])
     out_ref[0:96] = strips_ref[0:96]
     row = 96
     for pack, far in (
@@ -210,8 +216,9 @@
         out_ref[120 + 2 * side : 122 + 2 * side] = jnp.where(pack[56:58] == 1, far, own)
     out_ref[124:126] = strips_ref[100:102]
     y = place % 4
-    out_ref[126:127] = jnp.where((y == 1) | (y == 2), second_ref[61:62] + other[61:62], back_ref[2:3])
-    out_ref[127:128] = jnp.zeros((1, out_ref.shape[1]), jnp.float32)
+    sums = jnp.where((y == 1) | (y == 2), second_ref[61:62] + other[61:62], back_ref[2:3])
+    out_ref[126:128] = jnp.zeros((2, out_ref.shape[1]), jnp.float32)
+    sums_ref[...] = jnp.broadcast_to(sums, sums_ref.shape)
 
 
 def rate_column(diffusivity_ref, member_count):
@@ -252,12 +259,8 @@
     high_ref[...] = high
     low_ref[...] = low
 
-def sums_kernel(sent_ref, arrived_ref, out_ref):
-    out_ref[...] = jnp.broadcast_to(sent_ref[126:127] + arrived_ref[126:127], out_ref.shape)
-
-
 def final_kernel(
-    base_ref, operator_ref, high_ref, low_ref, arrived_ref, near_ref, other_ref, wrap_ref, far_ref, far2_ref,
+    base_ref, operator_ref, high_ref, low_ref, arrived_ref, near_ref, other_ref, wrap_ref, back_ref,
     diffusivity_ref, flip_ref, place_ref, perts_ref, gain_ref, term_ref,
     halo_ref,
 ):
@@ -266,7 +269,7 @@
     place = place_ref[0, 0]
     even = place % 2 == 0
     near = near_ref[...]
-    other = other_ref[...] + wrap_ref[...]
+    other = across(place, other_ref[...], wrap_ref[...])
     halo_ref[0:NS_ROWS] = arrived_ref[...]
     halo_ref[NS_ROWS : NS_ROWS + EW_ROWS] = jnp.where(even, near, other)
     halo_ref[NS_ROWS + EW_ROWS :] = jnp.where(even, other, near)
@@ -274,8 +277,7 @@
         for k, flag in ((0, 57), (1, 56)):
             flagged = (halo_ref[start + flag : start + flag + 1] == 1) & (place == here)
             old = halo_ref[row + k : row + k + 1]
-            straight = far_ref[k : k + 1] + far2_ref[k : k + 1]
-            halo_ref[row + k : row + k + 1] = jnp.where(flagged, straight, old)
+            halo_ref[row + k : row + k + 1] = jnp.where(flagged, back_ref[3 + k : 4 + k], old)
     halo = halo_ref[...]
     flags = [flip_ref[0, k] for k in range(4)]
     north_e = jnp.where(flags[N_] == 1, cell(LAST, 0), cell(LAST, LAST))
@@ -377,17 +379,14 @@
         return jax.ShapeDtypeStruct((count, lanes), jnp.float32)
 
     table = table_columns(west_table + east_table + ns_table + q_table + [(0, 0, -1)] * 4)
-    first, second, far, strips = pl.pallas_call(
+    first, second, wrap, strips = pl.pallas_call(
         pack_kernel,
-        out_shape=[rows_of(count) for count in (EW_ROWS, EW_ROWS, 8, 104)],
+        out_shape=[rows_of(count) for count in (EW_ROWS, EW_ROWS, EW_ROWS, 104)],
         in_specs=vmem(1) + [SMEM, SMEM] + vmem(1),
         out_specs=vmem(4),
         name="packs",
     )(control, edge_flip, place, jnp.asarray(table))
-    direct = [((k + half + 1) % tile_count, k - 1) for k in edges]
-    direct += [((k + half - 2) % tile_count, k % tile_count) for k in edges]
-    wrap = exchanged(second, [(k - 1, k) for k in edges])
-    far1 = lax.ppermute(far, "tile", [pair for pair in direct if pair[1] < half])
+    wrap = exchanged(wrap, [(k - 1, k) for k in edges] + [(k - 2, k + 1 + half) for k in edges])
     near = exchanged(first, pairs)
     control_there, first = lax.optimization_barrier((control, first))
     zero, one, edge = halo_rows()
@@ -420,51 +419,37 @@
     )(second, near)
     other = exchanged(second, between)
     back = pl.pallas_call(
-        third_kernel, out_shape=rows_of(8), in_specs=vmem(3), out_specs=vmem(1)[0], name="third", compiler_params=room(4)
-    )(second, other, wrap)
+        third_kernel, out_shape=rows_of(8), in_specs=vmem(3) + [SMEM], out_specs=vmem(1)[0], name="third", compiler_params=room(4)
+    )(second, other, wrap, place)
     back = exchanged(back, pairs)
-    ns_pack = pl.pallas_call(
+    ns_pack, sums = pl.pallas_call(
         relay_kernel,
-        out_shape=rows_of(NS_ROWS),
+        out_shape=[rows_of(NS_ROWS), rows_of(16)],
         in_specs=vmem(6) + [SMEM],
-        out_specs=vmem(1)[0],
+        out_specs=vmem(2),
         name="relay", compiler_params=room(4),
     )(strips, second, near, other, wrap, back, place)
     arrived = exchanged(ns_pack, [(i, i + half) for i in range(half)])
-    far, ns_pack, far1 = lax.optimization_barrier((far, ns_pack, far1))
-    far2 = lax.ppermute(far, "tile", [pair for pair in direct if pair[1] >= half])
-
-    arrived, far2 = lax.optimization_barrier((arrived, far2))
-    sums = pl.pallas_call(
-        sums_kernel,
-        out_shape=rows_of(64),
-        in_specs=vmem(2),
-        out_specs=vmem(1)[0],
-        name="sums",
-        compiler_params=room(4),
-    )(ns_pack, arrived)
-    groups = [
-        [low_bits + half * k + 4 * i for i in range(8)] for k in range(2) for low_bits in range(4)
-    ]
+    groups = [list(range(low_bits, tile_count, 4)) for low_bits in range(4)]
     sums = lax.all_to_all(sums, "tile", 0, 0, tiled=True, axis_index_groups=groups)
     pieces = pl.pallas_call(
         final_kernel,
         out_shape=jax.ShapeDtypeStruct((mem_count, level_count // mem_count, cell_count), jnp.float32),
-        in_specs=vmem(11) + [SMEM, SMEM] + vmem(2),
+        in_specs=vmem(10) + [SMEM, SMEM] + vmem(2),
         out_specs=vmem(1)[0],
         scratch_shapes=[pltpu.VMEM((NS_ROWS + 2 * EW_ROWS, lanes), jnp.float32)],
         name="localized",
-        compiler_params=room(16),
+                cost_estimate=pl.CostEstimate(flops=3450000000, bytes_accessed=1000000, transcendentals=0),
     )(
-        base, operator, high, low, arrived, near, other, wrap, far1, far2,
+        base, operator, high, low, arrived, near, other, wrap, back,
         spread, edge_flip, place, perts, gain,
     )
-    pieces, sums = lax.optimization_barrier((pieces, sums))
+    sums, pieces = lax.optimization_barrier((sums, pieces))
     pieces = lax.all_to_all(pieces, "mem", 0, 0, tiled=True)
     members_all = member_count * mem_count
     increment = jnp.sum(pieces, axis=0) / jnp.sqrt(jnp.float32(members_all - 1))
     norm_count = level_count * cell_count * tile_count
-    sums = jnp.sum(sums.reshape(64, member_count, level_count), axis=(0, 2)) / 8.0
+    sums = jnp.sum(sums.reshape(16, member_count, level_count), axis=(0, 2))
     member_cost = 0.5 * sums / norm_count
     return (increment, member_cost)
 

time: 87 us -> 79.6 us (0.915)
  waiting for transfers between devices: 25.7 us -> 5.52 us
  blocking collectives: 0 us -> 16.2 us
  starting transfers between devices: 50.5 us -> 46.2 us
    all_to_all x0 -> x1, blocking collectives: none -> 16.2 us  [local(): lax.all_to_all(sums, 'tile', 0, 0, tiled=True, axis_index_groups=groups)]
    ppermute x2 -> x0, waiting for transfers between devices: 12.3 us -> none  [the longest x1 12.3 us: local(): lax.ppermute(far, 'tile', [pair for pair in direct if pair[1] < half])]
    all_to_all x1 -> x0, waiting for transfers between devices: 6.61 us -> none  [local(): lax.all_to_all(sums, 'tile', 0, 0, tiled=True, axis_index_groups=groups)]
    all_to_all x1 -> x0, starting transfers between devices: 3.48 us -> none  [local(): lax.all_to_all(sums, 'tile', 0, 0, tiled=True, axis_index_groups=groups)]
    ppermute x2 -> x0, starting transfers between devices: 1.94 us -> none  [the longest x1 1.29 us: local(): lax.ppermute(far, 'tile', [pair for pair in direct if pair[1] < half])]
    ppermute x5, waiting for transfers between devices: 2.48 us -> 1.04 us  [exchanged(): return lax.ppermute(value, 'tile', both + [(j, i) for i, j in both])]
    ppermute x5, starting transfers between devices: 36.4 us -> 37.6 us  [exchanged(): return lax.ppermute(value, 'tile', both + [(j, i) for i, j in both])]
  transfers between devices with their start and end apart: 9 -> 6, of which waited for: 4 -> 2; matrix products, arithmetic and copies ran while one was open for 1% -> 1% of each run, Pallas kernels for 6% -> 3%
where the time goes in v4:
time: 79.6 us; the launch traced here: 79 us
  starting transfers between devices  46.2 us (58%)
  blocking collectives  16.2 us (20%)
  Pallas kernels  7.71 us (10%)
  waiting for transfers between devices  5.52 us (7%)
  local copies, waits for them, and re-layouts  1.3 us (2%)
  other arithmetic  1.27 us (2%)
  between operations  0.8 us (1%)
    ppermute x5, starting transfers between devices, exchanged(): return lax.ppermute(value, 'tile', both + [(j, i) for i, j in both])  37.6 us
    all_to_all x1, blocking collectives, local(): lax.all_to_all(sums, 'tile', 0, 0, tiled=True, axis_index_groups=groups)  16.2 us
    all_to_all x1, starting transfers between devices, local(): pieces = lax.all_to_all(pieces, 'mem', 0, 0, tiled=True)  8.59 us
    all_to_all x1, waiting for transfers between devices, local(): pieces = lax.all_to_all(pieces, 'mem', 0, 0, tiled=True)  4.49 us
    pallas_call x1, Pallas kernels, local(): pl.pallas_call(final_kernel, out_shape=jax.ShapeDtypeStruct((mem_count, l...  2.88 us
    pallas_call x1, Pallas kernels, local(): pl.pallas_call(own_kernel, out_shape=[jax.ShapeDtypeStruct((lanes, cell_c...  2.69 us
    pallas_call x1, Pallas kernels, local(): pl.pallas_call(pack_kernel, out_shape=[rows_of(count) for count in (EW_RO...  2.09 us
  transfers between devices with their start and end apart: 6, of which 2 were waited for; matrix products, arithmetic and copies ran while one was open for 1% of the time, Pallas kernels for 3%

profile of v4, /device:TPU:1, one launch (start us, length us, event | category | flops | bytes accessed | tf_op | source)
XLA Modules:
  0.0 79.0 jit_solution(9048524999493881335)
XLA Ops:
  0.6 2.1 %packs.1 = (f32[64,256]{1,0:T(8,128)}, f32[64,256]{1,0:T(8,128)}, f32[64,256]{1,0:T(8,128)}, f32[104,256]{1,0:T(8,128)}) custom-call(f32[8,32,256]{2,1,0:T(8,128)} %field_ref.2, s32[1,4]{1,0:T(1,128)} %flip_ref.5, s32[1,1]{1,0:T(1,128)} %bitcast.place_ref, s32[216,8]{1,0:T(8,128)} %constant.39.clone.table_ref), custom_call_target="tpu_custom_call" | custom-call | tf_op jit(solution)/shard_map/packs/pallas_call | solution.py:382
  2.7 4.0 %collective-permute-start = (f32[64,256]{1,0:T(8,128)}, f32[64,256]{1,0:T(8,128)S(1)}, u32[]{:S(2)}, u32[]{:S(2)}) collective-permute-start(f32[64,256]{1,0:T(8,128)} %get-tuple-element.19), channel_id=1, source_target_pairs={{0,8},{16,24},{32,40},{48,56},{64,72},{80,88},{96,104},{112,120},{... | collective-permute-start | bytes 196616 | tf_op jit(solution)/shard_map/ppermute | solution.py:368
  6.8 16.3 %collective-permute-start.2 = (f32[64,256]{1,0:T(8,128)}, f32[64,256]{1,0:T(8,128)S(1)}, u32[]{:S(2)}, u32[]{:S(2)}) collective-permute-start(f32[64,256]{1,0:T(8,128)} %get-tuple-element.23), channel_id=1, source_target_pairs={{120,128},{248,256},{376,384},{504,0},{112,392},{240,8},{368,136},... | collective-permute-start | bytes 196616 | tf_op jit(solution)/shard_map/ppermute | solution.py:368
  23.0 0.0 copy-start.4
  23.0 2.7 %own_cells.1 = (f32[256,256]{1,0:T(8,128)}, bf16[256,768]{1,0:T(8,128)(2,1)}, bf16[256,256]{1,0:T(8,128)(2,1)}, bf16[256,256]{1,0:T(8,128)(2,1)}) custom-call(f32[8,32,256]{2,1,0:T(8,128)} %field_ref.2, f32[1,32]{1,0:T(1,128)} %bitcast.8, f32[32,32]{1,0:T(8,128)} %vertical_ref.1, s32[1,4]{1,0:T(1,128)} %flip_ref.5, ...), custom_call_target="tpu_custom_call" | custom-call | tf_op jit(solution)/shard_map/own_cells/pallas_call | solution.py:395
  25.7 0.0 collective-permute-done.near_ref
  25.7 0.0 copy-start
  25.7 0.0 copy-done.4
  25.8 0.0 copy-start.3
  25.8 0.8 %collective-permute-start.1 = (f32[64,256]{1,0:T(8,128)S(1)}, f32[64,256]{1,0:T(8,128)S(1)}, u32[]{:S(2)}, u32[]{:S(2)}) collective-permute-start(f32[64,256]{1,0:T(8,128)S(1)} %second.1.second_ref), channel_id=1, source_target_pairs={{8,16},{24,32},{40,48},{56,64},{72,80},{88,96},{104,112},{136,144}... | collective-permute-start | bytes 196616 | tf_op jit(solution)/shard_map/ppermute | solution.py:368
  26.6 0.0 collective-permute-done.2.wrap_ref
  26.6 0.0 copy-start.1
  26.6 0.0 collective-permute-done.1.other_ref
  26.6 0.0 copy-start.2
  26.6 3.6 %collective-permute-start.3 = (f32[8,256]{1,0:T(8,128)S(1)}, f32[8,256]{1,0:T(8,128)S(1)}, u32[]{:S(2)}, u32[]{:S(2)}) collective-permute-start(f32[8,256]{1,0:T(8,128)S(1)} %third.1), channel_id=1, source_target_pairs={{0,8},{16,24},{32,40},{48,56},{64,72},{80,88},{96,104},{112,120},{... | collective-permute-start | bytes 24584 | tf_op jit(solution)/shard_map/ppermute | solution.py:368
  30.2 1.0 %collective-permute-done.3.back_ref = f32[8,256]{1,0:T(8,128)S(1)} collective-permute-done((f32[8,256]{1,0:T(8,128)S(1)}, f32[8,256]{1,0:T(8,128)S(1)}, u32[]{:S(2)}, u32[]{:S(2)}) %collective-permute-start.3) | collective-permute-done | bytes 8224 | tf_op jit(solution)/shard_map/ppermute | solution.py:368
  31.2 0.0 copy-start.5
  31.2 0.0 copy-done
  31.2 0.0 copy-done.1
  31.3 0.0 copy-done.2
  31.3 0.0 copy-done.3
  31.3 0.5 copy-done.5
  31.8 13.0 %collective-permute-start.4 = (f32[128,256]{1,0:T(8,128)S(1)}, f32[128,256]{1,0:T(8,128)S(1)}, u32[]{:S(2)}, u32[]{:S(2)}) collective-permute-start(f32[128,256]{1,0:T(8,128)S(1)} %get-tuple-element.29), channel_id=1, source_target_pairs={{0,256},{8,264},{16,272},{24,280},{32,288},{40,296},{48,304},{56,3... | collective-permute-start | bytes 393224 | tf_op jit(solution)/shard_map/ppermute | solution.py:368
  44.8 16.2 %all_to_all.17 = f32[16,1,256]{2,1,0:T(1,128)S(1)} all-to-all(f32[16,1,256]{2,1,0:T(1,128)S(1)} %copy.14), channel_id=1, replica_groups={{0,32,64,96,128,160,192,224,256,288,320,352,384,416,448,480},{8,40,72,1..., dimensions={0} | all-to-all | bytes 32768 | tf_op jit(solution)/shard_map/all_to_all | solution.py:434
  61.0 0.0 collective-permute-done.4.arrived_ref
  61.0 0.0 copy-start.6
  61.0 0.6 copy-done.6
  61.7 2.9 %localized.1 = f32[8,4,256]{2,1,0:T(4,128)} custom-call(f32[256,256]{1,0:T(8,128)} %get-tuple-element.25.base_ref, bf16[256,768]{1,0:T(8,128)(2,1)} %get-tuple-element.26.operator_ref, bf16[256,256]{1,0:T(8,128)(2,1)} %get-tuple-element.27.high_ref, bf16[256,256]{1,0:T(8,128)(2,1)} %get-tuple-element.28.low_ref, f32[128,256]{1,0:T(8,128)} %copy-done.6, ...), custom_call_target="tpu_custom_call" | custom-call | flops 3449999872 | bytes 1000000 | tf_op jit(solution)/shard_map/localized/pallas_call | solution.py:435
  64.6 0.1 reduce_sum.27
  64.7 0.1 reduce_sum.28
  64.8 8.6 %all-to-all-start.1 = ((f32[8,4,256]{2,1,0:T(4,128)}), f32[8,4,256]{2,1,0:T(4,128)S(1)}, u32[]{:S(2)}, u32[]{:S(2)}) async-start(f32[8,4,256]{2,1,0:T(4,128)} %localized.1), calls=%async_computation.1 | async-start | bytes 65536 | tf_op jit(solution)/shard_map/all_to_all | solution.py:448
  73.4 0.5 broadcast_multiply_fusion.1
  73.9 4.5 %all-to-all-done.1 = f32[8,4,256]{2,1,0:T(4,128)S(1)} async-done(((f32[8,4,256]{2,1,0:T(4,128)}), f32[8,4,256]{2,1,0:T(4,128)S(1)}, u32[]{:S(2)}, u32[]{:S(2)}) %all-to-all-start.1) | async-done | bytes 32800 | tf_op jit(solution)/shard_map/all_to_all | solution.py:448
  78.4 0.6 broadcast_multiply_fusion
  (7 shorter events, 0.1 us)
Async XLA Ops:
  2.7 23.0 %collective-permute-start = (f32[64,256]{1,0:T(8,128)}, f32[64,256]{1,0:T(8,128)S(1)}, u32[]{:S(2)}, u32[]{:S(2)}) collective-permute-start(f32[64,256]{1,0:T(8,128)} %get-tuple-element.19), channel_id=1, source_target_pairs={{0,8},{16,24},{32,40},{48,56},{64,72},{80,88},{96,104},{112,120},{... | collective-permute-start | bytes 196616 | tf_op jit(solution)/shard_map/ppermute | solution.py:368
  6.8 19.8 %collective-permute-start.2 = (f32[64,256]{1,0:T(8,128)}, f32[64,256]{1,0:T(8,128)S(1)}, u32[]{:S(2)}, u32[]{:S(2)}) collective-permute-start(f32[64,256]{1,0:T(8,128)} %get-tuple-element.23), channel_id=1, source_target_pairs={{120,128},{248,256},{376,384},{504,0},{112,392},{240,8},{368,136},... | collective-permute-start | bytes 196616 | tf_op jit(solution)/shard_map/ppermute | solution.py:368
  23.0 2.7 %copy-start.4 = (f32[64,256]{1,0:T(8,128)S(1)}, f32[64,256]{1,0:T(8,128)}, u32[]{:S(2)}) copy-start(f32[64,256]{1,0:T(8,128)} %get-tuple-element.18.second_ref) | copy-start | bytes 196612
  25.7 5.5 %copy-start = (f32[64,256]{1,0:T(8,128)}, f32[64,256]{1,0:T(8,128)S(1)}, u32[]{:S(2)}) copy-start(f32[64,256]{1,0:T(8,128)S(1)} %collective-permute-done.near_ref) | copy-start | bytes 196612
  25.8 5.5 %copy-start.3 = (f32[104,256]{1,0:T(8,128)S(1)}, f32[104,256]{1,0:T(8,128)}, u32[]{:S(2)}) copy-start(f32[104,256]{1,0:T(8,128)} %get-tuple-element.17.strips_ref) | copy-start | bytes 319492
  25.8 0.8 %collective-permute-start.1 = (f32[64,256]{1,0:T(8,128)S(1)}, f32[64,256]{1,0:T(8,128)S(1)}, u32[]{:S(2)}, u32[]{:S(2)}) collective-permute-start(f32[64,256]{1,0:T(8,128)S(1)} %second.1.second_ref), channel_id=1, source_target_pairs={{8,16},{24,32},{40,48},{56,64},{72,80},{88,96},{104,112},{136,144}... | collective-permute-start | bytes 196616 | tf_op jit(solution)/shard_map/ppermute | solution.py:368
  26.6 4.7 %copy-start.1 = (f32[64,256]{1,0:T(8,128)}, f32[64,256]{1,0:T(8,128)S(1)}, u32[]{:S(2)}) copy-start(f32[64,256]{1,0:T(8,128)S(1)} %collective-permute-done.2.wrap_ref) | copy-start | bytes 196612
  26.6 4.6 %copy-start.2 = (f32[64,256]{1,0:T(8,128)}, f32[64,256]{1,0:T(8,128)S(1)}, u32[]{:S(2)}) copy-start(f32[64,256]{1,0:T(8,128)S(1)} %collective-permute-done.1.other_ref) | copy-start | bytes 196612
  26.6 4.6 %collective-permute-start.3 = (f32[8,256]{1,0:T(8,128)S(1)}, f32[8,256]{1,0:T(8,128)S(1)}, u32[]{:S(2)}, u32[]{:S(2)}) collective-permute-start(f32[8,256]{1,0:T(8,128)S(1)} %third.1), channel_id=1, source_target_pairs={{0,8},{16,24},{32,40},{48,56},{64,72},{80,88},{96,104},{112,120},{... | collective-permute-start | bytes 24584 | tf_op jit(solution)/shard_map/ppermute | solution.py:368
  31.2 0.6 copy-start.5
  31.8 29.2 %collective-permute-start.4 = (f32[128,256]{1,0:T(8,128)S(1)}, f32[128,256]{1,0:T(8,128)S(1)}, u32[]{:S(2)}, u32[]{:S(2)}) collective-permute-start(f32[128,256]{1,0:T(8,128)S(1)} %get-tuple-element.29), channel_id=1, source_target_pairs={{0,256},{8,264},{16,272},{24,280},{32,288},{40,296},{48,304},{56,3... | collective-permute-start | bytes 393224 | tf_op jit(solution)/shard_map/ppermute | solution.py:368
  61.0 0.7 copy-start.6
  64.8 13.6 %all-to-all-start.1 = ((f32[8,4,256]{2,1,0:T(4,128)}), f32[8,4,256]{2,1,0:T(4,128)S(1)}, u32[]{:S(2)}, u32[]{:S(2)}) async-start(f32[8,4,256]{2,1,0:T(4,128)} %localized.1), calls=%async_computation.1 | async-start | bytes 65536 | tf_op jit(solution)/shard_map/all_to_all | solution.py:448

commit v5 on v4

--- a/solution.py
+++ b/solution.py
@@ -218,7 +218,7 @@
     y = place % 4
     sums = jnp.where((y == 1) | (y == 2), second_ref[61:62] + other[61:62], back_ref[2:3])
     out_ref[126:128] = jnp.zeros((2, out_ref.shape[1]), jnp.float32)
-    sums_ref[...] = jnp.broadcast_to(sums, sums_ref.shape)
+    sums_ref[...] = jnp.broadcast_to(sums[None], sums_ref.shape)
 
 
 def rate_column(diffusivity_ref, member_count):
@@ -424,7 +424,7 @@
     back = exchanged(back, pairs)
     ns_pack, sums = pl.pallas_call(
         relay_kernel,
-        out_shape=[rows_of(NS_ROWS), rows_of(16)],
+        out_shape=[rows_of(NS_ROWS), jax.ShapeDtypeStruct((GROUP, 1, lanes), jnp.float32)],
         in_specs=vmem(6) + [SMEM],
         out_specs=vmem(2),
         name="relay", compiler_params=room(4),
@@ -439,7 +439,7 @@
         out_specs=vmem(1)[0],
         scratch_shapes=[pltpu.VMEM((NS_ROWS + 2 * EW_ROWS, lanes), jnp.float32)],
         name="localized",
-                cost_estimate=pl.CostEstimate(flops=3450000000, bytes_accessed=1000000, transcendentals=0),
+                cost_estimate=pl.CostEstimate(flops=11499999999, bytes_accessed=1000000, transcendentals=0),
     )(
         base, operator, high, low, arrived, near, other, wrap, back,
         spread, edge_flip, place, perts, gain,
@@ -449,7 +449,7 @@
     members_all = member_count * mem_count
     increment = jnp.sum(pieces, axis=0) / jnp.sqrt(jnp.float32(members_all - 1))
     norm_count = level_count * cell_count * tile_count
-    sums = jnp.sum(sums.reshape(16, member_count, level_count), axis=(0, 2))
+    sums = jnp.sum(sums[:, 0].reshape(GROUP, member_count, level_count), axis=(0, 2))
     member_cost = 0.5 * sums / norm_count
     return (increment, member_cost)
 

time: 79.6 us -> 76.4 us (0.960)
  blocking collectives: 16.2 us -> 0 us
  waiting for transfers between devices: 5.52 us -> 15.6 us
  starting transfers between devices: 46.2 us -> 49 us
    all_to_all x1 -> x0, blocking collectives: 16.2 us -> none  [local(): lax.all_to_all(sums, 'tile', 0, 0, tiled=True, axis_index_groups=groups)]
    all_to_all x0 -> x1, waiting for transfers between devices: none -> 10.1 us  [local(): lax.all_to_all(sums, 'tile', 0, 0, tiled=True, axis_index_groups=groups)]
    all_to_all x0 -> x1, starting transfers between devices: none -> 3.49 us  [local(): lax.all_to_all(sums, 'tile', 0, 0, tiled=True, axis_index_groups=groups)]
  transfers between devices with their start and end apart: 6 -> 7, of which waited for: 2 -> 3; matrix products, arithmetic and copies ran while one was open for 1% -> 1% of each run, Pallas kernels for 3% -> 7%
where the time goes in v5:
time: 76.4 us; the launch traced here: 75.7 us
  starting transfers between devices  49 us (64%)
  waiting for transfers between devices  15.6 us (20%)
  Pallas kernels  8.3 us (11%)
  other arithmetic  1.29 us (2%)
  between operations  0.81 us (1%)
    ppermute x5, starting transfers between devices, exchanged(): return lax.ppermute(value, 'tile', both + [(j, i) for i, j in both])  37.6 us
    all_to_all x1, waiting for transfers between devices, local(): lax.all_to_all(sums, 'tile', 0, 0, tiled=True, axis_index_groups=groups)  10.1 us
    all_to_all x1, starting transfers between devices, local(): pieces = lax.all_to_all(pieces, 'mem', 0, 0, tiled=True)  7.9 us
    all_to_all x1, waiting for transfers between devices, local(): pieces = lax.all_to_all(pieces, 'mem', 0, 0, tiled=True)  4.49 us
    all_to_all x1, starting transfers between devices, local(): lax.all_to_all(sums, 'tile', 0, 0, tiled=True, axis_index_groups=groups)  3.49 us
    pallas_call x1, Pallas kernels, local(): pl.pallas_call(final_kernel, out_shape=jax.ShapeDtypeStruct((mem_count, l...  2.88 us
    pallas_call x1, Pallas kernels, local(): pl.pallas_call(own_kernel, out_shape=[jax.ShapeDtypeStruct((lanes, cell_c...  2.68 us
    pallas_call x1, Pallas kernels, local(): pl.pallas_call(pack_kernel, out_shape=[rows_of(count) for count in (EW_RO...  2.1 us
  transfers between devices with their start and end apart: 7, of which 3 were waited for; matrix products, arithmetic and copies ran while one was open for 1% of the time, Pallas kernels for 7%

profile of v5, /device:TPU:1, one launch (start us, length us, event | category | flops | bytes accessed | tf_op | source)
XLA Modules:
  0.0 75.7 jit_solution(7672684555151126551)
XLA Ops:
  0.6 2.1 %packs.1 = (f32[64,256]{1,0:T(8,128)}, f32[64,256]{1,0:T(8,128)}, f32[64,256]{1,0:T(8,128)}, f32[104,256]{1,0:T(8,128)}) custom-call(f32[8,32,256]{2,1,0:T(8,128)} %field_ref.2, s32[1,4]{1,0:T(1,128)} %flip_ref.5, s32[1,1]{1,0:T(1,128)} %bitcast.place_ref, s32[216,8]{1,0:T(8,128)} %constant.39.clone.table_ref), custom_call_target="tpu_custom_call" | custom-call | tf_op jit(solution)/shard_map/packs/pallas_call | solution.py:382
  2.7 4.0 %collective-permute-start = (f32[64,256]{1,0:T(8,128)}, f32[64,256]{1,0:T(8,128)S(1)}, u32[]{:S(2)}, u32[]{:S(2)}) collective-permute-start(f32[64,256]{1,0:T(8,128)} %get-tuple-element.19), channel_id=1, source_target_pairs={{0,8},{16,24},{32,40},{48,56},{64,72},{80,88},{96,104},{112,120},{... | collective-permute-start | bytes 196616 | tf_op jit(solution)/shard_map/ppermute | solution.py:368
  6.8 16.3 %collective-permute-start.2 = (f32[64,256]{1,0:T(8,128)}, f32[64,256]{1,0:T(8,128)S(1)}, u32[]{:S(2)}, u32[]{:S(2)}) collective-permute-start(f32[64,256]{1,0:T(8,128)} %get-tuple-element.23), channel_id=1, source_target_pairs={{120,128},{248,256},{376,384},{504,0},{112,392},{240,8},{368,136},... | collective-permute-start | bytes 196616 | tf_op jit(solution)/shard_map/ppermute | solution.py:368
  23.0 0.0 copy-start.4
  23.1 2.7 %own_cells.1 = (f32[256,256]{1,0:T(8,128)}, bf16[256,768]{1,0:T(8,128)(2,1)}, bf16[256,256]{1,0:T(8,128)(2,1)}, bf16[256,256]{1,0:T(8,128)(2,1)}) custom-call(f32[8,32,256]{2,1,0:T(8,128)} %field_ref.2, f32[1,32]{1,0:T(1,128)} %bitcast.2, f32[32,32]{1,0:T(8,128)} %vertical_ref.1, s32[1,4]{1,0:T(1,128)} %flip_ref.5, ...), custom_call_target="tpu_custom_call" | custom-call | tf_op jit(solution)/shard_map/own_cells/pallas_call | solution.py:395
  25.7 0.0 collective-permute-done.near_ref
  25.7 0.0 copy-start
  25.8 0.0 copy-done.4
  25.8 0.0 copy-start.3
  25.8 0.8 %collective-permute-start.1 = (f32[64,256]{1,0:T(8,128)S(1)}, f32[64,256]{1,0:T(8,128)S(1)}, u32[]{:S(2)}, u32[]{:S(2)}) collective-permute-start(f32[64,256]{1,0:T(8,128)S(1)} %second.1.second_ref), channel_id=1, source_target_pairs={{8,16},{24,32},{40,48},{56,64},{72,80},{88,96},{104,112},{136,144}... | collective-permute-start | bytes 196616 | tf_op jit(solution)/shard_map/ppermute | solution.py:368
  26.6 0.0 collective-permute-done.2.wrap_ref
  26.6 0.0 copy-start.1
  26.6 0.0 collective-permute-done.1.other_ref
  26.6 0.0 copy-start.2
  26.7 3.6 %collective-permute-start.3 = (f32[8,256]{1,0:T(8,128)S(1)}, f32[8,256]{1,0:T(8,128)S(1)}, u32[]{:S(2)}, u32[]{:S(2)}) collective-permute-start(f32[8,256]{1,0:T(8,128)S(1)} %third.1), channel_id=1, source_target_pairs={{0,8},{16,24},{32,40},{48,56},{64,72},{80,88},{96,104},{112,120},{... | collective-permute-start | bytes 24584 | tf_op jit(solution)/shard_map/ppermute | solution.py:368
  30.2 1.0 %collective-permute-done.3.back_ref = f32[8,256]{1,0:T(8,128)S(1)} collective-permute-done((f32[8,256]{1,0:T(8,128)S(1)}, f32[8,256]{1,0:T(8,128)S(1)}, u32[]{:S(2)}, u32[]{:S(2)}) %collective-permute-start.3) | collective-permute-done | bytes 8224 | tf_op jit(solution)/shard_map/ppermute | solution.py:368
  31.2 0.0 copy-start.5
  31.3 0.0 copy-done
  31.3 0.0 copy-done.1
  31.3 0.0 copy-done.2
  31.3 0.0 copy-done.3
  31.3 0.6 relay.1
  31.9 0.0 copy-done.5
  31.9 13.0 %collective-permute-start.4 = (f32[128,256]{1,0:T(8,128)S(1)}, f32[128,256]{1,0:T(8,128)S(1)}, u32[]{:S(2)}, u32[]{:S(2)}) collective-permute-start(f32[128,256]{1,0:T(8,128)S(1)} %get-tuple-element.29), channel_id=1, source_target_pairs={{0,256},{8,264},{16,272},{24,280},{32,288},{40,296},{48,304},{56,3... | collective-permute-start | bytes 393224 | tf_op jit(solution)/shard_map/ppermute | solution.py:368
  44.9 3.5 %all-to-all-start = ((f32[16,1,256]{2,1,0:T(1,128)}), f32[16,1,256]{2,1,0:T(1,128)S(1)}, u32[]{:S(2)}, u32[]{:S(2)}) async-start(f32[16,1,256]{2,1,0:T(1,128)} %get-tuple-element.24), calls=%async_computation | async-start | bytes 32768 | tf_op jit(solution)/shard_map/all_to_all | solution.py:434
  48.4 0.0 collective-permute-done.4.arrived_ref
  48.4 0.0 copy-start.6
  48.4 0.6 copy-done.6
  49.0 2.9 %localized.1 = f32[8,4,256]{2,1,0:T(4,128)} custom-call(f32[256,256]{1,0:T(8,128)} %get-tuple-element.25.base_ref, bf16[256,768]{1,0:T(8,128)(2,1)} %get-tuple-element.26.operator_ref, bf16[256,256]{1,0:T(8,128)(2,1)} %get-tuple-element.27.high_ref, bf16[256,256]{1,0:T(8,128)(2,1)} %get-tuple-element.28.low_ref, f32[128,256]{1,0:T(8,128)} %copy-done.6, ...), custom_call_target="tpu_custom_call" | custom-call | flops 11500000256 | bytes 1000000 | tf_op jit(solution)/shard_map/localized/pallas_call | solution.py:435
  51.9 10.1 %all-to-all-done = f32[16,1,256]{2,1,0:T(1,128)S(1)} async-done(((f32[16,1,256]{2,1,0:T(1,128)}), f32[16,1,256]{2,1,0:T(1,128)S(1)}, u32[]{:S(2)}, u32[]{:S(2)}) %all-to-all-start) | async-done | bytes 16416 | tf_op jit(solution)/shard_map/all_to_all | solution.py:434
  62.0 0.1 reduce_sum.27
  62.1 0.1 reduce_sum.28
  62.2 7.9 %all-to-all-start.1 = ((f32[8,4,256]{2,1,0:T(4,128)}), f32[8,4,256]{2,1,0:T(4,128)S(1)}, u32[]{:S(2)}, u32[]{:S(2)}) async-start(f32[8,4,256]{2,1,0:T(4,128)} %localized.1), calls=%async_computation.1 | async-start | bytes 65536 | tf_op jit(solution)/shard_map/all_to_all | solution.py:448
  70.1 0.5 broadcast_multiply_fusion.1
  70.6 4.5 %all-to-all-done.1 = f32[8,4,256]{2,1,0:T(4,128)S(1)} async-done(((f32[8,4,256]{2,1,0:T(4,128)}), f32[8,4,256]{2,1,0:T(4,128)S(1)}, u32[]{:S(2)}, u32[]{:S(2)}) %all-to-all-start.1) | async-done | bytes 32800 | tf_op jit(solution)/shard_map/all_to_all | solution.py:448
  75.1 0.6 broadcast_multiply_fusion
  (4 shorter events, 0.1 us)
Async XLA Ops:
  2.7 23.0 %collective-permute-start = (f32[64,256]{1,0:T(8,128)}, f32[64,256]{1,0:T(8,128)S(1)}, u32[]{:S(2)}, u32[]{:S(2)}) collective-permute-start(f32[64,256]{1,0:T(8,128)} %get-tuple-element.19), channel_id=1, source_target_pairs={{0,8},{16,24},{32,40},{48,56},{64,72},{80,88},{96,104},{112,120},{... | collective-permute-start | bytes 196616 | tf_op jit(solution)/shard_map/ppermute | solution.py:368
  6.8 19.8 %collective-permute-start.2 = (f32[64,256]{1,0:T(8,128)}, f32[64,256]{1,0:T(8,128)S(1)}, u32[]{:S(2)}, u32[]{:S(2)}) collective-permute-start(f32[64,256]{1,0:T(8,128)} %get-tuple-element.23), channel_id=1, source_target_pairs={{120,128},{248,256},{376,384},{504,0},{112,392},{240,8},{368,136},... | collective-permute-start | bytes 196616 | tf_op jit(solution)/shard_map/ppermute | solution.py:368
  23.0 2.7 %copy-start.4 = (f32[64,256]{1,0:T(8,128)S(1)}, f32[64,256]{1,0:T(8,128)}, u32[]{:S(2)}) copy-start(f32[64,256]{1,0:T(8,128)} %get-tuple-element.18.second_ref) | copy-start | bytes 196612
  25.7 5.5 %copy-start = (f32[64,256]{1,0:T(8,128)}, f32[64,256]{1,0:T(8,128)S(1)}, u32[]{:S(2)}) copy-start(f32[64,256]{1,0:T(8,128)S(1)} %collective-permute-done.near_ref) | copy-start | bytes 196612
  25.8 5.5 %copy-start.3 = (f32[104,256]{1,0:T(8,128)S(1)}, f32[104,256]{1,0:T(8,128)}, u32[]{:S(2)}) copy-start(f32[104,256]{1,0:T(8,128)} %get-tuple-element.17.strips_ref) | copy-start | bytes 319492
  25.8 0.8 %collective-permute-start.1 = (f32[64,256]{1,0:T(8,128)S(1)}, f32[64,256]{1,0:T(8,128)S(1)}, u32[]{:S(2)}, u32[]{:S(2)}) collective-permute-start(f32[64,256]{1,0:T(8,128)S(1)} %second.1.second_ref), channel_id=1, source_target_pairs={{8,16},{24,32},{40,48},{56,64},{72,80},{88,96},{104,112},{136,144}... | collective-permute-start | bytes 196616 | tf_op jit(solution)/shard_map/ppermute | solution.py:368
  26.6 4.7 %copy-start.1 = (f32[64,256]{1,0:T(8,128)}, f32[64,256]{1,0:T(8,128)S(1)}, u32[]{:S(2)}) copy-start(f32[64,256]{1,0:T(8,128)S(1)} %collective-permute-done.2.wrap_ref) | copy-start | bytes 196612
  26.6 4.6 %copy-start.2 = (f32[64,256]{1,0:T(8,128)}, f32[64,256]{1,0:T(8,128)S(1)}, u32[]{:S(2)}) copy-start(f32[64,256]{1,0:T(8,128)S(1)} %collective-permute-done.1.other_ref) | copy-start | bytes 196612
  26.7 4.6 %collective-permute-start.3 = (f32[8,256]{1,0:T(8,128)S(1)}, f32[8,256]{1,0:T(8,128)S(1)}, u32[]{:S(2)}, u32[]{:S(2)}) collective-permute-start(f32[8,256]{1,0:T(8,128)S(1)} %third.1), channel_id=1, source_target_pairs={{0,8},{16,24},{32,40},{48,56},{64,72},{80,88},{96,104},{112,120},{... | collective-permute-start | bytes 24584 | tf_op jit(solution)/shard_map/ppermute | solution.py:368
  31.2 0.6 copy-start.5
  31.9 16.5 %collective-permute-start.4 = (f32[128,256]{1,0:T(8,128)S(1)}, f32[128,256]{1,0:T(8,128)S(1)}, u32[]{:S(2)}, u32[]{:S(2)}) collective-permute-start(f32[128,256]{1,0:T(8,128)S(1)} %get-tuple-element.29), channel_id=1, source_target_pairs={{0,256},{8,264},{16,272},{24,280},{32,288},{40,296},{48,304},{56,3... | collective-permute-start | bytes 393224 | tf_op jit(solution)/shard_map/ppermute | solution.py:368
  44.9 17.1 %all-to-all-start = ((f32[16,1,256]{2,1,0:T(1,128)}), f32[16,1,256]{2,1,0:T(1,128)S(1)}, u32[]{:S(2)}, u32[]{:S(2)}) async-start(f32[16,1,256]{2,1,0:T(1,128)} %get-tuple-element.24), calls=%async_computation | async-start | bytes 32768 | tf_op jit(solution)/shard_map/all_to_all | solution.py:434
  48.4 0.7 copy-start.6
  62.2 12.9 %all-to-all-start.1 = ((f32[8,4,256]{2,1,0:T(4,128)}), f32[8,4,256]{2,1,0:T(4,128)S(1)}, u32[]{:S(2)}, u32[]{:S(2)}) async-start(f32[8,4,256]{2,1,0:T(4,128)} %localized.1), calls=%async_computation.1 | async-start | bytes 65536 | tf_op jit(solution)/shard_map/all_to_all | solution.py:448

commit v6 on v5

--- a/solution.py
+++ b/solution.py
@@ -388,7 +388,23 @@
     )(control, edge_flip, place, jnp.asarray(table))
     wrap = exchanged(wrap, [(k - 1, k) for k in edges] + [(k - 2, k + 1 + half) for k in edges])
     near = exchanged(first, pairs)
-    control_there, first = lax.optimization_barrier((control, first))
+    second = pl.pallas_call(
+        second_kernel, out_shape=rows_of(EW_ROWS), in_specs=vmem(2), out_specs=vmem(1)[0], name="second", compiler_params=room(4)
+    )(second, near)
+    other = exchanged(second, between)
+    back = pl.pallas_call(
+        third_kernel, out_shape=rows_of(8), in_specs=vmem(3) + [SMEM], out_specs=vmem(1)[0], name="third", compiler_params=room(4)
+    )(second, other, wrap, place)
+    back = exchanged(back, pairs)
+    ns_pack, sums = pl.pallas_call(
+        relay_kernel,
+        out_shape=[rows_of(NS_ROWS), jax.ShapeDtypeStruct((GROUP, 1, lanes), jnp.float32)],
+        in_specs=vmem(6) + [SMEM],
+        out_specs=vmem(2),
+        name="relay", compiler_params=room(4),
+    )(strips, second, near, other, wrap, back, place)
+    arrived = exchanged(ns_pack, [(i, i + half) for i in range(half)])
+    control_there, ns_pack = lax.optimization_barrier((control, ns_pack))
     zero, one, edge = halo_rows()
     spread = diffusivity.reshape(1, level_count)
     wide = PASSES * cell_count
@@ -413,23 +429,6 @@
         jnp.asarray(one, jnp.bfloat16),
         jnp.asarray(edge),
     )
-    near, base = lax.optimization_barrier((near, base))
-    second = pl.pallas_call(
-        second_kernel, out_shape=rows_of(EW_ROWS), in_specs=vmem(2), out_specs=vmem(1)[0], name="second", compiler_params=room(4)
-    )(second, near)
-    other = exchanged(second, between)
-    back = pl.pallas_call(
-        third_kernel, out_shape=rows_of(8), in_specs=vmem(3) + [SMEM], out_specs=vmem(1)[0], name="third", compiler_params=room(4)
-    )(second, other, wrap, place)
-    back = exchanged(back, pairs)
-    ns_pack, sums = pl.pallas_call(
-        relay_kernel,
-        out_shape=[rows_of(NS_ROWS), jax.ShapeDtypeStruct((GROUP, 1, lanes), jnp.float32)],
-        in_specs=vmem(6) + [SMEM],
-        out_specs=vmem(2),
-        name="relay", compiler_params=room(4),
-    )(strips, second, near, other, wrap, back, place)
-    arrived = exchanged(ns_pack, [(i, i + half) for i in range(half)])
     groups = [list(range(low_bits, tile_count, 4)) for low_bits in range(4)]
     sums = lax.all_to_all(sums, "tile", 0, 0, tiled=True, axis_index_groups=groups)
     pieces = pl.pallas_call(

time: 76.4 us -> 76.4 us (level)
  waiting for transfers between devices: 15.6 us -> 13.8 us
  starting transfers between devices: 49 us -> 50 us
  local copies, waits for them, and re-layouts: 0.75 us -> 1.6 us
    all_to_all x1, waiting for transfers between devices: 10.1 us -> 7.42 us  [local(): lax.all_to_all(sums, 'tile', 0, 0, tiled=True, axis_index_groups=groups)]
    ppermute x5, starting transfers between devices: 37.6 us -> 38.6 us  [exchanged(): return lax.ppermute(value, 'tile', both + [(j, i) for i, j in both])]
    ppermute x5, waiting for transfers between devices: 1.04 us -> 1.92 us  [exchanged(): return lax.ppermute(value, 'tile', both + [(j, i) for i, j in both])]
    unnamed x14, local copies, waits for them, and re-layouts: 0.67 us -> 1.52 us
  transfers between devices with their start and end apart: 7 -> 7, of which waited for: 3 -> 4; matrix products, arithmetic and copies ran while one was open for 1% -> 1% of each run, Pallas kernels for 7% -> 7%
where the time goes in v6:
time: 76.4 us; the launch traced here: 75.7 us
  starting transfers between devices  50 us (65%)
  waiting for transfers between devices  13.8 us (18%)
  Pallas kernels  8.25 us (11%)
  local copies, waits for them, and re-layouts  1.6 us (2%)
  other arithmetic  1.29 us (2%)
    ppermute x5, starting transfers between devices, exchanged(): return lax.ppermute(value, 'tile', both + [(j, i) for i, j in both])  38.6 us
    all_to_all x1, starting transfers between devices, local(): pieces = lax.all_to_all(pieces, 'mem', 0, 0, tiled=True)  7.9 us
    all_to_all x1, waiting for transfers between devices, local(): lax.all_to_all(sums, 'tile', 0, 0, tiled=True, axis_index_groups=groups)  7.42 us
    all_to_all x1, waiting for transfers between devices, local(): pieces = lax.all_to_all(pieces, 'mem', 0, 0, tiled=True)  4.49 us
    all_to_all x1, starting transfers between devices, local(): lax.all_to_all(sums, 'tile', 0, 0, tiled=True, axis_index_groups=groups)  3.49 us
    pallas_call x1, Pallas kernels, local(): pl.pallas_call(final_kernel, out_shape=jax.ShapeDtypeStruct((mem_count, l...  2.88 us
    pallas_call x1, Pallas kernels, local(): pl.pallas_call(own_kernel, out_shape=[jax.ShapeDtypeStruct((lanes, cell_c...  2.65 us
    pallas_call x1, Pallas kernels, local(): pl.pallas_call(pack_kernel, out_shape=[rows_of(count) for count in (EW_RO...  2.08 us
  transfers between devices with their start and end apart: 7, of which 4 were waited for; matrix products, arithmetic and copies ran while one was open for 1% of the time, Pallas kernels for 7%

profile of v6, /device:TPU:1, one launch (start us, length us, event | category | flops | bytes accessed | tf_op | source)
XLA Modules:
  0.0 75.7 jit_solution(13059337983318031594)
XLA Ops:
  0.6 2.1 %packs.1 = (f32[64,256]{1,0:T(8,128)}, f32[64,256]{1,0:T(8,128)}, f32[64,256]{1,0:T(8,128)}, f32[104,256]{1,0:T(8,128)}) custom-call(f32[8,32,256]{2,1,0:T(8,128)} %field_ref.2, s32[1,4]{1,0:T(1,128)} %flip_ref.5, s32[1,1]{1,0:T(1,128)} %bitcast.place_ref, s32[216,8]{1,0:T(8,128)} %constant.39.clone.table_ref), custom_call_target="tpu_custom_call" | custom-call | tf_op jit(solution)/shard_map/packs/pallas_call | solution.py:382
  2.7 4.0 %collective-permute-start = (f32[64,256]{1,0:T(8,128)}, f32[64,256]{1,0:T(8,128)S(1)}, u32[]{:S(2)}, u32[]{:S(2)}) collective-permute-start(f32[64,256]{1,0:T(8,128)} %get-tuple-element.17), channel_id=1, source_target_pairs={{0,8},{16,24},{32,40},{48,56},{64,72},{80,88},{96,104},{112,120},{... | collective-permute-start | bytes 196616 | tf_op jit(solution)/shard_map/ppermute | solution.py:368
  6.8 16.3 %collective-permute-start.2 = (f32[64,256]{1,0:T(8,128)}, f32[64,256]{1,0:T(8,128)S(1)}, u32[]{:S(2)}, u32[]{:S(2)}) collective-permute-start(f32[64,256]{1,0:T(8,128)} %get-tuple-element.18), channel_id=1, source_target_pairs={{120,128},{248,256},{376,384},{504,0},{112,392},{240,8},{368,136},... | collective-permute-start | bytes 196616 | tf_op jit(solution)/shard_map/ppermute | solution.py:368
  23.0 0.0 collective-permute-done.near_ref
  23.0 0.0 copy-start
  23.0 0.0 copy-start.4
  23.1 0.9 %copy-done.4 = f32[64,256]{1,0:T(8,128)S(1)} copy-done((f32[64,256]{1,0:T(8,128)S(1)}, f32[64,256]{1,0:T(8,128)}, u32[]{:S(2)}) %copy-start.4) | copy-done | bytes 65560
  23.9 0.0 copy-start.3
  23.9 0.8 %collective-permute-start.1 = (f32[64,256]{1,0:T(8,128)S(1)}, f32[64,256]{1,0:T(8,128)S(1)}, u32[]{:S(2)}, u32[]{:S(2)}) collective-permute-start(f32[64,256]{1,0:T(8,128)S(1)} %second.1.second_ref), channel_id=1, source_target_pairs={{8,16},{24,32},{40,48},{56,64},{72,80},{88,96},{104,112},{136,144}... | collective-permute-start | bytes 196616 | tf_op jit(solution)/shard_map/ppermute | solution.py:368
  24.7 0.4 collective-permute-done.2.wrap_ref
  25.2 0.0 copy-start.1
  25.2 0.0 collective-permute-done.1.other_ref
  25.2 0.0 copy-start.2
  25.2 2.9 %collective-permute-start.3 = (f32[8,256]{1,0:T(8,128)S(1)}, f32[8,256]{1,0:T(8,128)S(1)}, u32[]{:S(2)}, u32[]{:S(2)}) collective-permute-start(f32[8,256]{1,0:T(8,128)S(1)} %third.1), channel_id=1, source_target_pairs={{0,8},{16,24},{32,40},{48,56},{64,72},{80,88},{96,104},{112,120},{... | collective-permute-start | bytes 24584 | tf_op jit(solution)/shard_map/ppermute | solution.py:368
  28.1 1.5 %collective-permute-done.3.back_ref = f32[8,256]{1,0:T(8,128)S(1)} collective-permute-done((f32[8,256]{1,0:T(8,128)S(1)}, f32[8,256]{1,0:T(8,128)S(1)}, u32[]{:S(2)}, u32[]{:S(2)}) %collective-permute-start.3) | collective-permute-done | bytes 8224 | tf_op jit(solution)/shard_map/ppermute | solution.py:368
  29.6 0.0 copy-start.5
  29.6 0.0 copy-done
  29.6 0.0 copy-done.1
  29.6 0.0 copy-done.2
  29.6 0.0 copy-done.3
  29.6 0.6 relay.1
  30.2 0.0 copy-done.5
  30.2 14.6 %collective-permute-start.4 = (f32[128,256]{1,0:T(8,128)S(1)}, f32[128,256]{1,0:T(8,128)S(1)}, u32[]{:S(2)}, u32[]{:S(2)}) collective-permute-start(f32[128,256]{1,0:T(8,128)S(1)} %get-tuple-element.20), channel_id=1, source_target_pairs={{0,256},{8,264},{16,272},{24,280},{32,288},{40,296},{48,304},{56,3... | collective-permute-start | bytes 393224 | tf_op jit(solution)/shard_map/ppermute | solution.py:368
  44.9 3.5 %all-to-all-start = ((f32[16,1,256]{2,1,0:T(1,128)}), f32[16,1,256]{2,1,0:T(1,128)S(1)}, u32[]{:S(2)}, u32[]{:S(2)}) async-start(f32[16,1,256]{2,1,0:T(1,128)} %get-tuple-element.19), calls=%async_computation | async-start | bytes 32768 | tf_op jit(solution)/shard_map/all_to_all | solution.py:433
  48.4 2.6 %own_cells.1 = (f32[256,256]{1,0:T(8,128)}, bf16[256,768]{1,0:T(8,128)(2,1)}, bf16[256,256]{1,0:T(8,128)(2,1)}, bf16[256,256]{1,0:T(8,128)(2,1)}) custom-call(f32[8,32,256]{2,1,0:T(8,128)} %field_ref.2, f32[1,32]{1,0:T(1,128)} %bitcast.2, f32[32,32]{1,0:T(8,128)} %vertical_ref.1, s32[1,4]{1,0:T(1,128)} %flip_ref.5, ...), custom_call_target="tpu_custom_call" | custom-call | tf_op jit(solution)/shard_map/own_cells/pallas_call | solution.py:411
  51.0 0.0 collective-permute-done.4.arrived_ref
  51.0 0.0 copy-start.6
  51.0 0.6 copy-done.6
  51.7 2.9 %localized.1 = f32[8,4,256]{2,1,0:T(4,128)} custom-call(f32[256,256]{1,0:T(8,128)} %get-tuple-element.22.base_ref, bf16[256,768]{1,0:T(8,128)(2,1)} %get-tuple-element.23.operator_ref, bf16[256,256]{1,0:T(8,128)(2,1)} %get-tuple-element.24.high_ref, bf16[256,256]{1,0:T(8,128)(2,1)} %get-tuple-element.25.low_ref, f32[128,256]{1,0:T(8,128)} %copy-done.6, ...), custom_call_target="tpu_custom_call" | custom-call | flops 11500000256 | bytes 1000000 | tf_op jit(solution)/shard_map/localized/pallas_call | solution.py:434
  54.5 7.4 %all-to-all-done = f32[16,1,256]{2,1,0:T(1,128)S(1)} async-done(((f32[16,1,256]{2,1,0:T(1,128)}), f32[16,1,256]{2,1,0:T(1,128)S(1)}, u32[]{:S(2)}, u32[]{:S(2)}) %all-to-all-start) | async-done | bytes 16416 | tf_op jit(solution)/shard_map/all_to_all | solution.py:433
  62.0 0.1 reduce_sum.27
  62.1 0.1 reduce_sum.28
  62.2 7.9 %all-to-all-start.1 = ((f32[8,4,256]{2,1,0:T(4,128)}), f32[8,4,256]{2,1,0:T(4,128)S(1)}, u32[]{:S(2)}, u32[]{:S(2)}) async-start(f32[8,4,256]{2,1,0:T(4,128)} %localized.1), calls=%async_computation.1 | async-start | bytes 65536 | tf_op jit(solution)/shard_map/all_to_all | solution.py:447
  70.1 0.5 broadcast_multiply_fusion.1
  70.6 4.5 %all-to-all-done.1 = f32[8,4,256]{2,1,0:T(4,128)S(1)} async-done(((f32[8,4,256]{2,1,0:T(4,128)}), f32[8,4,256]{2,1,0:T(4,128)S(1)}, u32[]{:S(2)}, u32[]{:S(2)}) %all-to-all-start.1) | async-done | bytes 32800 | tf_op jit(solution)/shard_map/all_to_all | solution.py:447
  75.1 0.6 broadcast_multiply_fusion
  (4 shorter events, 0.1 us)
Async XLA Ops:
  2.7 20.3 %collective-permute-start = (f32[64,256]{1,0:T(8,128)}, f32[64,256]{1,0:T(8,128)S(1)}, u32[]{:S(2)}, u32[]{:S(2)}) collective-permute-start(f32[64,256]{1,0:T(8,128)} %get-tuple-element.17), channel_id=1, source_target_pairs={{0,8},{16,24},{32,40},{48,56},{64,72},{80,88},{96,104},{112,120},{... | collective-permute-start | bytes 196616 | tf_op jit(solution)/shard_map/ppermute | solution.py:368
  6.8 18.4 %collective-permute-start.2 = (f32[64,256]{1,0:T(8,128)}, f32[64,256]{1,0:T(8,128)S(1)}, u32[]{:S(2)}, u32[]{:S(2)}) collective-permute-start(f32[64,256]{1,0:T(8,128)} %get-tuple-element.18), channel_id=1, source_target_pairs={{120,128},{248,256},{376,384},{504,0},{112,392},{240,8},{368,136},... | collective-permute-start | bytes 196616 | tf_op jit(solution)/shard_map/ppermute | solution.py:368
  23.0 6.6 %copy-start = (f32[64,256]{1,0:T(8,128)}, f32[64,256]{1,0:T(8,128)S(1)}, u32[]{:S(2)}) copy-start(f32[64,256]{1,0:T(8,128)S(1)} %collective-permute-done.near_ref) | copy-start | bytes 196612
  23.0 0.9 %copy-start.4 = (f32[64,256]{1,0:T(8,128)S(1)}, f32[64,256]{1,0:T(8,128)}, u32[]{:S(2)}) copy-start(f32[64,256]{1,0:T(8,128)} %get-tuple-element.16.second_ref) | copy-start | bytes 196612
  23.9 5.7 %copy-start.3 = (f32[104,256]{1,0:T(8,128)S(1)}, f32[104,256]{1,0:T(8,128)}, u32[]{:S(2)}) copy-start(f32[104,256]{1,0:T(8,128)} %get-tuple-element.15.strips_ref) | copy-start | bytes 319492
  23.9 1.2 %collective-permute-start.1 = (f32[64,256]{1,0:T(8,128)S(1)}, f32[64,256]{1,0:T(8,128)S(1)}, u32[]{:S(2)}, u32[]{:S(2)}) collective-permute-start(f32[64,256]{1,0:T(8,128)S(1)} %second.1.second_ref), channel_id=1, source_target_pairs={{8,16},{24,32},{40,48},{56,64},{72,80},{88,96},{104,112},{136,144}... | collective-permute-start | bytes 196616 | tf_op jit(solution)/shard_map/ppermute | solution.py:368
  25.2 4.4 %copy-start.1 = (f32[64,256]{1,0:T(8,128)}, f32[64,256]{1,0:T(8,128)S(1)}, u32[]{:S(2)}) copy-start(f32[64,256]{1,0:T(8,128)S(1)} %collective-permute-done.2.wrap_ref) | copy-start | bytes 196612
  25.2 4.4 %copy-start.2 = (f32[64,256]{1,0:T(8,128)}, f32[64,256]{1,0:T(8,128)S(1)}, u32[]{:S(2)}) copy-start(f32[64,256]{1,0:T(8,128)S(1)} %collective-permute-done.1.other_ref) | copy-start | bytes 196612
  25.2 4.4 %collective-permute-start.3 = (f32[8,256]{1,0:T(8,128)S(1)}, f32[8,256]{1,0:T(8,128)S(1)}, u32[]{:S(2)}, u32[]{:S(2)}) collective-permute-start(f32[8,256]{1,0:T(8,128)S(1)} %third.1), channel_id=1, source_target_pairs={{0,8},{16,24},{32,40},{48,56},{64,72},{80,88},{96,104},{112,120},{... | collective-permute-start | bytes 24584 | tf_op jit(solution)/shard_map/ppermute | solution.py:368
  29.6 0.6 copy-start.5
  30.2 20.8 %collective-permute-start.4 = (f32[128,256]{1,0:T(8,128)S(1)}, f32[128,256]{1,0:T(8,128)S(1)}, u32[]{:S(2)}, u32[]{:S(2)}) collective-permute-start(f32[128,256]{1,0:T(8,128)S(1)} %get-tuple-element.20), channel_id=1, source_target_pairs={{0,256},{8,264},{16,272},{24,280},{32,288},{40,296},{48,304},{56,3... | collective-permute-start | bytes 393224 | tf_op jit(solution)/shard_map/ppermute | solution.py:368
  44.9 17.1 %all-to-all-start = ((f32[16,1,256]{2,1,0:T(1,128)}), f32[16,1,256]{2,1,0:T(1,128)S(1)}, u32[]{:S(2)}, u32[]{:S(2)}) async-start(f32[16,1,256]{2,1,0:T(1,128)} %get-tuple-element.19), calls=%async_computation | async-start | bytes 32768 | tf_op jit(solution)/shard_map/all_to_all | solution.py:433
  51.0 0.7 copy-start.6
  62.2 12.9 %all-to-all-start.1 = ((f32[8,4,256]{2,1,0:T(4,128)}), f32[8,4,256]{2,1,0:T(4,128)S(1)}, u32[]{:S(2)}, u32[]{:S(2)}) async-start(f32[8,4,256]{2,1,0:T(4,128)} %localized.1), calls=%async_computation.1 | async-start | bytes 65536 | tf_op jit(solution)/shard_map/all_to_all | solution.py:447

commit v7 on v6

--- a/solution.py
+++ b/solution.py
@@ -229,6 +229,11 @@
     return jnp.concatenate([column] * member_count, axis=0)
 
 
+def rates_kernel(diffusivity_ref, first_ref, out_ref):
+    member_count = out_ref.shape[0] // diffusivity_ref.shape[1]
+    out_ref[...] = jnp.broadcast_to(rate_column(diffusivity_ref, member_count), out_ref.shape)
+
+
 def weighted(walks, rates):
     one, two, three = (walks[:, k * CELLS : (k + 1) * CELLS] for k in range(PASSES))
     return rates * (3.0 * one + rates * (3.0 * two + rates * three))
@@ -261,11 +266,11 @@
 
 def final_kernel(
     base_ref, operator_ref, high_ref, low_ref, arrived_ref, near_ref, other_ref, wrap_ref, back_ref,
-    diffusivity_ref, flip_ref, place_ref, perts_ref, gain_ref, term_ref,
+    rates_ref, flip_ref, place_ref, perts_ref, gain_ref, term_ref,
     halo_ref,
 ):
     member_count, level_count, _ = perts_ref.shape
-    rates = rate_column(diffusivity_ref, member_count)
+    rates = rates_ref[:, 0:1]
     place = place_ref[0, 0]
     even = place % 2 == 0
     near = near_ref[...]
@@ -388,6 +393,16 @@
     )(control, edge_flip, place, jnp.asarray(table))
     wrap = exchanged(wrap, [(k - 1, k) for k in edges] + [(k - 2, k + 1 + half) for k in edges])
     near = exchanged(first, pairs)
+    rates = pl.pallas_call(
+        rates_kernel,
+        out_shape=jax.ShapeDtypeStruct((lanes, 128), jnp.float32),
+        in_specs=vmem(2),
+        out_specs=vmem(1)[0],
+        name="rates",
+        compiler_params=room(4),
+        cost_estimate=pl.CostEstimate(flops=4600000000, bytes_accessed=1000000, transcendentals=0),
+    )(diffusivity.reshape(1, level_count), first)
+    near, rates = lax.optimization_barrier((near, rates))
     second = pl.pallas_call(
         second_kernel, out_shape=rows_of(EW_ROWS), in_specs=vmem(2), out_specs=vmem(1)[0], name="second", compiler_params=room(4)
     )(second, near)
@@ -441,7 +456,7 @@
                 cost_estimate=pl.CostEstimate(flops=11499999999, bytes_accessed=1000000, transcendentals=0),
     )(
         base, operator, high, low, arrived, near, other, wrap, back,
-        spread, edge_flip, place, perts, gain,
+        rates, edge_flip, place, perts, gain,
     )
     sums, pieces = lax.optimization_barrier((sums, pieces))
     pieces = lax.all_to_all(pieces, "mem", 0, 0, tiled=True)

time: 76.4 us -> 76.9 us (level)
  waiting for transfers between devices: 13.8 us -> 15.2 us
  starting transfers between devices: 50 us -> 49.1 us
    ppermute x5, starting transfers between devices: 38.6 us -> 34 us  [exchanged(): return lax.ppermute(value, 'tile', both + [(j, i) for i, j in both])]
    all_to_all x1, starting transfers between devices: 3.49 us -> 6.35 us  [local(): lax.all_to_all(sums, 'tile', 0, 0, tiled=True, axis_index_groups=groups)]
    ppermute x5, waiting for transfers between devices: 1.92 us -> 3.3 us  [exchanged(): return lax.ppermute(value, 'tile', both + [(j, i) for i, j in both])]
    all_to_all x1, starting transfers between devices: 7.9 us -> 8.78 us  [local(): pieces = lax.all_to_all(pieces, 'mem', 0, 0, tiled=True)]
where the time goes in v7:
time: 76.9 us; the launch traced here: 76.5 us
  starting transfers between devices  49.1 us (64%)
  waiting for transfers between devices  15.2 us (20%)
  Pallas kernels  8.44 us (11%)
  local copies, waits for them, and re-layouts  1.6 us (2%)
  other arithmetic  1.29 us (2%)
  between operations  0.81 us (1%)
    ppermute x5, starting transfers between devices, exchanged(): return lax.ppermute(value, 'tile', both + [(j, i) for i, j in both])  34 us
    all_to_all x1, starting transfers between devices, local(): pieces = lax.all_to_all(pieces, 'mem', 0, 0, tiled=True)  8.78 us
    all_to_all x1, waiting for transfers between devices, local(): lax.all_to_all(sums, 'tile', 0, 0, tiled=True, axis_index_groups=groups)  7.45 us
    all_to_all x1, starting transfers between devices, local(): lax.all_to_all(sums, 'tile', 0, 0, tiled=True, axis_index_groups=groups)  6.35 us
    all_to_all x1, waiting for transfers between devices, local(): pieces = lax.all_to_all(pieces, 'mem', 0, 0, tiled=True)  4.49 us
    ppermute x5, waiting for transfers between devices, exchanged(): return lax.ppermute(value, 'tile', both + [(j, i) for i, j in both])  3.3 us
    pallas_call x1, Pallas kernels, local(): pl.pallas_call(final_kernel, out_shape=jax.ShapeDtypeStruct((mem_count, l...  2.89 us
    pallas_call x1, Pallas kernels, local(): pl.pallas_call(own_kernel, out_shape=[jax.ShapeDtypeStruct((lanes, cell_c...  2.67 us
  transfers between devices with their start and end apart: 7, of which 4 were waited for; matrix products, arithmetic and copies ran while one was open for 1% of the time, Pallas kernels for 7%

profile of v7, /device:TPU:1, one launch (start us, length us, event | category | flops | bytes accessed | tf_op | source)
XLA Modules:
  0.0 76.5 jit_solution(176991450715546393)
XLA Ops:
  0.6 2.1 %packs.1 = (f32[64,256]{1,0:T(8,128)}, f32[64,256]{1,0:T(8,128)}, f32[64,256]{1,0:T(8,128)}, f32[104,256]{1,0:T(8,128)}) custom-call(f32[8,32,256]{2,1,0:T(8,128)} %field_ref.2, s32[1,4]{1,0:T(1,128)} %flip_ref.5, s32[1,1]{1,0:T(1,128)} %bitcast.place_ref, s32[216,8]{1,0:T(8,128)} %constant.39.clone.table_ref), custom_call_target="tpu_custom_call" | custom-call | tf_op jit(solution)/shard_map/packs/pallas_call | solution.py:387
  2.7 17.9 %collective-permute-start.2 = (f32[64,256]{1,0:T(8,128)}, f32[64,256]{1,0:T(8,128)S(1)}, u32[]{:S(2)}, u32[]{:S(2)}) collective-permute-start(f32[64,256]{1,0:T(8,128)} %get-tuple-element.21), channel_id=1, source_target_pairs={{120,128},{248,256},{376,384},{504,0},{112,392},{240,8},{368,136},... | collective-permute-start | bytes 196616 | tf_op jit(solution)/shard_map/ppermute | solution.py:373
  20.7 0.0 copy-start.6
  20.7 1.9 %collective-permute-start = (f32[64,256]{1,0:T(8,128)}, f32[64,256]{1,0:T(8,128)S(1)}, u32[]{:S(2)}, u32[]{:S(2)}) collective-permute-start(f32[64,256]{1,0:T(8,128)} %get-tuple-element.19.first_ref), channel_id=1, source_target_pairs={{0,8},{16,24},{32,40},{48,56},{64,72},{80,88},{96,104},{112,120},{... | collective-permute-start | bytes 196616 | tf_op jit(solution)/shard_map/ppermute | solution.py:373
  22.6 0.0 copy-done.6
  22.6 0.0 copy-start.7
  22.6 0.8 %copy-done.7 = f32[64,256]{1,0:T(8,128)S(1)} copy-done((f32[64,256]{1,0:T(8,128)S(1)}, f32[64,256]{1,0:T(8,128)}, u32[]{:S(2)}) %copy-start.7) | copy-done | bytes 65560
  23.4 0.0 copy-start.4
  23.4 0.1 rates.1.rates_ref
  23.6 0.0 copy-start.8
  23.6 2.3 %collective-permute-done.near_ref = f32[64,256]{1,0:T(8,128)S(1)} collective-permute-done((f32[64,256]{1,0:T(8,128)}, f32[64,256]{1,0:T(8,128)S(1)}, u32[]{:S(2)}, u32[]{:S(2)}) %collective-permute-start) | collective-permute-done | bytes 65568 | tf_op jit(solution)/shard_map/ppermute | solution.py:373
  25.9 0.0 copy-start.1
  25.9 0.0 copy-done.4
  25.9 0.0 copy-start.3
  25.9 0.8 %collective-permute-start.1 = (f32[64,256]{1,0:T(8,128)S(1)}, f32[64,256]{1,0:T(8,128)S(1)}, u32[]{:S(2)}, u32[]{:S(2)}) collective-permute-start(f32[64,256]{1,0:T(8,128)S(1)} %second.1.second_ref), channel_id=1, source_target_pairs={{8,16},{24,32},{40,48},{56,64},{72,80},{88,96},{104,112},{136,144}... | collective-permute-start | bytes 196616 | tf_op jit(solution)/shard_map/ppermute | solution.py:373
  26.7 0.0 collective-permute-done.2.wrap_ref
  26.7 0.0 copy-start
  26.7 0.0 collective-permute-done.1.other_ref
  26.7 0.0 copy-start.2
  26.8 0.0 copy-done.8
  26.8 6.2 %collective-permute-start.3 = (f32[8,256]{1,0:T(8,128)S(1)}, f32[8,256]{1,0:T(8,128)S(1)}, u32[]{:S(2)}, u32[]{:S(2)}) collective-permute-start(f32[8,256]{1,0:T(8,128)S(1)} %third.1), channel_id=1, source_target_pairs={{0,8},{16,24},{32,40},{48,56},{64,72},{80,88},{96,104},{112,120},{... | collective-permute-start | bytes 24584 | tf_op jit(solution)/shard_map/ppermute | solution.py:373
  33.0 1.0 %collective-permute-done.3.back_ref = f32[8,256]{1,0:T(8,128)S(1)} collective-permute-done((f32[8,256]{1,0:T(8,128)S(1)}, f32[8,256]{1,0:T(8,128)S(1)}, u32[]{:S(2)}, u32[]{:S(2)}) %collective-permute-start.3) | collective-permute-done | bytes 8224 | tf_op jit(solution)/shard_map/ppermute | solution.py:373
  34.0 0.0 copy-start.5
  34.0 0.0 copy-done.1
  34.0 0.0 copy-done
  34.0 0.0 copy-done.2
  34.0 0.0 copy-done.3
  34.1 0.6 relay.1
  34.7 0.0 copy-done.5
  34.7 7.1 %collective-permute-start.4 = (f32[128,256]{1,0:T(8,128)S(1)}, f32[128,256]{1,0:T(8,128)S(1)}, u32[]{:S(2)}, u32[]{:S(2)}) collective-permute-start(f32[128,256]{1,0:T(8,128)S(1)} %get-tuple-element.23), channel_id=1, source_target_pairs={{0,256},{8,264},{16,272},{24,280},{32,288},{40,296},{48,304},{56,3... | collective-permute-start | bytes 393224 | tf_op jit(solution)/shard_map/ppermute | solution.py:373
  41.8 6.3 %all-to-all-start = ((f32[16,1,256]{2,1,0:T(1,128)}), f32[16,1,256]{2,1,0:T(1,128)S(1)}, u32[]{:S(2)}, u32[]{:S(2)}) async-start(f32[16,1,256]{2,1,0:T(1,128)} %get-tuple-element.22), calls=%async_computation | async-start | bytes 32768 | tf_op jit(solution)/shard_map/all_to_all | solution.py:448
  48.2 2.7 %own_cells.1 = (f32[256,256]{1,0:T(8,128)}, bf16[256,768]{1,0:T(8,128)(2,1)}, bf16[256,256]{1,0:T(8,128)(2,1)}, bf16[256,256]{1,0:T(8,128)(2,1)}) custom-call(f32[8,32,256]{2,1,0:T(8,128)} %field_ref.2, f32[1,32]{1,0:T(1,128)} %bitcast.2, f32[32,32]{1,0:T(8,128)} %vertical_ref.1, s32[1,4]{1,0:T(1,128)} %flip_ref.5, ...), custom_call_target="tpu_custom_call" | custom-call | tf_op jit(solution)/shard_map/own_cells/pallas_call | solution.py:426
  50.8 0.0 collective-permute-done.4.arrived_ref
  50.8 0.0 copy-start.9
  50.9 0.6 copy-done.9
  51.5 2.9 %localized.1 = f32[8,4,256]{2,1,0:T(4,128)} custom-call(f32[256,256]{1,0:T(8,128)} %get-tuple-element.25.base_ref, bf16[256,768]{1,0:T(8,128)(2,1)} %get-tuple-element.26.operator_ref, bf16[256,256]{1,0:T(8,128)(2,1)} %get-tuple-element.27.high_ref, bf16[256,256]{1,0:T(8,128)(2,1)} %get-tuple-element.28.low_ref, f32[128,256]{1,0:T(8,128)} %copy-done.9, ...), custom_call_target="tpu_custom_call" | custom-call | flops 11500000256 | bytes 1000000 | tf_op jit(solution)/shard_map/localized/pallas_call | solution.py:449
  54.4 7.4 %all-to-all-done = f32[16,1,256]{2,1,0:T(1,128)S(1)} async-done(((f32[16,1,256]{2,1,0:T(1,128)}), f32[16,1,256]{2,1,0:T(1,128)S(1)}, u32[]{:S(2)}, u32[]{:S(2)}) %all-to-all-start) | async-done | bytes 16416 | tf_op jit(solution)/shard_map/all_to_all | solution.py:448
  61.9 0.1 reduce_sum.27
  61.9 0.1 reduce_sum.28
  62.1 8.8 %all-to-all-start.1 = ((f32[8,4,256]{2,1,0:T(4,128)}), f32[8,4,256]{2,1,0:T(4,128)S(1)}, u32[]{:S(2)}, u32[]{:S(2)}) async-start(f32[8,4,256]{2,1,0:T(4,128)} %localized.1), calls=%async_computation.1 | async-start | bytes 65536 | tf_op jit(solution)/shard_map/all_to_all | solution.py:462
  70.8 0.5 broadcast_multiply_fusion.1
  71.4 4.5 %all-to-all-done.1 = f32[8,4,256]{2,1,0:T(4,128)S(1)} async-done(((f32[8,4,256]{2,1,0:T(4,128)}), f32[8,4,256]{2,1,0:T(4,128)S(1)}, u32[]{:S(2)}, u32[]{:S(2)}) %all-to-all-start.1) | async-done | bytes 32800 | tf_op jit(solution)/shard_map/all_to_all | solution.py:462
  75.9 0.6 broadcast_multiply_fusion
  (4 shorter events, 0.1 us)
Async XLA Ops:
  2.7 24.0 %collective-permute-start.2 = (f32[64,256]{1,0:T(8,128)}, f32[64,256]{1,0:T(8,128)S(1)}, u32[]{:S(2)}, u32[]{:S(2)}) collective-permute-start(f32[64,256]{1,0:T(8,128)} %get-tuple-element.21), channel_id=1, source_target_pairs={{120,128},{248,256},{376,384},{504,0},{112,392},{240,8},{368,136},... | collective-permute-start | bytes 196616 | tf_op jit(solution)/shard_map/ppermute | solution.py:373
  20.7 1.9 %copy-start.6 = (f32[32]{0:T(128)S(1)}, f32[32]{0:T(128)}, u32[]{:S(2)}) copy-start(f32[32]{0:T(128)} %param.13) | copy-start | bytes 388
  20.7 5.2 %collective-permute-start = (f32[64,256]{1,0:T(8,128)}, f32[64,256]{1,0:T(8,128)S(1)}, u32[]{:S(2)}, u32[]{:S(2)}) collective-permute-start(f32[64,256]{1,0:T(8,128)} %get-tuple-element.19.first_ref), channel_id=1, source_target_pairs={{0,8},{16,24},{32,40},{48,56},{64,72},{80,88},{96,104},{112,120},{... | collective-permute-start | bytes 196616 | tf_op jit(solution)/shard_map/ppermute | solution.py:373
  22.6 0.8 %copy-start.7 = (f32[64,256]{1,0:T(8,128)S(1)}, f32[64,256]{1,0:T(8,128)}, u32[]{:S(2)}) copy-start(f32[64,256]{1,0:T(8,128)} %get-tuple-element.19.first_ref) | copy-start | bytes 196612
  23.4 2.4 %copy-start.4 = (f32[64,256]{1,0:T(8,128)S(1)}, f32[64,256]{1,0:T(8,128)}, u32[]{:S(2)}) copy-start(f32[64,256]{1,0:T(8,128)} %get-tuple-element.18.second_ref) | copy-start | bytes 196612
  23.6 3.2 %copy-start.8 = (f32[256,128]{1,0:T(8,128)}, f32[256,128]{1,0:T(8,128)S(1)}, u32[]{:S(2)}) copy-start(f32[256,128]{1,0:T(8,128)S(1)} %rates.1.rates_ref) | copy-start | bytes 393220
  25.9 8.2 %copy-start.1 = (f32[64,256]{1,0:T(8,128)}, f32[64,256]{1,0:T(8,128)S(1)}, u32[]{:S(2)}) copy-start(f32[64,256]{1,0:T(8,128)S(1)} %collective-permute-done.near_ref) | copy-start | bytes 196612
  25.9 8.1 %copy-start.3 = (f32[104,256]{1,0:T(8,128)S(1)}, f32[104,256]{1,0:T(8,128)}, u32[]{:S(2)}) copy-start(f32[104,256]{1,0:T(8,128)} %get-tuple-element.17.strips_ref) | copy-start | bytes 319492
  25.9 0.8 %collective-permute-start.1 = (f32[64,256]{1,0:T(8,128)S(1)}, f32[64,256]{1,0:T(8,128)S(1)}, u32[]{:S(2)}, u32[]{:S(2)}) collective-permute-start(f32[64,256]{1,0:T(8,128)S(1)} %second.1.second_ref), channel_id=1, source_target_pairs={{8,16},{24,32},{40,48},{56,64},{72,80},{88,96},{104,112},{136,144}... | collective-permute-start | bytes 196616 | tf_op jit(solution)/shard_map/ppermute | solution.py:373
  26.7 7.3 %copy-start = (f32[64,256]{1,0:T(8,128)}, f32[64,256]{1,0:T(8,128)S(1)}, u32[]{:S(2)}) copy-start(f32[64,256]{1,0:T(8,128)S(1)} %collective-permute-done.2.wrap_ref) | copy-start | bytes 196612
  26.7 7.3 %copy-start.2 = (f32[64,256]{1,0:T(8,128)}, f32[64,256]{1,0:T(8,128)S(1)}, u32[]{:S(2)}) copy-start(f32[64,256]{1,0:T(8,128)S(1)} %collective-permute-done.1.other_ref) | copy-start | bytes 196612
  26.8 7.2 %collective-permute-start.3 = (f32[8,256]{1,0:T(8,128)S(1)}, f32[8,256]{1,0:T(8,128)S(1)}, u32[]{:S(2)}, u32[]{:S(2)}) collective-permute-start(f32[8,256]{1,0:T(8,128)S(1)} %third.1), channel_id=1, source_target_pairs={{0,8},{16,24},{32,40},{48,56},{64,72},{80,88},{96,104},{112,120},{... | collective-permute-start | bytes 24584 | tf_op jit(solution)/shard_map/ppermute | solution.py:373
  34.0 0.7 copy-start.5
  34.7 16.2 %collective-permute-start.4 = (f32[128,256]{1,0:T(8,128)S(1)}, f32[128,256]{1,0:T(8,128)S(1)}, u32[]{:S(2)}, u32[]{:S(2)}) collective-permute-start(f32[128,256]{1,0:T(8,128)S(1)} %get-tuple-element.23), channel_id=1, source_target_pairs={{0,256},{8,264},{16,272},{24,280},{32,288},{40,296},{48,304},{56,3... | collective-permute-start | bytes 393224 | tf_op jit(solution)/shard_map/ppermute | solution.py:373
  41.8 20.0 %all-to-all-start = ((f32[16,1,256]{2,1,0:T(1,128)}), f32[16,1,256]{2,1,0:T(1,128)S(1)}, u32[]{:S(2)}, u32[]{:S(2)}) async-start(f32[16,1,256]{2,1,0:T(1,128)} %get-tuple-element.22), calls=%async_computation | async-start | bytes 32768 | tf_op jit(solution)/shard_map/all_to_all | solution.py:448
  50.8 0.6 copy-start.9
  62.1 13.8 %all-to-all-start.1 = ((f32[8,4,256]{2,1,0:T(4,128)}), f32[8,4,256]{2,1,0:T(4,128)S(1)}, u32[]{:S(2)}, u32[]{:S(2)}) async-start(f32[8,4,256]{2,1,0:T(4,128)} %localized.1), calls=%async_computation.1 | async-start | bytes 65536 | tf_op jit(solution)/shard_map/all_to_all | solution.py:462
